TPU v7x, 128 devices: a whole 4x4x4 slice. The times are simulated.
128 devices in a mesh: mp: 16 (over z_lo, y, core), dp: 8 (over x, z_hi).
Axes of the slice: x: 4, y: 4, z: 4 (z_hi: 2, z_lo: 2; z = z_hi * 2 + z_lo), core: 2. Of those that a mesh axis runs over, the one named last changes fastest.
Arguments:
- inputs: bfloat16 [2, 512, 13, 13, 384], P(None, 'dp'), may hold values from -6 to 6
- conv_weight: bfloat16 [2, 3, 3, 384, 256], P(None, None, None, None, 'mp'), may hold values from -0.125 to 0.125
- conv_bias: float32 [2, 256], P(None, 'mp'), may hold values from -3 to 3
- first_stitch: float32 [256, 2, 2], P('mp'), may hold values from 0.2 to 1
- fc_weight: bfloat16 [2, 9216, 4096], P(None, 'mp'), may hold values from -0.25 to 0.25
- fc_bias: float32 [4096, 2], P('mp'), may hold values from -3 to 3
- second_stitch: float32 [4096, 2, 2], P('mp'), may hold values from 0.2 to 1
- crop_counts: int32 [64], P('dp'), may hold values from 1 to 8, as said below
- out_grad: bfloat16 [4096, 2, 512], P('mp', None, 'dp'), may hold values from -6 to 6
Outputs:
- output: bfloat16 [4096, 2, 512], P('mp', None, 'dp')
- input_grad: bfloat16 [2, 512, 13, 13, 384], P(None, 'dp', None, None, 'mp')
- conv_weight_grad: float32 [2, 3, 3, 384, 256], P(None, None, None, None, 'mp')
- conv_bias_grad: float32 [2, 256], P(None, 'mp')
- first_stitch_grad: float32 [256, 2, 2], P('mp')
- fc_weight_grad: float32 [2, 9216, 4096], P(None, 'mp', 'dp')
- fc_bias_grad: float32 [4096, 2], P('mp')
- second_stitch_grad: float32 [4096, 2, 2], P('mp')
Inputs may be any that keep to these rules, and one draw needn't show every extreme that they name: `crop_counts`: images of dp index d are images d * 8 onward; their crops fill that index's 64 rows from the first, the rest is padding; in every draw all images of some index hold 8 crops.
All inputs are finite; a program needn't handle non-finite values.
Results may differ from a plain program's by a relative error of at most 0.024.
Values may be sent and summed in bfloat16 or wider, within the bound.
No kernel may reach another device: no remote copies, remote signals or barrier semaphores. Data moves between devices by JAX's collectives and lax.ppermute only.
A program may use at most 192 MiB of HBM per device.

v0:
```python
import jax
import jax.numpy as jnp
from jax import lax
from jax.sharding import PartitionSpec as P


def in_blocks(array, dim, count):
    before, after = (array.shape[:dim], array.shape[dim + 1 :])
    return jnp.moveaxis(array.reshape(*before, count, -1, *after), dim, 0)


def sent_and_summed(array, axis, dim):
    count = lax.axis_size(axis)
    tiles = lax.all_to_all(in_blocks(array, dim, count), axis, 0, 0, tiled=True)
    return jnp.sum(tiles.astype(jnp.float32), axis=0)


def copy_for_each(array, axis):
    count = lax.axis_size(axis)
    return lax.all_to_all(
        jnp.broadcast_to(array[None], (count, *array.shape)), axis, 0, 0, tiled=True
    )


def in_order(tiles, dim):
    lengths = list(tiles.shape[1:])
    lengths[dim] *= tiles.shape[0]
    return jnp.moveaxis(tiles, 0, dim).reshape(lengths)


def gathered_copies(array, axis, dim):
    tiles = copy_for_each(array, axis)
    return in_order(tiles, dim)


def taken_together(array, axis):
    everything = copy_for_each(array, axis)
    return jnp.sum(everything.astype(jnp.float32), axis=0)


def pool_axis(values, axis):
    first = lax.slice_in_dim(values, 0, 11, 2, axis)
    second = lax.slice_in_dim(values, 1, 12, 2, axis)
    third = lax.slice_in_dim(values, 2, 13, 2, axis)
    return first + second + third


def unpool_axis(values, axis):
    total = None
    for offset in range(3):
        config = [(0, 0, 0)] * values.ndim
        config[axis] = (offset, 2 - offset, 1)
        placed = lax.pad(values, jnp.float32(0.0), config)
        total = placed if total is None else total + placed
    return total


def back_conv(grad_part, kernel):
    turned = jnp.transpose(jnp.flip(kernel, (0, 1)), (0, 1, 3, 2))
    return lax.conv_general_dilated(
        grad_part,
        turned,
        (1, 1),
        "SAME",
        dimension_numbers=("NHWC", "HWIO", "NHWC"),
        preferred_element_type=jnp.float32,
    )


def local(
    inputs,
    conv_weight,
    conv_bias,
    first_stitch,
    fc_weight,
    fc_bias,
    second_stitch,
    crop_counts,
    out_grad,
):
    num_rows = inputs.shape[1]
    local_ch = conv_weight.shape[4]
    flat_rows = fc_weight.shape[1]
    live = jnp.sum(crop_counts)
    row_mask = (jnp.arange(num_rows) < live).astype(jnp.float32)
    pre_list = []
    for tower_index in range(2):
        conv_out = lax.conv_general_dilated(
            inputs[tower_index],
            conv_weight[tower_index],
            (1, 1),
            "SAME",
            dimension_numbers=("NHWC", "HWIO", "NHWC"),
            preferred_element_type=jnp.float32,
        )
        pre_list.append(conv_out + conv_bias[tower_index])
    pre_act = jnp.stack(pre_list)
    activation, conv_gelu_back = jax.vjp(jax.nn.gelu, pre_act)
    pooled = pool_axis(pool_axis(activation, 2), 3) / 9.0
    stitch_one = jnp.transpose(first_stitch, (1, 2, 0))
    mixed = jnp.stack(
        [
            stitch_one[to_tower, 0] * pooled[0] + stitch_one[to_tower, 1] * pooled[1]
            for to_tower in range(2)
        ]
    )
    flat = (
        jnp.transpose(mixed, (0, 1, 4, 2, 3)).reshape(2, num_rows, flat_rows).astype(jnp.bfloat16)
    )
    columns = fc_weight
    fc_pre = (
        sent_and_summed(
            jnp.einsum("trk,tkf->ftr", flat, columns, preferred_element_type=jnp.float32).astype(
                jnp.bfloat16
            ),
            "mp",
            0,
        )
        + fc_bias[:, :, None]
    )
    hidden, fc_gelu_back = jax.vjp(jax.nn.gelu, fc_pre)
    output = (
        jnp.sum(second_stitch[:, :, :, None] * hidden[:, None, :, :], axis=2)
        * row_mask[None, None, :]
    )
    out_cot = out_grad.astype(jnp.float32) * row_mask[None, None, :]
    second_stitch_grad = jnp.sum(out_cot[:, :, None, :] * hidden[:, None, :, :], axis=3)
    hidden_grad = jnp.sum(second_stitch[:, :, :, None] * out_cot[:, :, None, :], axis=1)
    fc_grad = fc_gelu_back(hidden_grad)[0].astype(jnp.bfloat16)
    fc_bias_grad = jnp.sum(fc_grad.astype(jnp.float32), axis=2)
    shard_part = gathered_copies(fc_grad, "mp", 0)
    columns = fc_weight
    flat_grad = jnp.einsum("ftr,tkf->trk", shard_part, columns, preferred_element_type=jnp.float32)
    weight_part = jnp.einsum("trk,ftr->tkf", flat, shard_part, preferred_element_type=jnp.float32)
    flat_grad, fc_weight_grad = (flat_grad, weight_part)
    mixed_grad = jnp.transpose(flat_grad.reshape(2, num_rows, local_ch, 6, 6), (0, 1, 3, 4, 2))
    stitch_sums = jnp.sum(mixed_grad[:, None] * pooled[None], axis=(2, 3, 4))
    first_stitch_grad = jnp.transpose(stitch_sums, (2, 0, 1))
    pooled_grad = jnp.stack(
        [
            stitch_one[0, from_tower] * mixed_grad[0] + stitch_one[1, from_tower] * mixed_grad[1]
            for from_tower in range(2)
        ]
    )
    activation_grad = unpool_axis(unpool_axis(pooled_grad / 9.0, 2), 3)
    pre_grad = conv_gelu_back(activation_grad)[0].astype(jnp.bfloat16)
    conv_bias_grad = jnp.sum(pre_grad.astype(jnp.float32), axis=(1, 2, 3))
    padded = jnp.pad(inputs, ((0, 0), (0, 0), (1, 1), (1, 1), (0, 0)))
    tap_grads = []
    for row_tap in range(3):
        for col_tap in range(3):
            window_in = padded[:, :, row_tap : row_tap + 13, col_tap : col_tap + 13, :]
            tap_grads.append(
                jnp.einsum(
                    "trijc,trijo->tco", window_in, pre_grad, preferred_element_type=jnp.float32
                )
            )
    conv_weight_grad = jnp.stack(tap_grads, axis=1).reshape(2, 3, 3, inputs.shape[4], local_ch)
    kernel_rows = lax.all_to_all(conv_weight, "mp", split_axis=3, concat_axis=4, tiled=True)
    own_in = kernel_rows.shape[3]
    start_grad = jnp.zeros((2, num_rows, 13, 13, own_in), jnp.float32)
    grad_part = lax.all_gather(pre_grad, "mp", axis=4, tiled=True)
    part_out = grad_part.shape[4]
    kernels = lax.slice_in_dim(kernel_rows, 0, part_out, axis=4)
    terms = [back_conv(grad_part[tower_index], kernels[tower_index]) for tower_index in range(2)]
    input_grad = (start_grad + jnp.stack(terms)).astype(jnp.bfloat16)
    fc_weight_grad = lax.psum_scatter(
        fc_weight_grad.astype(jnp.bfloat16), "dp", scatter_dimension=2, tiled=True
    ).astype(jnp.float32)
    conv_weight_grad, conv_bias_grad, first_stitch_grad, fc_bias_grad, second_stitch_grad = (
        taken_together(conv_weight_grad.astype(jnp.bfloat16), "dp").astype(jnp.float32),
        taken_together(conv_bias_grad.astype(jnp.bfloat16), "dp").astype(jnp.float32),
        taken_together(first_stitch_grad.astype(jnp.bfloat16), "dp").astype(jnp.float32),
        taken_together(fc_bias_grad.astype(jnp.bfloat16), "dp").astype(jnp.float32),
        taken_together(second_stitch_grad.astype(jnp.bfloat16), "dp").astype(jnp.float32),
    )
    return (
        output.astype(jnp.bfloat16),
        input_grad,
        conv_weight_grad,
        conv_bias_grad,
        first_stitch_grad,
        fc_weight_grad,
        fc_bias_grad,
        second_stitch_grad,
    )


def solution(mesh):
    placed = (
        P(None, "dp", None, None, None),
        P(None, None, None, None, "mp"),
        P(None, "mp"),
        P("mp", None, None),
        P(None, "mp", None),
        P("mp", None),
        P("mp", None, None),
        P("dp"),
        P("mp", None, "dp"),
    )
    return jax.shard_map(
        local,
        mesh=mesh,
        in_specs=placed,
        out_specs=(
            P("mp", None, "dp"),
            P(None, "dp", None, None, "mp"),
            P(None, None, None, None, "mp"),
            P(None, "mp"),
            P("mp", None, None),
            P(None, "mp", "dp"),
            P("mp", None),
            P("mp", None, None),
        ),
        check_vma=False,
    )
```

profile of v0, /device:TPU:1, one launch (start us, length us, event | category | flops | bytes accessed | tf_op | source)
XLA Modules:
  0.0 543.6 jit_solution(9472175553102597434)
XLA Ops:
  9.5 33.3 %fusion.28 = f32[1,64,13,13,16]{1,4,3,2,0:T(8,128)S(1)} fusion(bf16[2,64,13,13,384]{4,1,3,2,0:T(8,128)(2,1)} %param.9, f32[16]{0:T(128)S(1)} %get-tuple-element.25, bf16[2,3,3,384,16]{3,4,2,1,0:T(8,128)(2,1)} %param.10), kind=kOutput, calls=%fused_computation.46 | convolution fusion | flops 1076798464 | bytes 9109568 | tf_op jit(solution)/shard_map/conv_general_dilated | solution.py:88
  42.8 28.1 %fusion.34 = f32[1,64,13,13,16]{1,4,3,2,0:T(8,128)S(1)} fusion(bf16[2,64,13,13,384]{4,1,3,2,0:T(8,128)(2,1)S(1)} %copy-done.9, f32[16]{0:T(128)S(1)} %get-tuple-element.26, bf16[2,3,3,384,16]{3,4,2,1,0:T(8,128)(2,1)S(1)} %copy-done.4), kind=kOutput, calls=%fused_computation.48 | convolution fusion | flops 1076798464 | bytes 9110016 | tf_op jit(solution)/shard_map/conv_general_dilated | solution.py:88
  81.1 7.3 %all-to-all-start = ((bf16[16,256,2,64]{1,3,2,0:T(8,128)(2,1)}), bf16[16,256,2,64]{1,3,2,0:T(8,128)(2,1)S(1)}, u32[]{:S(2)}, u32[]{:S(2)}) async-start(bf16[16,256,2,64]{1,3,2,0:T(8,128)(2,1)} %bitcast.227), calls=%async_computation | async-start | bytes 2097152 | tf_op jit(solution)/shard_map/all_to_all | solution.py:14
  89.9 14.4 %all-to-all-done = bf16[16,256,2,64]{1,3,2,0:T(8,128)(2,1)S(1)} async-done(((bf16[16,256,2,64]{1,3,2,0:T(8,128)(2,1)}), bf16[16,256,2,64]{1,3,2,0:T(8,128)(2,1)S(1)}, u32[]{:S(2)}, u32[]{:S(2)}) %all-to-all-start) | async-done | bytes 1048608 | tf_op jit(solution)/shard_map/all_to_all | solution.py:14
  104.8 18.8 %all_to_all.50 = bf16[16,256,2,64]{1,3,2,0:T(8,128)(2,1)S(1)} all-to-all(bf16[16,256,2,64]{1,3,2,0:T(8,128)(2,1)S(1)} %broadcast_in_dim.12), channel_id=1, replica_groups=mesh['mp'=16,'dp'=8] {'mp'}, dimensions={0} | all-to-all | bytes 2097152 | tf_op jit(solution)/shard_map/all_to_all | solution.py:20
  128.9 7.3 %fusion.108 = f32[2,64,576]{2,1,0:T(8,128)} fusion(bf16[4096,2,64]{0,2,1:T(8,128)(2,1)S(1)} %bitcast.223, bf16[2,576,4096]{2,1,0:T(8,128)(2,1)} %param.13), kind=kOutput, calls=%fused_computation.151 | convolution fusion | flops 603979776 | bytes 10780672 | tf_op jit(solution)/shard_map/ftr,tkf->trk/dot_general | solution.py:133
  138.4 22.5 %pad.24 = f32[2,64,13,6,16]{1,4,3,2,0:T(8,128)} pad(f32[2,64,6,6,16]{1,4,3,2,0:T(8,128)S(1)} %maximum_multiply_fusion, f32[]{:T(128)} %constant.9.clone.1), padding=0_0_0x0_0_0x2_0_1x0_0_0x0_0_0 | pad | bytes 933892 | tf_op jit(solution)/shard_map/pad | solution.py:53
  161.0 22.4 %pad.23 = f32[2,64,13,6,16]{1,4,3,2,0:T(8,128)} pad(f32[2,64,6,6,16]{1,4,3,2,0:T(8,128)S(1)} %maximum_multiply_fusion, f32[]{:T(128)} %constant.9.clone.1), padding=0_0_0x0_0_0x1_1_1x0_0_0x0_0_0 | pad | bytes 933892 | tf_op jit(solution)/shard_map/pad | solution.py:53
  183.4 22.4 %pad.22 = f32[2,64,13,6,16]{1,4,3,2,0:T(8,128)} pad(f32[2,64,6,6,16]{1,4,3,2,0:T(8,128)S(1)} %maximum_multiply_fusion, f32[]{:T(128)} %constant.9.clone.1), padding=0_0_0x0_0_0x0_2_1x0_0_0x0_0_0 | pad | bytes 933892 | tf_op jit(solution)/shard_map/pad | solution.py:53
  208.2 47.9 %pad.27 = f32[2,64,13,13,16]{1,4,3,2,0:T(8,128)} pad(f32[2,64,13,6,16]{1,4,3,2,0:T(8,128)S(1)} %add_add_fusion, f32[]{:T(128)} %constant.9.clone.1), padding=0_0_0x0_0_0x0_0_0x2_0_1x0_0_0 | pad | bytes 2023428 | tf_op jit(solution)/shard_map/pad | solution.py:53
  256.1 47.8 %pad.26 = f32[2,64,13,13,16]{1,4,3,2,0:T(8,128)} pad(f32[2,64,13,6,16]{1,4,3,2,0:T(8,128)S(1)} %add_add_fusion, f32[]{:T(128)} %constant.9.clone.1), padding=0_0_0x0_0_0x0_0_0x1_1_1x0_0_0 | pad | bytes 2023428 | tf_op jit(solution)/shard_map/pad | solution.py:53
  303.9 47.9 %pad.25 = f32[2,64,13,13,16]{1,4,3,2,0:T(8,128)} pad(f32[2,64,13,6,16]{1,4,3,2,0:T(8,128)S(1)} %add_add_fusion, f32[]{:T(128)} %constant.9.clone.1), padding=0_0_0x0_0_0x0_0_0x0_2_1x0_0_0 | pad | bytes 2023428 | tf_op jit(solution)/shard_map/pad | solution.py:53
  351.8 7.3 %fusion.105 = (bf16[2,16]{1,0:T(2,128)(2,1)S(1)}, bf16[2,64,13,13,16]{1,4,3,2,0:T(8,128)(2,1)}) fusion(f32[1,64,13,13,16]{1,4,3,2,0:T(8,128)} %copy-done.1, f32[1,64,13,13,16]{1,4,3,2,0:T(8,128)S(1)} %fusion.28, f32[2,64,13,13,16]{1,4,3,2,0:T(8,128)} %pad.27, f32[2,64,13,13,16]{1,4,3,2,0:T(8,128)} %pad.25, f32[2,64,13,13,16]{1,4,3,2,0:T(8,128)} %pad.26), kind=kLoop, calls=%fused_computation.149 | loop fusion | flops 8306656 | bytes 6230080 | tf_op jit(solution)/shard_map/reduce_sum | solution.py:147
  370.2 7.6 %fusion.71 = bf16[2,9,384,16]{2,3,0,1:T(8,128)(2,1)S(1)} fusion(bf16[2,64,13,13,16]{1,4,3,2,0:T(8,128)(2,1)} %get-tuple-element.14, bf16[2,64,13,13,384]{4,1,3,2,0:T(8,128)(2,1)} %param.9), kind=kOutput, calls=%fused_computation.87 | convolution fusion | flops 265826304 | bytes 17330176 | tf_op jit(solution)/shard_map/trijc,trijo->tco/dot_general | solution.py:154
  377.9 7.5 %fusion.69 = bf16[2,9,384,16]{2,3,0,1:T(8,128)(2,1)S(1)} fusion(bf16[2,9,384,16]{2,3,0,1:T(8,128)(2,1)S(1)} %fusion.71, bf16[2,64,13,13,16]{1,4,3,2,0:T(8,128)(2,1)S(1)} %copy-done, bf16[2,64,13,13,384]{4,1,3,2,0:T(8,128)(2,1)} %param.9), kind=kOutput, calls=%fused_computation.85 | convolution fusion | flops 265826304 | bytes 18022400 | tf_op jit(solution)/shard_map/trijc,trijo->tco/dot_general | solution.py:154
  391.0 7.4 %fusion.73 = bf16[2,9,384,16]{2,3,0,1:T(8,128)(2,1)S(1)} fusion(bf16[2,9,384,16]{2,3,0,1:T(8,128)(2,1)S(1)} %fusion.65, bf16[2,64,13,13,16]{1,4,3,2,0:T(8,128)(2,1)S(1)} %copy-done, bf16[2,64,13,13,384]{4,1,3,2,0:T(8,128)(2,1)} %param.9), kind=kOutput, calls=%fused_computation.89 | convolution fusion | flops 265826304 | bytes 18022400 | tf_op jit(solution)/shard_map/trijc,trijo->tco/dot_general | solution.py:154
  398.4 6.6 %fusion.63 = bf16[2,9,384,16]{2,3,0,1:T(8,128)(2,1)S(1)} fusion(bf16[2,9,384,16]{2,3,0,1:T(8,128)(2,1)S(1)} %fusion.73, bf16[2,64,13,13,16]{1,4,3,2,0:T(8,128)(2,1)S(1)} %copy-done, bf16[2,64,13,13,384]{4,1,3,2,0:T(8,128)(2,1)} %param.9), kind=kOutput, calls=%fused_computation.79 | convolution fusion | flops 265826304 | bytes 18022400 | tf_op jit(solution)/shard_map/trijc,trijo->tco/dot_general | solution.py:154
  405.7 7.0 %all-to-all-start.6 = ((bf16[8,256,2]{1,2,0:T(2,128)(2,1)}), bf16[8,256,2]{1,2,0:T(2,128)(2,1)S(1)}, u32[]{:S(2)}, u32[]{:S(2)}) async-start(bf16[8,256,2]{1,2,0:T(2,128)(2,1)} %broadcast_in_dim.16), calls=%async_computation.7 | async-start | bytes 16384 | tf_op jit(solution)/shard_map/all_to_all | solution.py:20
  426.2 6.8 %fusion.59 = bf16[2,9,384,16]{2,3,0,1:T(8,128)(2,1)S(1)} fusion(bf16[2,9,384,16]{2,3,0,1:T(8,128)(2,1)S(1)} %fusion.61, bf16[2,64,13,13,16]{1,4,3,2,0:T(8,128)(2,1)S(1)} %copy-done, bf16[2,64,13,13,384]{4,1,3,2,0:T(8,128)(2,1)} %param.9), kind=kOutput, calls=%fused_computation.75 | convolution fusion | flops 265826304 | bytes 18022400 | tf_op jit(solution)/shard_map/trijc,trijo->tco/dot_general | solution.py:154
  450.6 7.0 %fusion.57 = bf16[2,9,384,16]{2,3,0,1:T(8,128)(2,1)S(1)} fusion(bf16[2,9,384,16]{2,3,0,1:T(8,128)(2,1)S(1)} %fusion.59, bf16[2,64,13,13,16]{1,4,3,2,0:T(8,128)(2,1)S(1)} %copy-done, bf16[2,64,13,13,384]{4,1,3,2,0:T(8,128)(2,1)} %param.9), kind=kOutput, calls=%fused_computation.73 | convolution fusion | flops 265826304 | bytes 18022400 | tf_op jit(solution)/shard_map/trijc,trijo->tco/dot_general | solution.py:154
  474.4 17.7 %all-to-all-done.3 = bf16[8,2,3,3,384,16]{4,5,3,2,1,0:T(8,128)(2,1)} async-done(((bf16[8,2,3,3,384,16]{4,5,3,2,1,0:T(8,128)(2,1)}), bf16[8,2,3,3,384,16]{4,5,3,2,1,0:T(8,128)(2,1)}, u32[]{:S(2)}, u32[]{:S(2)}) %all-to-all-start.3) | async-done | bytes 1769504 | tf_op jit(solution)/shard_map/all_to_all | solution.py:20
  497.7 7.3 %all-gather.2.cloned.1.call-done = bf16[2,64,13,13,256]{1,4,3,2,0:T(8,128)(2,1)} async-done(((bf16[2,64,13,13,16]{1,4,3,2,0:T(8,128)(2,1)}), bf16[2,64,13,13,256]{1,4,3,2,0:T(8,128)(2,1)}) %all-gather.2.cloned.1.call-update) | async-done | bytes 11075600 | tf_op jit(solution)/shard_map/all_gather | solution.py:162
  505.0 16.7 %fusion.37 = bf16[1,64,13,13,24]{1,4,3,2,0:T(8,128)(2,1)S(1)} fusion(bf16[3,3,24,256]{3,2,1,0:T(8,128)(2,1)S(1)} %squeeze.39, bf16[2,64,13,13,256]{1,4,3,2,0:T(8,128)(2,1)} %all-gather.2.cloned.1.call-done), kind=kOutput, calls=%fused_computation.49 | convolution fusion | flops 1076884992 | bytes 11705344 | tf_op jit(solution)/shard_map/conv_general_dilated | solution.py:60
  521.8 12.2 %fusion.38 = bf16[1,64,13,13,24]{1,4,3,2,0:T(8,128)(2,1)S(1)} fusion(bf16[3,3,24,256]{3,2,1,0:T(8,128)(2,1)S(1)} %squeeze.37, bf16[2,64,13,13,256]{1,4,3,2,0:T(8,128)(2,1)S(1)} %copy-done.8), kind=kOutput, calls=%fused_computation.50 | convolution fusion | flops 1076884992 | bytes 11705344 | tf_op jit(solution)/shard_map/conv_general_dilated | solution.py:60
  (97 shorter events, 95.8 us)
Async XLA Ops:
  9.5 33.3 %copy-start.4 = (bf16[2,3,3,384,16]{3,4,2,1,0:T(8,128)(2,1)S(1)}, bf16[2,3,3,384,16]{3,4,2,1,0:T(8,128)(2,1)}, u32[]{:S(2)}) copy-start(bf16[2,3,3,384,16]{3,4,2,1,0:T(8,128)(2,1)} %param.10) | copy-start | bytes 663556
  9.5 33.3 %copy-start.9 = (bf16[2,64,13,13,384]{4,1,3,2,0:T(8,128)(2,1)S(1)}, bf16[2,64,13,13,384]{4,1,3,2,0:T(8,128)(2,1)}, u32[]{:S(2)}) copy-start(bf16[2,64,13,13,384]{4,1,3,2,0:T(8,128)(2,1)} %param.9) | copy-start | bytes 49840132
  70.9 1.1 copy-start.1
  79.9 8.5 %copy-start.10 = (s32[8]{0:T(128)S(1)}, s32[8]{0:T(128)}, u32[]{:S(2)}) copy-start(s32[8]{0:T(128)} %param.16) | copy-start | bytes 100
  80.0 9.8 %copy-start.5 = (bf16[256,2,64]{0,2,1:T(8,128)(2,1)S(1)}, bf16[256,2,64]{0,2,1:T(8,128)(2,1)}, u32[]{:S(2)}) copy-start(bf16[256,2,64]{0,2,1:T(8,128)(2,1)} %param.17) | copy-start | bytes 196612
  80.0 24.5 %copy-start.6 = (f32[256,2]{0,1:T(2,128)S(1)}, f32[256,2]{0,1:T(2,128)}, u32[]{:S(2)}) copy-start(f32[256,2]{0,1:T(2,128)} %param.14) | copy-start | bytes 6148
  80.0 24.5 %copy-start.7 = (f32[256,2,2]{0,2,1:T(2,128)S(1)}, f32[256,2,2]{0,2,1:T(2,128)}, u32[]{:S(2)}) copy-start(f32[256,2,2]{0,2,1:T(2,128)} %param.15) | copy-start | bytes 12292
  81.1 23.2 %all-to-all-start = ((bf16[16,256,2,64]{1,3,2,0:T(8,128)(2,1)}), bf16[16,256,2,64]{1,3,2,0:T(8,128)(2,1)S(1)}, u32[]{:S(2)}, u32[]{:S(2)}) async-start(bf16[16,256,2,64]{1,3,2,0:T(8,128)(2,1)} %bitcast.227), calls=%async_computation | async-start | bytes 2097152 | tf_op jit(solution)/shard_map/all_to_all | solution.py:14
  88.4 406.2 %reduce-scatter.2.cloned.1.call-start = ((), (), s32[]{:S(2)}) async-start(), calls=%async_computation.10 | async-start | bytes 10616832 | tf_op jit(solution)/shard_map/reduce_scatter | solution.py:167
  128.8 376.2 %all-gather.2.cloned.1.call-start = ((), (), s32[]{:S(2)}) async-start(), calls=%async_computation.9 | async-start | bytes 23535616 | tf_op jit(solution)/shard_map/all_gather | solution.py:162
  137.6 0.8 copy-start.2
  365.5 39.5 %all-to-all-start.2 = ((bf16[16,2,3456]{2,1,0:T(2,128)(2,1)}), bf16[16,2,3456]{2,1,0:T(2,128)(2,1)S(1)}, u32[]{:S(2)}, u32[]{:S(2)}) async-start(bf16[16,2,3456]{2,1,0:T(2,128)(2,1)} %reshape.110), calls=%async_computation.2 | async-start | bytes 442368 | tf_op jit(solution)/shard_map/all_to_all | solution.py:159
  370.2 7.6 %copy-start = (bf16[2,64,13,13,16]{1,4,3,2,0:T(8,128)(2,1)S(1)}, bf16[2,64,13,13,16]{1,4,3,2,0:T(8,128)(2,1)}, u32[]{:S(2)}) copy-start(bf16[2,64,13,13,16]{1,4,3,2,0:T(8,128)(2,1)} %get-tuple-element.14) | copy-start | bytes 2076676
  370.2 15.1 %slice-start = ((s8[16613376]{0:T(1024)(128)(4,1)}), s8[4194304]{0:T(1024)(128)(4,1)S(1)}, s32[]{:S(2)}) async-start(s8[16613376]{0:T(1024)(128)(4,1)} %bitcast.234), calls=%async_computation.11 | async-start | bytes 8388608
  370.2 15.1 %slice-start.1 = ((s8[16613376]{0:T(1024)(128)(4,1)}), s8[4194304]{0:T(1024)(128)(4,1)S(1)}, s32[]{:S(2)}) async-start(s8[16613376]{0:T(1024)(128)(4,1)} %bitcast.234), calls=%async_computation.12 | async-start | bytes 8388608
  370.2 15.1 %slice-start.2 = ((s8[16613376]{0:T(1024)(128)(4,1)}), s8[4194304]{0:T(1024)(128)(4,1)S(1)}, s32[]{:S(2)}) async-start(s8[16613376]{0:T(1024)(128)(4,1)} %bitcast.234), calls=%async_computation.13 | async-start | bytes 8388608
  377.8 8.2 %slice-start.3 = ((s8[16613376]{0:T(1024)(128)(4,1)}), s8[4030464]{0:T(1024)(128)(4,1)S(1)}, s32[]{:S(2)}) async-start(s8[16613376]{0:T(1024)(128)(4,1)} %bitcast.234), calls=%async_computation.14 | async-start | bytes 8060928
  405.7 13.6 %all-to-all-start.6 = ((bf16[8,256,2]{1,2,0:T(2,128)(2,1)}), bf16[8,256,2]{1,2,0:T(2,128)(2,1)S(1)}, u32[]{:S(2)}, u32[]{:S(2)}) async-start(bf16[8,256,2]{1,2,0:T(2,128)(2,1)} %broadcast_in_dim.16), calls=%async_computation.7 | async-start | bytes 16384 | tf_op jit(solution)/shard_map/all_to_all | solution.py:20
  419.9 13.2 %all-to-all-start.7 = ((bf16[8,256,2,2]{1,3,2,0:T(2,128)(2,1)}), bf16[8,256,2,2]{1,3,2,0:T(2,128)(2,1)S(1)}, u32[]{:S(2)}, u32[]{:S(2)}) async-start(bf16[8,256,2,2]{1,3,2,0:T(2,128)(2,1)} %broadcast_in_dim.17), calls=%async_computation.8 | async-start | bytes 32768 | tf_op jit(solution)/shard_map/all_to_all | solution.py:20
  426.2 14.0 %copy-start.3 = (f32[2,64,16,6,6]{1,2,4,3,0:T(8,128)S(1)}, f32[2,64,16,6,6]{1,2,4,3,0:T(8,128)}, u32[]{:S(2)}) copy-start(f32[2,64,16,6,6]{1,2,4,3,0:T(8,128)} %copy-done.2) | copy-start | bytes 884740
  433.7 13.0 %all-to-all-start.4 = ((bf16[8,2,16]{2,1,0:T(2,128)(2,1)}), bf16[8,2,16]{2,1,0:T(2,128)(2,1)S(1)}, u32[]{:S(2)}, u32[]{:S(2)}) async-start(bf16[8,2,16]{2,1,0:T(2,128)(2,1)} %broadcast_in_dim.14), calls=%async_computation.4 | async-start | bytes 8192 | tf_op jit(solution)/shard_map/all_to_all | solution.py:20
  447.3 10.4 %all-to-all-start.5 = ((bf16[8,16,2,2]{1,3,2,0:T(2,128)(2,1)}), bf16[8,16,2,2]{1,3,2,0:T(2,128)(2,1)S(1)}, u32[]{:S(2)}, u32[]{:S(2)}) async-start(bf16[8,16,2,2]{1,3,2,0:T(2,128)(2,1)} %broadcast_in_dim.15), calls=%async_computation.5 | async-start | bytes 16384 | tf_op jit(solution)/shard_map/all_to_all | solution.py:20
  459.0 33.1 %all-to-all-start.3 = ((bf16[8,2,3,3,384,16]{4,5,3,2,1,0:T(8,128)(2,1)}), bf16[8,2,3,3,384,16]{4,5,3,2,1,0:T(8,128)(2,1)}, u32[]{:S(2)}, u32[]{:S(2)}) async-start(bf16[8,2,3,3,384,16]{4,5,3,2,1,0:T(8,128)(2,1)} %broadcast_in_dim.13), calls=%async_computation.3 | async-start | bytes 3538944 | tf_op jit(solution)/shard_map/all_to_all | solution.py:20
  505.0 16.7 %copy-start.8 = (bf16[2,64,13,13,256]{1,4,3,2,0:T(8,128)(2,1)S(1)}, bf16[2,64,13,13,256]{1,4,3,2,0:T(8,128)(2,1)}, u32[]{:S(2)}) copy-start(bf16[2,64,13,13,256]{1,4,3,2,0:T(8,128)(2,1)} %all-gather.2.cloned.1.call-done) | copy-start | bytes 33226756
Sparse Core Ops, SparseCore 0:
  129.0 125.5 reduce-scatter.1
Sparse Core Ops, SparseCore 1:
  359.3 145.7 all-gather.1
where the time goes:
time: 548 us; the launch traced here: 544 us
  local copies, waits for them, and re-layouts  234 us (43%)
  matrix products  163 us (30%)
  waiting for transfers between devices  46 us (8%)
  starting transfers between devices  41.9 us (8%)
  other arithmetic  23.7 us (4%)
  blocking collectives  18.8 us (3%)
  between operations  16.4 us (3%)
    pad x6, local copies, waits for them, and re-layouts, unpool_axis(): placed = lax.pad(values, jnp.float32(0.0), config)  211 us
    conv_general_dilated x2, matrix products, local(): lax.conv_general_dilated(inputs[tower_index], conv_weight[tower_index], (...  61.4 us
    dot_general x9, matrix products, local(): jnp.einsum('trijc,trijo->tco', window_in, pre_grad, preferred_element_typ...  54.1 us
    all_to_all x5, starting transfers between devices, copy_for_each(): lax.all_to_all(jnp.broadcast_to(array[None], (count, *array.shape)), axis...  29.9 us
    conv_general_dilated x2, matrix products, back_conv(): lax.conv_general_dilated(grad_part, turned, (1, 1), 'SAME', dimension_num...  28.9 us
    all_to_all x5, waiting for transfers between devices, copy_for_each(): lax.all_to_all(jnp.broadcast_to(array[None], (count, *array.shape)), axis...  24.2 us
    all_to_all x1, blocking collectives, copy_for_each(): lax.all_to_all(jnp.broadcast_to(array[None], (count, *array.shape)), axis...  18.8 us
    all_to_all x1, waiting for transfers between devices, sent_and_summed(): tiles = lax.all_to_all(in_blocks(array, dim, count), axis, 0, 0, tiled=True)  14.4 us
  transfers between devices with their start and end apart: 9, of which 5 were waited for; matrix products, arithmetic and copies ran while one was open for 57% of the time, Pallas kernels for 0%

commit v1 on v0

v1 whole, which is shorter than its diff:
```python
import jax
import jax.numpy as jnp
from jax import lax
from jax.experimental import pallas as pl
from jax.experimental.pallas import tpu as pltpu
from jax.sharding import PartitionSpec as P

F32 = jnp.float32
BF16 = jnp.bfloat16
VMEM_LIMIT = 40 * 1024 * 1024


def params():
    return pltpu.CompilerParams(vmem_limit_bytes=VMEM_LIMIT)


def cost(flops, read):
    return pl.CostEstimate(flops=int(flops), bytes_accessed=int(read), transcendentals=0)


def nt_dot(left, right):
    return lax.dot_general(left, right, (((1,), (1,)), ((), ())), preferred_element_type=F32)


def nn_dot(left, right):
    return lax.dot_general(left, right, (((1,), (0,)), ((), ())), preferred_element_type=F32)


def first_half(shape):
    return lax.broadcasted_iota(jnp.int32, shape, len(shape) - 1) < 64


def swap_halves(value):
    return pltpu.roll(value, 64, value.ndim - 1)


def gelu_parts(x):
    root, cubic = 0.7978845608028654, 0.044715
    square = x * x
    tanh = jnp.tanh(root * x * (1.0 + cubic * square))
    half = 0.5 + 0.5 * tanh
    slope = half + 0.5 * x * (1.0 - tanh * tanh) * (root * (1.0 + 3.0 * cubic * square))
    return x * half, slope


def exchange(slabs, width):
    count = len(slabs)
    block = lax.broadcasted_iota(jnp.int32, slabs[0].shape, slabs[0].ndim - 1) // width
    step = 1
    while step < count:
        low = (block & step) == 0
        fresh = list(slabs)
        for p in range(count):
            if p & step == 0:
                q = p + step
                lanes = slabs[p].shape[-1]
                fresh[p] = jnp.where(low, slabs[p], pltpu.roll(slabs[q], step * width, slabs[p].ndim - 1))
                fresh[q] = jnp.where(low, pltpu.roll(slabs[p], lanes - step * width, slabs[p].ndim - 1), slabs[q])
        slabs = fresh
        step *= 2
    return slabs


def conv_kernel(x_ref, w_ref, const_ref, perm_ref, slope_ref, pooled_ref, flat_ref, flat_t_ref, acc, pool):
    i = pl.program_id(0)
    lead = first_half((16, 128))

    @pl.when(i == 0)
    def _():
        acc[...] = jnp.zeros_like(acc)
        pool[...] = jnp.zeros_like(pool)

    @pl.when(i < 13)
    def _():
        weights = w_ref[...]
        for start in range(0, 13, 2):
            width = min(2, 13 - start)
            rows = jnp.concatenate(
                [x_ref[t, 0, start + k] for k in range(width) for t in range(2)], axis=0
            )
            product = nt_dot(weights, rows)
            for k in range(width):
                lanes = slice(128 * k, 128 * k + 128)
                for a in range(3):
                    for b in range(3):
                        top = 16 * (3 * a + b)
                        term = jnp.where(
                            lead, product[top : top + 16, lanes], product[144 + top : 160 + top, lanes]
                        )
                        acc[i + 2 - a, start + k + 2 - b] += term

    @pl.when(i > 0)
    def _():
        row = i - 1
        acts = []
        for j in range(13):
            act, slope = gelu_parts(acc[i, j + 1] + const_ref[0])
            slope_ref[0, j] = slope.astype(BF16)
            acts.append(act)
        sums = [acts[2 * q] + acts[2 * q + 1] + acts[2 * q + 2] for q in range(6)]
        for q in range(6):
            pool[row // 2 + 1, q] += sums[q]

        @pl.when(row % 2 == 0)
        def _():
            for q in range(6):
                pool[row // 2, q] += sums[q]

    @pl.when(i == 13)
    def _():
        pooled = pool[1:7].reshape(36, 16, 128) * (1.0 / 9.0)
        pooled_ref[...] = pooled
        mixed = const_ref[1][None] * pooled + const_ref[2][None] * swap_halves(pooled)
        flat_t = nn_dot(perm_ref[...], mixed.reshape(576, 128).astype(BF16))
        flat_t_ref[...] = flat_t.astype(BF16)
        flat_ref[...] = flat_t.T.astype(BF16)


def conv_forward(x, w, consts, perm):
    return pl.pallas_call(
        conv_kernel,
        grid=(14,),
        in_specs=[
            pl.BlockSpec((2, 1, 13, 64, 384), lambda i: (0, jnp.minimum(i, 12), 0, 0, 0)),
            pl.BlockSpec((288, 384), lambda i: (0, 0)),
            pl.BlockSpec((4, 16, 128), lambda i: (0, 0, 0)),
            pl.BlockSpec((576, 576), lambda i: (0, 0)),
        ],
        out_specs=[
            pl.BlockSpec((1, 13, 16, 128), lambda i: (jnp.maximum(i - 1, 0), 0, 0, 0)),
            pl.BlockSpec((36, 16, 128), lambda i: (0, 0, 0)),
            pl.BlockSpec((128, 576), lambda i: (0, 0)),
            pl.BlockSpec((576, 128), lambda i: (0, 0)),
        ],
        out_shape=[
            jax.ShapeDtypeStruct((13, 13, 16, 128), BF16),
            jax.ShapeDtypeStruct((36, 16, 128), F32),
            jax.ShapeDtypeStruct((128, 576), BF16),
            jax.ShapeDtypeStruct((576, 128), BF16),
        ],
        scratch_shapes=[pltpu.VMEM((15, 15, 16, 128), F32), pltpu.VMEM((8, 6, 16, 128), F32)],
        compiler_params=params(),
        cost_estimate=cost(10e9, 20e6),
        name="conv_forward",
    )(x, w, consts, perm)


def fc_kernel(flat_ref, w_ref, out_ref):
    for t in range(2):
        product = nn_dot(flat_ref[64 * t : 64 * t + 64], w_ref[t])
        for g in range(2):
            out_ref[g, 64 * t : 64 * t + 64] = product[:, 256 * g : 256 * g + 256].astype(BF16)


def fc_forward(flat, w):
    return pl.pallas_call(
        fc_kernel,
        grid=(8,),
        in_specs=[
            pl.BlockSpec((128, 576), lambda i: (0, 0)),
            pl.BlockSpec((2, 576, 512), lambda i: (0, 0, i)),
        ],
        out_specs=pl.BlockSpec((2, 128, 256), lambda i: (i, 0, 0)),
        out_shape=jax.ShapeDtypeStruct((16, 128, 256), BF16),
        compiler_params=params(),
        cost_estimate=cost(4e9, 10e6),
        name="fc_forward",
    )(flat, w)


def hidden_kernel(counts_ref, parts_ref, bias_ref, stitch_ref, cot_ref, out_ref, grad_ref, sums_ref):
    live = counts_ref[0]
    for k in range(1, 8):
        live += counts_ref[k]
    mask = (lax.broadcasted_iota(jnp.int32, (64, 256), 0) < live).astype(F32)
    total = parts_ref[0].astype(F32)
    for k in range(1, 16):
        total += parts_ref[k].astype(F32)
    hidden, slope = [], []
    for t in range(2):
        act, der = gelu_parts(total[64 * t : 64 * t + 64] + bias_ref[t][None])
        hidden.append(act)
        slope.append(der)
    cots = [cot_ref[u].astype(F32) * mask for u in range(2)]
    stitch = [[stitch_ref[u, v][None] for v in range(2)] for u in range(2)]
    sums = []
    for u in range(2):
        out_ref[u] = (mask * (stitch[u][0] * hidden[0] + stitch[u][1] * hidden[1])).astype(BF16)
    for v in range(2):
        grad = (stitch[0][v] * cots[0] + stitch[1][v] * cots[1]) * slope[v]
        grad = grad.astype(BF16)
        for k in range(16):
            grad_ref[k, 64 * v : 64 * v + 64] = grad
        sums.append(jnp.sum(grad.astype(F32), axis=0, keepdims=True))
    for u in range(2):
        for v in range(2):
            sums.append(jnp.sum(cots[u] * hidden[v], axis=0, keepdims=True))
    sums_ref[...] = jnp.concatenate(sums + [jnp.zeros((2, 256), F32)], axis=0)


def hidden_layer(counts, parts, bias, stitch, cot):
    vmem = pl.BlockSpec(memory_space=pltpu.VMEM)
    return pl.pallas_call(
        hidden_kernel,
        in_specs=[pl.BlockSpec(memory_space=pltpu.SMEM), vmem, vmem, vmem, vmem],
        out_specs=[vmem, vmem, vmem],
        out_shape=[
            jax.ShapeDtypeStruct((2, 64, 256), BF16),
            jax.ShapeDtypeStruct((16, 128, 256), BF16),
            jax.ShapeDtypeStruct((8, 256), F32),
        ],
        compiler_params=params(),
        cost_estimate=cost(1e7, 3e6),
        name="hidden_layer",
    )(counts, parts, bias, stitch, cot)


def back_kernel(grad_ref, w_ref, perm_ref, const_ref, pooled_ref, slope_ref, send_ref, pre_ref, stats_ref, acc):
    step = pl.program_id(0)
    rows = jnp.concatenate([grad_ref[0], grad_ref[1]], axis=1)
    for t in range(2):
        product = nt_dot(w_ref[t], rows)

        @pl.when(step == 0)
        def _():
            acc[t] = product

        @pl.when(step > 0)
        def _():
            acc[t] += product

    @pl.when(step == 7)
    def _():
        flat_grad = jnp.where(first_half((576, 128)), acc[0], acc[1])
        high = flat_grad.astype(BF16)
        low = (flat_grad - high.astype(F32)).astype(BF16)
        perm = perm_ref[...]
        mixed_grad = (nn_dot(perm, high) + nn_dot(perm, low)).reshape(36, 16, 128)
        pooled = pooled_ref[...]
        lead = first_half((16, 128))
        own = jnp.sum(mixed_grad * pooled, axis=0)
        cross = jnp.sum(mixed_grad * swap_halves(pooled), axis=0)
        pooled_grad = const_ref[1][None] * mixed_grad + const_ref[3][None] * swap_halves(mixed_grad)
        pooled_grad = (pooled_grad * (1.0 / 9.0)).reshape(6, 6, 16, 128)
        bias_sum = jnp.zeros((16, 128), F32)
        zero = jnp.zeros((16, 128), F32)
        spread = []
        for p in range(6):
            line = []
            for j in range(13):
                terms = [pooled_grad[p, q] for q in range(6) if 2 * q <= j <= 2 * q + 2]
                line.append(terms[0] if len(terms) == 1 else terms[0] + terms[1])
            spread.append(line)
        for i in range(13):
            windows = [p for p in range(6) if 2 * p <= i <= 2 * p + 2]
            slabs = []
            for j in range(13):
                value = spread[windows[0]][j]
                if len(windows) == 2:
                    value = value + spread[windows[1]][j]
                value = (value * slope_ref[i, j].astype(F32)).astype(BF16)
                pre_ref[i, j] = value
                value = value.astype(F32)
                bias_sum = bias_sum + value
                slabs.append(value)
            slabs = exchange(slabs + [zero] * 3, 8)
            for m in range(16):
                block = (m % 2) * 8 + m // 2
                send_ref[m, :, 128 * i : 128 * i + 128] = slabs[block].astype(BF16)
        lane = lax.broadcasted_iota(jnp.int32, (16, 128), 1)
        stats = jnp.zeros((16, 128), F32)
        for k, value in enumerate((own, cross, bias_sum)):
            for t in range(2):
                half = jnp.sum(jnp.where(lead == (t == 0), value, 0.0), axis=1, keepdims=True)
                stats = jnp.where(lane == 2 * k + t, half, stats)
        stats_ref[...] = stats


def back_fc(grads, w, perm, consts, pooled, slope):
    whole = lambda *shape: pl.BlockSpec(shape, lambda i: (0,) * len(shape))
    return pl.pallas_call(
        back_kernel,
        grid=(8,),
        in_specs=[
            pl.BlockSpec((2, 128, 256), lambda i: (i, 0, 0)),
            pl.BlockSpec((2, 576, 512), lambda i: (0, 0, i)),
            whole(576, 576),
            whole(4, 16, 128),
            whole(36, 16, 128),
            whole(13, 13, 16, 128),
        ],
        out_specs=[whole(16, 16, 1664), whole(13, 13, 16, 128), whole(16, 128)],
        out_shape=[
            jax.ShapeDtypeStruct((16, 16, 1664), BF16),
            jax.ShapeDtypeStruct((13, 13, 16, 128), BF16),
            jax.ShapeDtypeStruct((16, 128), F32),
        ],
        scratch_shapes=[pltpu.VMEM((2, 576, 128), F32)],
        compiler_params=params(),
        cost_estimate=cost(4e9, 12e6),
        name="back_fc",
    )(grads, w, perm, consts, pooled, slope)


def weight_kernel(x_ref, pre_ref, sums_ref, stats_ref, out_ref, parts, acc):
    i = pl.program_id(0)

    @pl.when(i == 0)
    def _():
        parts[...] = jnp.zeros_like(parts)
        lead = first_half((13, 13, 16, 128))
        value = pre_ref[...]
        none = jnp.zeros_like(value)
        parts[0, 1:14, 1:14] = jnp.where(lead, value, none)
        parts[1, 1:14, 1:14] = jnp.where(lead, none, value)

    left = jnp.concatenate(
        [
            jnp.concatenate([parts[t, i + 2 - a, j + 2 - b] for j in range(13)], axis=1)
            for t in range(2)
            for a in range(3)
            for b in range(3)
        ],
        axis=0,
    )
    right = jnp.concatenate([x_ref[t, 0, j] for j in range(13) for t in range(2)], axis=0)
    product = nn_dot(left, right)

    @pl.when(i == 0)
    def _():
        acc[...] = product

    @pl.when(i > 0)
    def _():
        acc[...] += product

    @pl.when(i == 12)
    def _():
        out_ref[0:288] = acc[...].astype(BF16)
        small = jnp.concatenate([sums_ref[...], jnp.zeros((8, 256), F32)], axis=0)
        out_ref[288:304] = jnp.concatenate([small, stats_ref[...]], axis=1).astype(BF16)


def weight_grad(x, pre, sums, stats):
    whole = lambda *shape: pl.BlockSpec(shape, lambda i: (0,) * len(shape))
    return pl.pallas_call(
        weight_kernel,
        grid=(13,),
        in_specs=[
            pl.BlockSpec((2, 1, 13, 64, 384), lambda i: (0, i, 0, 0, 0)),
            whole(13, 13, 16, 128),
            whole(8, 256),
            whole(16, 128),
        ],
        out_specs=whole(304, 384),
        out_shape=jax.ShapeDtypeStruct((304, 384), BF16),
        scratch_shapes=[pltpu.VMEM((2, 15, 15, 16, 128), BF16), pltpu.VMEM((288, 384), F32)],
        compiler_params=params(),
        cost_estimate=cost(10e9, 20e6),
        name="weight_grad",
    )(x, pre, sums, stats)


def turn_kernel(w_ref, out_ref):
    for tap in range(9):
        rows = w_ref[:, 16 * tap : 16 * tap + 16].reshape(256, 384)
        out_ref[:, 256 * tap : 256 * tap + 256] = rows.T


def turned(w):
    return pl.pallas_call(
        turn_kernel,
        out_shape=jax.ShapeDtypeStruct((384, 2304), BF16),
        compiler_params=params(),
        cost_estimate=cost(1e9, 4e6),
        name="turned_kernels",
    )(w)


def input_kernel(g_ref, w_ref, out_ref, taps):
    g = g_ref[...].reshape(256, 1664).astype(F32)
    zero = jnp.zeros((256, 128), BF16)
    for b in range(3):
        taps[b, :, 0:128] = zero
        taps[b, :, 1792:1920] = zero
        for i in range(13):
            row = g[:, 128 * i : 128 * i + 128]
            if b == 0:
                row = pltpu.roll(row, 120, 1)
            if b == 2:
                row = pltpu.roll(row, 8, 1)
            taps[b, :, 128 * i + 128 : 128 * i + 256] = row.astype(BF16)
    weights = w_ref[...]
    for start in range(0, 13, 2):
        width = 128 * min(2, 13 - start)
        right = jnp.concatenate(
            [
                taps[b, :, 128 * (start + 2 - a) : 128 * (start + 2 - a) + width]
                for a in range(3)
                for b in range(3)
            ],
            axis=0,
        )
        product = nn_dot(weights, right)
        for m in range(16):
            out_ref[m, :, 128 * start : 128 * start + width] = product[24 * m : 24 * m + 24].astype(BF16)


def input_grad_part(g, w):
    return pl.pallas_call(
        input_kernel,
        out_shape=jax.ShapeDtypeStruct((16, 24, 1664), BF16),
        scratch_shapes=[pltpu.VMEM((3, 256, 1920), BF16)],
        compiler_params=params(),
        cost_estimate=cost(4e9, 4e6),
        name="input_grad",
    )(g, w)


def place_kernel(part_ref, out_ref):
    slabs = [part_ref[2 * (block % 8) + block // 8].astype(F32) for block in range(16)]
    slabs = exchange(slabs, 8)
    for j in range(13):
        out_ref[0, 0, j] = slabs[j][:, 0:64].astype(BF16)
        out_ref[1, 0, j] = swap_halves(slabs[j])[:, 0:64].astype(BF16)


def placed_back(parts):
    return pl.pallas_call(
        place_kernel,
        grid=(13,),
        in_specs=[pl.BlockSpec((16, 24, 128), lambda i: (0, 0, i))],
        out_specs=pl.BlockSpec((2, 1, 13, 24, 64), lambda i: (0, i, 0, 0, 0)),
        out_shape=jax.ShapeDtypeStruct((2, 13, 13, 24, 64), BF16),
        compiler_params=params(),
        cost_estimate=cost(1e8, 3e6),
        name="placed_back",
    )(parts)


def fc_weight_kernel(flat_ref, grad_ref, out_ref):
    t = pl.program_id(0)
    lead = first_half((576, 128)) == (t == 0)
    zero = jnp.zeros((576, 128), BF16)
    left = jnp.concatenate([jnp.where(lead, flat_ref[d], zero) for d in range(8)], axis=1)
    for g in range(2):
        right = jnp.concatenate([grad_ref[d, g] for d in range(8)], axis=0)
        out_ref[0, :, 256 * g : 256 * g + 256] = nn_dot(left, right)


def fc_weight_grad_of(flats, grads):
    return pl.pallas_call(
        fc_weight_kernel,
        grid=(2,),
        in_specs=[
            pl.BlockSpec((8, 576, 128), lambda t: (0, 0, 0)),
            pl.BlockSpec((8, 2, 128, 256), lambda t: (0, 0, 0, 0)),
        ],
        out_specs=pl.BlockSpec((1, 576, 512), lambda t: (t, 0, 0)),
        out_shape=jax.ShapeDtypeStruct((2, 576, 512), F32),
        compiler_params=params(),
        cost_estimate=cost(3e9, 5e6),
        name="fc_weight_grad",
    )(flats, grads)


def total_kernel(parts_ref, conv_ref, sums_ref, stats_ref):
    total = parts_ref[0].astype(F32)
    for k in range(1, 8):
        total += parts_ref[k].astype(F32)
    conv_ref[...] = total[0:288]
    sums_ref[...] = total[288:296, 0:256]
    stats_ref[...] = total[288:304, 256:384]


def summed(parts):
    return pl.pallas_call(
        total_kernel,
        out_shape=[
            jax.ShapeDtypeStruct((288, 384), F32),
            jax.ShapeDtypeStruct((8, 256), F32),
            jax.ShapeDtypeStruct((16, 128), F32),
        ],
        compiler_params=params(),
        cost_estimate=cost(1e7, 3e6),
        name="summed",
    )(parts)


def dealt(array, axis):
    return lax.all_to_all(array, axis, 0, 0, tiled=True)


def copies(array, count):
    return jnp.broadcast_to(array[None], (count, *array.shape))


def local(
    inputs,
    conv_weight,
    conv_bias,
    first_stitch,
    fc_weight,
    fc_bias,
    second_stitch,
    crop_counts,
    out_grad,
):
    x = jnp.transpose(inputs, (0, 2, 3, 1, 4))
    kernels = jnp.transpose(conv_weight, (0, 1, 2, 4, 3)).reshape(2, 144, 384)

    fc_row = jnp.arange(576)
    slab_row = (fc_row % 36) * 16 + fc_row // 36
    perm = (slab_row[:, None] == fc_row[None, :]).astype(BF16)
    perm_back = (slab_row[None, :] == fc_row[:, None]).astype(BF16)

    def lanes(pair):
        return jnp.repeat(pair, 64, axis=1)

    own = jnp.stack([first_stitch[:, 0, 0], first_stitch[:, 1, 1]], axis=1)
    consts = jnp.stack(
        [
            lanes(conv_bias.T),
            lanes(own),
            lanes(jnp.stack([first_stitch[:, 0, 1], first_stitch[:, 1, 0]], axis=1)),
            lanes(jnp.stack([first_stitch[:, 1, 0], first_stitch[:, 0, 1]], axis=1)),
        ]
    )

    slope, pooled, flat, flat_t = conv_forward(x, kernels.reshape(288, 384), consts, perm)
    parts = dealt(fc_forward(flat, fc_weight), "mp")
    output, grad_copies, sums = hidden_layer(
        crop_counts,
        parts,
        fc_bias.T,
        jnp.transpose(second_stitch, (1, 2, 0)),
        jnp.transpose(out_grad, (1, 2, 0)),
    )
    grads = dealt(grad_copies, "mp")
    send, pre, stats = back_fc(grads, fc_weight, perm_back, consts, pooled, slope)
    pre_all = dealt(send, "mp")

    kernels_all = turned(dealt(jnp.tile(kernels, (8, 1, 1)), "mp"))
    part = dealt(input_grad_part(pre_all, kernels_all), "mp")
    input_grad = jnp.transpose(placed_back(part), (0, 4, 1, 2, 3))

    gathered = dealt(copies(weight_grad(x, pre, sums, stats), 8), "dp")
    conv_sum, f_sums, c_sums = summed(gathered)
    flats = dealt(copies(flat_t, 8), "dp")
    grads_dp = dealt(grads.reshape(8, 2, 128, 256), "dp")
    fc_weight_grad = fc_weight_grad_of(flats, grads_dp)

    conv_weight_grad = jnp.transpose(conv_sum.reshape(2, 3, 3, 16, 384), (0, 1, 2, 4, 3))
    first_stitch_grad = jnp.stack(
        [
            jnp.stack([c_sums[:, 0], c_sums[:, 2]], axis=1),
            jnp.stack([c_sums[:, 3], c_sums[:, 1]], axis=1),
        ],
        axis=1,
    )
    conv_bias_grad = c_sums[:, 4:6].T
    fc_bias_grad = f_sums[0:2].T
    second_stitch_grad = jnp.transpose(f_sums[2:6].reshape(2, 2, 256), (2, 0, 1))
    return (
        jnp.transpose(output, (2, 0, 1)),
        input_grad,
        conv_weight_grad,
        conv_bias_grad,
        first_stitch_grad,
        fc_weight_grad,
        fc_bias_grad,
        second_stitch_grad,
    )


def solution(mesh):
    placed = (
        P(None, "dp", None, None, None),
        P(None, None, None, None, "mp"),
        P(None, "mp"),
        P("mp", None, None),
        P(None, "mp", None),
        P("mp", None),
        P("mp", None, None),
        P("dp"),
        P("mp", None, "dp"),
    )
    return jax.shard_map(
        local,
        mesh=mesh,
        in_specs=placed,
        out_specs=(
            P("mp", None, "dp"),
            P(None, "dp", None, None, "mp"),
            P(None, None, None, None, "mp"),
            P(None, "mp"),
            P("mp", None, None),
            P(None, "mp", "dp"),
            P("mp", None),
            P("mp", None, None),
        ),
        check_vma=False,
    )
```

time: 548 us -> 227 us (0.41)
  local copies, waits for them, and re-layouts: 234 us -> 22.6 us
  matrix products: 163 us -> 0 us
  Pallas kernels: 0 us -> 63.2 us
  blocking collectives: 18.8 us -> 61.4 us
  other arithmetic: 23.7 us -> 1.89 us
  between operations: 16.4 us -> 0.89 us
  starting transfers between devices: 41.9 us -> 27.5 us
    pad x6 -> x0, local copies, waits for them, and re-layouts: 211 us -> none  [unpool_axis(): placed = lax.pad(values, jnp.float32(0.0), config)]
    conv_general_dilated x4 -> x0, matrix products: 90.3 us -> none  [the longest x2 61.4 us: local(): lax.conv_general_dilated(inputs[tower_index], conv_weight[tower_index], (...]
    dot_general x12 -> x0, matrix products: 72.5 us -> none  [the longest x9 54.1 us: local(): jnp.einsum('trijc,trijo->tco', window_in, pre_grad, preferred_element_typ...]
    pallas_call x0 -> x10, Pallas kernels: none -> 63.2 us  [the longest x1 16.1 us: conv_forward(): pl.pallas_call(conv_kernel, grid=(14,), in_specs=[pl.BlockSpec((2, 1, 13,...]
    all_to_all x1 -> x3, blocking collectives: 18.8 us -> 61.4 us  [dealt(): return lax.all_to_all(array, axis, 0, 0, tiled=True)]
    all_to_all x7 -> x5, starting transfers between devices: 41.8 us -> 27.5 us  [dealt(): return lax.all_to_all(array, axis, 0, 0, tiled=True)]
    reduce_sum x11 -> x0, other arithmetic: 13.4 us -> none  [the longest x1 7.34 us: local(): conv_bias_grad = jnp.sum(pre_grad.astype(jnp.float32), axis=(1, 2, 3))]
    all_to_all x7 -> x5, waiting for transfers between devices: 38.6 us -> 48.3 us  [dealt(): return lax.all_to_all(array, axis, 0, 0, tiled=True)]
  transfers between devices with their start and end apart: 9 -> 5, of which waited for: 5 -> 5; matrix products, arithmetic and copies ran while one was open for 57% -> 1% of each run, Pallas kernels for 0% -> 16%
where the time goes in v1:
time: 227 us; the launch traced here: 226 us
  Pallas kernels  63.2 us (28%)
  blocking collectives  61.4 us (27%)
  waiting for transfers between devices  48.3 us (21%)
  starting transfers between devices  27.5 us (12%)
  local copies, waits for them, and re-layouts  22.6 us (10%)
    all_to_all x3, blocking collectives, dealt(): return lax.all_to_all(array, axis, 0, 0, tiled=True)  61.4 us
    all_to_all x5, waiting for transfers between devices, dealt(): return lax.all_to_all(array, axis, 0, 0, tiled=True)  48.3 us
    all_to_all x5, starting transfers between devices, dealt(): return lax.all_to_all(array, axis, 0, 0, tiled=True)  27.5 us
    pallas_call x1, Pallas kernels, conv_forward(): pl.pallas_call(conv_kernel, grid=(14,), in_specs=[pl.BlockSpec((2, 1, 13,...  16.1 us
    pallas_call x1, Pallas kernels, weight_grad(): pl.pallas_call(weight_kernel, grid=(13,), in_specs=[pl.BlockSpec((2, 1, 1...  15.2 us
    unnamed x56, local copies, waits for them, and re-layouts  14.4 us
    pallas_call x1, Pallas kernels, back_fc(): pl.pallas_call(back_kernel, grid=(8,), in_specs=[pl.BlockSpec((2, 128, 25...  11.3 us
    pallas_call x1, Pallas kernels, placed_back(): pl.pallas_call(place_kernel, grid=(13,), in_specs=[pl.BlockSpec((16, 24,...  7.95 us
  transfers between devices with their start and end apart: 5, of which 5 were waited for; matrix products, arithmetic and copies ran while one was open for 1% of the time, Pallas kernels for 16%

profile of v1, /device:TPU:1, one launch (start us, length us, event | category | flops | bytes accessed | tf_op | source)
XLA Modules:
  0.0 225.8 jit_solution(763824337965536883)
XLA Ops:
  4.4 16.1 %conv_forward.1 = (bf16[13,13,16,128]{3,2,1,0:T(8,128)(2,1)S(1)}, f32[36,16,128]{2,1,0:T(8,128)S(1)}, bf16[128,576]{1,0:T(8,128)(2,1)S(1)}, bf16[576,128]{1,0:T(8,128)(2,1)S(1)}) custom-call(bf16[2,13,13,64,384]{4,3,2,1,0:T(8,128)(2,1)} %bitcast.45, bf16[288,384]{1,0:T(8,128)(2,1)S(1)} %bitcast.34, ...), custom_call_target="tpu_custom_call" | custom-call | flops 10000000000 | bytes 20000000 | tf_op jit(solution)/shard_map/conv_forward/pallas_call | solution.py:120
  20.6 3.5 %fc_forward.1 = bf16[16,128,256]{2,1,0:T(8,128)(2,1)S(1)} custom-call(bf16[128,576]{1,0:T(8,128)(2,1)S(1)} %get-tuple-element.21.flat_ref, bf16[2,576,4096]{2,1,0:T(8,128)(2,1)S(1)} %bitcast.40), custom_call_target="tpu_custom_call" | custom-call | flops 4000000000 | bytes 10000000 | tf_op jit(solution)/shard_map/fc_forward/pallas_call | solution.py:156
  24.2 22.6 %all_to_all.40.parts_ref = bf16[16,128,256]{2,1,0:T(8,128)(2,1)S(1)} all-to-all(bf16[16,128,256]{2,1,0:T(8,128)(2,1)S(1)} %fc_forward.1), channel_id=1, replica_groups=mesh['mp'=16,'dp'=8] {'mp'}, dimensions={0} | all-to-all | bytes 2097152 | tf_op jit(solution)/shard_map/all_to_all | solution.py:491
  48.0 7.0 %all-to-all-start.6 = ((bf16[8,576,128]{2,1,0:T(8,128)(2,1)}), bf16[8,576,128]{2,1,0:T(8,128)(2,1)S(1)}, u32[]{:S(2)}, u32[]{:S(2)}) async-start(bf16[8,576,128]{2,1,0:T(8,128)(2,1)} %broadcast_in_dim.33), calls=%async_computation.6 | async-start | bytes 2359296 | tf_op jit(solution)/shard_map/all_to_all | solution.py:491
  55.9 1.5 hidden_layer.1
  57.4 14.4 %all-to-all-done.6.flat_ref = bf16[8,576,128]{2,1,0:T(8,128)(2,1)S(1)} async-done(((bf16[8,576,128]{2,1,0:T(8,128)(2,1)}), bf16[8,576,128]{2,1,0:T(8,128)(2,1)S(1)}, u32[]{:S(2)}, u32[]{:S(2)}) %all-to-all-start.6) | async-done | bytes 1179680 | tf_op jit(solution)/shard_map/all_to_all | solution.py:491
  71.9 21.1 %all_to_all.41.grad_ref = bf16[16,128,256]{2,1,0:T(8,128)(2,1)} all-to-all(bf16[16,128,256]{2,1,0:T(8,128)(2,1)S(1)} %get-tuple-element.23), channel_id=1, replica_groups=mesh['mp'=16,'dp'=8] {'mp'}, dimensions={0} | all-to-all | bytes 2097152 | tf_op jit(solution)/shard_map/all_to_all | solution.py:491
  93.0 1.4 tile.11
  94.3 4.7 %all-to-all-start.3 = ((bf16[16,144,384]{2,1,0:T(8,128)(2,1)}), bf16[16,144,384]{2,1,0:T(8,128)(2,1)S(1)}, u32[]{:S(2)}, u32[]{:S(2)}) async-start(bf16[16,144,384]{2,1,0:T(8,128)(2,1)} %bitcast.41), calls=%async_computation.3 | async-start | bytes 3538944 | tf_op jit(solution)/shard_map/all_to_all | solution.py:491
  99.1 3.7 %copy-done.14 = bf16[2,576,4096]{2,1,0:T(8,128)(2,1)S(1)} copy-done((bf16[2,576,4096]{2,1,0:T(8,128)(2,1)S(1)}, bf16[2,576,4096]{2,1,0:T(8,128)(2,1)}, u32[]{:S(2)}) %copy-start.14) | copy-done | bytes 9437208
  104.8 11.3 %back_fc.1 = (bf16[16,16,1664]{2,1,0:T(8,128)(2,1)S(1)}, bf16[13,13,16,128]{3,2,1,0:T(8,128)(2,1)S(1)}, f32[16,128]{1,0:T(8,128)S(1)}) custom-call(bf16[16,128,256]{2,1,0:T(8,128)(2,1)} %all_to_all.41.grad_ref, bf16[2,576,4096]{2,1,0:T(8,128)(2,1)S(1)} %copy-done.14, bf16[576,576]{1,0:T(8,128)(2,1)S(1)} %copy-done.8, ...), custom_call_target="tpu_custom_call" | custom-call | flops 4000000000 | bytes 12000000 | tf_op jit(solution)/shard_map/back_fc/pallas_call | solution.py:281
  117.5 5.2 %all-to-all-done.3.w_ref = bf16[16,144,384]{2,1,0:T(8,128)(2,1)S(1)} async-done(((bf16[16,144,384]{2,1,0:T(8,128)(2,1)}), bf16[16,144,384]{2,1,0:T(8,128)(2,1)S(1)}, u32[]{:S(2)}, u32[]{:S(2)}) %all-to-all-start.3) | async-done | bytes 1769504 | tf_op jit(solution)/shard_map/all_to_all | solution.py:491
  122.7 17.6 %all_to_all.42.g_ref = bf16[16,16,1664]{2,1,0:T(8,128)(2,1)} all-to-all(bf16[16,16,1664]{2,1,0:T(8,128)(2,1)S(1)} %get-tuple-element.26), channel_id=1, replica_groups=mesh['mp'=16,'dp'=8] {'mp'}, dimensions={0} | all-to-all | bytes 1703936 | tf_op jit(solution)/shard_map/all_to_all | solution.py:491
  140.4 3.6 %all-to-all-start.7 = ((bf16[8,2,128,256]{3,2,1,0:T(8,128)(2,1)}), bf16[8,2,128,256]{3,2,1,0:T(8,128)(2,1)S(1)}, u32[]{:S(2)}, u32[]{:S(2)}) async-start(bf16[8,2,128,256]{3,2,1,0:T(8,128)(2,1)} %bitcast.20), calls=%async_computation.7 | async-start | bytes 2097152 | tf_op jit(solution)/shard_map/all_to_all | solution.py:491
  144.0 15.2 %weight_grad.1 = bf16[304,384]{1,0:T(8,128)(2,1)S(1)} custom-call(bf16[2,13,13,64,384]{4,3,2,1,0:T(8,128)(2,1)} %bitcast.46, bf16[13,13,16,128]{3,2,1,0:T(8,128)(2,1)S(1)} %copy-done.18, f32[8,256]{1,0:T(8,128)S(1)} %get-tuple-element.28.sums_ref, f32[16,128]{1,0:T(8,128)S(1)} %copy-done.22), custom_call_target="tpu_custom_call" | custom-call | flops 10000000000 | bytes 20000000 | tf_op jit(solution)/shard_map/weight_grad/pallas_call | solution.py:346
  159.6 1.5 broadcast_in_dim.32
  161.1 6.3 %all-to-all-start.5 = ((bf16[8,304,384]{2,1,0:T(8,128)(2,1)}), bf16[8,304,384]{2,1,0:T(8,128)(2,1)S(1)}, u32[]{:S(2)}, u32[]{:S(2)}) async-start(bf16[8,304,384]{2,1,0:T(8,128)(2,1)} %broadcast_in_dim.32), calls=%async_computation.5 | async-start | bytes 3735552 | tf_op jit(solution)/shard_map/all_to_all | solution.py:491
  167.4 1.5 copy-done.1
  170.1 3.5 %input_grad.1 = bf16[16,24,1664]{2,1,0:T(8,128)(2,1)S(1)} custom-call(bf16[16,16,1664]{2,1,0:T(8,128)(2,1)S(1)} %copy-done.7, bf16[384,2304]{1,0:T(8,128)(2,1)S(1)} %turned_kernels.1.w_ref), custom_call_target="tpu_custom_call" | custom-call | flops 4000000000 | bytes 4000000 | tf_op jit(solution)/shard_map/input_grad/pallas_call | solution.py:410
  174.6 19.0 %all-to-all-done.5.parts_ref = bf16[8,304,384]{2,1,0:T(8,128)(2,1)S(1)} async-done(((bf16[8,304,384]{2,1,0:T(8,128)(2,1)}), bf16[8,304,384]{2,1,0:T(8,128)(2,1)S(1)}, u32[]{:S(2)}, u32[]{:S(2)}) %all-to-all-start.5) | async-done | bytes 1867808 | tf_op jit(solution)/shard_map/all_to_all | solution.py:491
  193.6 5.9 %all-to-all-start.4 = ((bf16[16,24,1664]{2,1,0:T(8,128)(2,1)}), bf16[16,24,1664]{2,1,0:T(8,128)(2,1)S(1)}, u32[]{:S(2)}, u32[]{:S(2)}) async-start(bf16[16,24,1664]{2,1,0:T(8,128)(2,1)} %copy-done.2), calls=%async_computation.4 | async-start | bytes 2555904 | tf_op jit(solution)/shard_map/all_to_all | solution.py:491
  202.0 2.6 %fc_weight_grad.1 = f32[2,576,512]{2,1,0:T(8,128)} custom-call(bf16[8,576,128]{2,1,0:T(8,128)(2,1)S(1)} %copy-done.4, bf16[8,2,128,256]{3,2,1,0:T(8,128)(2,1)S(1)} %copy-done.6), custom_call_target="tpu_custom_call" | custom-call | flops 3000000000 | bytes 5000000 | tf_op jit(solution)/shard_map/fc_weight_grad/pallas_call | solution.py:452
  208.5 9.4 %all-to-all-done.4.part_ref = bf16[16,24,1664]{2,1,0:T(8,128)(2,1)S(1)} async-done(((bf16[16,24,1664]{2,1,0:T(8,128)(2,1)}), bf16[16,24,1664]{2,1,0:T(8,128)(2,1)S(1)}, u32[]{:S(2)}, u32[]{:S(2)}) %all-to-all-start.4) | async-done | bytes 1277984 | tf_op jit(solution)/shard_map/all_to_all | solution.py:491
  217.8 8.0 %placed_back.1 = bf16[2,13,13,24,64]{4,3,2,1,0:T(8,128)(2,1)} custom-call(bf16[16,24,1664]{2,1,0:T(8,128)(2,1)S(1)} %all-to-all-done.4.part_ref), custom_call_target="tpu_custom_call" | custom-call | flops 100000000 | bytes 3000000 | tf_op jit(solution)/shard_map/placed_back/pallas_call | solution.py:429
  (88 shorter events, 18.3 us)
Async XLA Ops:
  0.6 3.8 %copy-start.9 = (bf16[2,3,3,384,16]{3,4,2,1,0:T(8,128)(2,1)S(1)}, bf16[2,3,3,384,16]{3,4,2,1,0:T(8,128)(2,1)}, u32[]{:S(2)}) copy-start(bf16[2,3,3,384,16]{3,4,2,1,0:T(8,128)(2,1)} %param.10) | copy-start | bytes 663556
  3.1 17.5 %slice-start = ((s8[9437184]{0:T(1024)(128)(4,1)}), s8[4194304]{0:T(1024)(128)(4,1)S(1)}, s32[]{:S(2)}) async-start(s8[9437184]{0:T(1024)(128)(4,1)} %bitcast.39), calls=%async_computation.8 | async-start | bytes 8388608
  4.4 16.2 %slice-start.1 = ((s8[9437184]{0:T(1024)(128)(4,1)}), s8[4194304]{0:T(1024)(128)(4,1)S(1)}, s32[]{:S(2)}) async-start(s8[9437184]{0:T(1024)(128)(4,1)} %bitcast.39), calls=%async_computation.9 | async-start | bytes 8388608
  4.4 16.2 %slice-start.2 = ((s8[9437184]{0:T(1024)(128)(4,1)}), s8[1048576]{0:T(1024)(128)(4,1)S(1)}, s32[]{:S(2)}) async-start(s8[9437184]{0:T(1024)(128)(4,1)} %bitcast.39), calls=%async_computation.10 | async-start | bytes 2097152
  20.6 3.6 %copy-start.15 = (bf16[13,13,16,128]{3,2,1,0:T(8,128)(2,1)}, bf16[13,13,16,128]{3,2,1,0:T(8,128)(2,1)S(1)}, u32[]{:S(2)}) copy-start(bf16[13,13,16,128]{3,2,1,0:T(8,128)(2,1)S(1)} %get-tuple-element.25.slope_ref) | copy-start | bytes 2076676
  20.6 3.6 %copy-start.19 = (f32[36,16,128]{2,1,0:T(8,128)}, f32[36,16,128]{2,1,0:T(8,128)S(1)}, u32[]{:S(2)}) copy-start(f32[36,16,128]{2,1,0:T(8,128)S(1)} %get-tuple-element.24.pooled_ref) | copy-start | bytes 884740
  46.8 8.2 %copy-start.11 = (f32[256,2,2]{0,2,1:T(2,128)S(1)}, f32[256,2,2]{0,2,1:T(2,128)}, u32[]{:S(2)}) copy-start(f32[256,2,2]{0,2,1:T(2,128)} %param.15) | copy-start | bytes 12292
  46.8 8.2 %copy-start.12 = (f32[256,2]{0,1:T(2,128)S(1)}, f32[256,2]{0,1:T(2,128)}, u32[]{:S(2)}) copy-start(f32[256,2]{0,1:T(2,128)} %param.14) | copy-start | bytes 6148
  46.8 8.2 %copy-start.13 = (s32[8]{0:T(128)S(1)}, s32[8]{0:T(128)}, u32[]{:S(2)}) copy-start(s32[8]{0:T(128)} %counts_ref.1) | copy-start | bytes 100
  48.0 23.9 %all-to-all-start.6 = ((bf16[8,576,128]{2,1,0:T(8,128)(2,1)}), bf16[8,576,128]{2,1,0:T(8,128)(2,1)S(1)}, u32[]{:S(2)}, u32[]{:S(2)}) async-start(bf16[8,576,128]{2,1,0:T(8,128)(2,1)} %broadcast_in_dim.33), calls=%async_computation.6 | async-start | bytes 2359296 | tf_op jit(solution)/shard_map/all_to_all | solution.py:491
  71.9 22.5 %copy-start.3 = (bf16[8,576,128]{2,1,0:T(8,128)(2,1)}, bf16[8,576,128]{2,1,0:T(8,128)(2,1)S(1)}, u32[]{:S(2)}) copy-start(bf16[8,576,128]{2,1,0:T(8,128)(2,1)S(1)} %all-to-all-done.6.flat_ref) | copy-start | bytes 3538948
  94.3 4.7 %copy-start.8 = (bf16[576,576]{1,0:T(8,128)(2,1)S(1)}, bf16[576,576]{1,0:T(8,128)(2,1)}, u32[]{:S(2)}) copy-start(bf16[576,576]{1,0:T(8,128)(2,1)} %get-tuple-element.54.perm_ref) | copy-start | bytes 1990660
  94.3 28.4 %all-to-all-start.3 = ((bf16[16,144,384]{2,1,0:T(8,128)(2,1)}), bf16[16,144,384]{2,1,0:T(8,128)(2,1)S(1)}, u32[]{:S(2)}, u32[]{:S(2)}) async-start(bf16[16,144,384]{2,1,0:T(8,128)(2,1)} %bitcast.41), calls=%async_computation.3 | async-start | bytes 3538944 | tf_op jit(solution)/shard_map/all_to_all | solution.py:491
  99.1 3.7 %copy-start.14 = (bf16[2,576,4096]{2,1,0:T(8,128)(2,1)S(1)}, bf16[2,576,4096]{2,1,0:T(8,128)(2,1)}, u32[]{:S(2)}) copy-start(bf16[2,576,4096]{2,1,0:T(8,128)(2,1)} %w_ref.3) | copy-start | bytes 28311556
  122.7 17.6 %copy-start = (bf16[16,144,384]{2,1,0:T(8,128)(2,1)}, bf16[16,144,384]{2,1,0:T(8,128)(2,1)S(1)}, u32[]{:S(2)}) copy-start(bf16[16,144,384]{2,1,0:T(8,128)(2,1)S(1)} %all-to-all-done.3.w_ref) | copy-start | bytes 5308420
  122.7 21.2 %copy-start.18 = (bf16[13,13,16,128]{3,2,1,0:T(8,128)(2,1)S(1)}, bf16[13,13,16,128]{3,2,1,0:T(8,128)(2,1)}, u32[]{:S(2)}) copy-start(bf16[13,13,16,128]{3,2,1,0:T(8,128)(2,1)} %copy-done.17) | copy-start | bytes 2076676
  122.7 21.2 %copy-start.22 = (f32[16,128]{1,0:T(8,128)S(1)}, f32[16,128]{1,0:T(8,128)}, u32[]{:S(2)}) copy-start(f32[16,128]{1,0:T(8,128)} %copy-done.21) | copy-start | bytes 24580
  140.4 19.2 %all-to-all-start.7 = ((bf16[8,2,128,256]{3,2,1,0:T(8,128)(2,1)}), bf16[8,2,128,256]{3,2,1,0:T(8,128)(2,1)S(1)}, u32[]{:S(2)}, u32[]{:S(2)}) async-start(bf16[8,2,128,256]{3,2,1,0:T(8,128)(2,1)} %bitcast.20), calls=%async_computation.7 | async-start | bytes 2097152 | tf_op jit(solution)/shard_map/all_to_all | solution.py:491
  159.6 1.6 copy-start.5
  161.1 32.5 %all-to-all-start.5 = ((bf16[8,304,384]{2,1,0:T(8,128)(2,1)}), bf16[8,304,384]{2,1,0:T(8,128)(2,1)S(1)}, u32[]{:S(2)}, u32[]{:S(2)}) async-start(bf16[8,304,384]{2,1,0:T(8,128)(2,1)} %broadcast_in_dim.32), calls=%async_computation.5 | async-start | bytes 3735552 | tf_op jit(solution)/shard_map/all_to_all | solution.py:491
  167.4 1.5 copy-start.1
  193.6 24.2 %all-to-all-start.4 = ((bf16[16,24,1664]{2,1,0:T(8,128)(2,1)}), bf16[16,24,1664]{2,1,0:T(8,128)(2,1)S(1)}, u32[]{:S(2)}, u32[]{:S(2)}) async-start(bf16[16,24,1664]{2,1,0:T(8,128)(2,1)} %copy-done.2), calls=%async_computation.4 | async-start | bytes 2555904 | tf_op jit(solution)/shard_map/all_to_all | solution.py:491
  199.5 1.3 copy-start.4
  200.8 1.2 copy-start.6
  (7 other events, 6.6 us)

commit v2 on v0

v2 whole, which is shorter than its diff:
```python
import jax
import jax.numpy as jnp
from jax import lax
from jax.experimental import pallas as pl
from jax.experimental.pallas import tpu as pltpu
from jax.sharding import PartitionSpec as P

F32 = jnp.float32
BF16 = jnp.bfloat16
LARGE, SMALL = 58, 16


def params(mib=LARGE):
    return pltpu.CompilerParams(vmem_limit_bytes=mib * 1024 * 1024)


def cost(flops, read):
    return pl.CostEstimate(flops=int(flops), bytes_accessed=int(read), transcendentals=0)


def nt_dot(left, right):
    return lax.dot_general(left, right, (((1,), (1,)), ((), ())), preferred_element_type=F32)


def nn_dot(left, right):
    return lax.dot_general(left, right, (((1,), (0,)), ((), ())), preferred_element_type=F32)


def first_half(shape):
    return lax.broadcasted_iota(jnp.int32, shape, len(shape) - 1) < 64


def swap_halves(value):
    return pltpu.roll(value, 64, value.ndim - 1)


def gelu_parts(x):
    root, cubic = 0.7978845608028654, 0.044715
    square = x * x
    tanh = jnp.tanh(root * x * (1.0 + cubic * square))
    half = 0.5 + 0.5 * tanh
    slope = half + 0.5 * x * (1.0 - tanh * tanh) * (root * (1.0 + 3.0 * cubic * square))
    return x * half, slope


def spread(slabs):
    lane = lax.broadcasted_iota(jnp.int32, slabs[0].shape, 1)
    for bit in range(4):
        odd = (lane & (8 << bit)) != 0
        slabs = [jnp.where(odd, slabs[(k + (1 << bit)) % 16], slabs[k]) for k in range(16)]
    return slabs


def exchange(slabs):
    slabs = spread(slabs)
    slabs = [slabs[0]] + [pltpu.roll(slabs[k], 8 * k, 1) for k in range(1, 16)]
    slabs = spread(slabs)
    return [slabs[-k % 16] for k in range(16)]


def column(row):
    size = row.shape[1]
    eye = lax.broadcasted_iota(jnp.int32, (size, size), 0) == lax.broadcasted_iota(jnp.int32, (size, size), 1)
    return jnp.sum(jnp.where(eye, row, 0.0), axis=1, keepdims=True)


def by_tower(first, second):
    lead = first_half((16, 128))
    return jnp.where(lead, column(first), column(second))


def stitch_slabs(stitch_ref):
    part = [[stitch_ref[u, v : v + 1] for v in range(2)] for u in range(2)]
    own = by_tower(part[0][0], part[1][1])
    into = by_tower(part[0][1], part[1][0])
    back = by_tower(part[1][0], part[0][1])
    return own, into, back


def slab_order(fc_axis):
    fc_row = lax.broadcasted_iota(jnp.int32, (576, 576), fc_axis)
    slab_row = lax.broadcasted_iota(jnp.int32, (576, 576), 1 - fc_axis)
    return (fc_row == 36 * (slab_row & 15) + (slab_row >> 4)).astype(F32).astype(BF16)


def front_kernel(
    core_ref, x_ref, w_ref, kernel_ref, bias_ref, stitch_ref,
    slope_ref, pooled_ref, flat_t_ref, own_ref, other_ref,
    xs, ws, acc, ready, pool, slopes, pooled_out, flat_t_out, parts, x_sem, w_sem, slope_sem, out_sem,
):
    def x_copy(i):
        return pltpu.make_async_copy(x_ref.at[:, i], xs.at[:, i], x_sem.at[i])

    def w_copy(t):
        return pltpu.make_async_copy(w_ref.at[t], ws.at[t], w_sem.at[t])

    def slope_copy(i):
        return pltpu.make_async_copy(slopes.at[i], slope_ref.at[i], slope_sem.at[i])

    for i in range(13):
        x_copy(i).start()
    for t in range(2):
        w_copy(t).start()
    acc[...] = jnp.zeros_like(acc)
    ready[...] = jnp.zeros_like(ready)
    pool[...] = jnp.zeros_like(pool)
    lead = first_half((16, 128))
    bias = by_tower(bias_ref[0:1], bias_ref[1:2])
    own, into, _ = stitch_slabs(stitch_ref)

    def gather(row):
        for t in range(2):
            right = pltpu.roll(acc[t, 0, row + 1], 64, 1)
            left = pltpu.roll(acc[t, 2, row + 1], 832, 1)
            ready[t] = acc[t, 1, row + 1] + right + left

    def finish(row):
        acts = []
        for j in range(13):
            lanes = slice(j // 2 * 128, j // 2 * 128 + 128)
            zero, one = ready[0, :, lanes], ready[1, :, lanes]
            if j % 2 == 0:
                pre_act = jnp.where(lead, zero, swap_halves(one))
            else:
                pre_act = jnp.where(lead, swap_halves(zero), one)
            act, slope = gelu_parts(pre_act + bias)
            slopes[jnp.maximum(row, 0), j] = slope.astype(BF16)
            acts.append(act)
        even = row % 2 == 0
        for q in range(6):
            total = acts[2 * q] + acts[2 * q + 1] + acts[2 * q + 2]
            pool[(row + 2) // 2, q] += total
            pool[jnp.maximum(row, 0) // 2, q] += jnp.where(even, total, 0.0)

    def line(i, carry):
        x_copy(i).wait()
        finish(i - 2)
        for t in range(2):
            weights = kernel_ref[144 * t : 144 * t + 144]
            for start in range(0, 13, 4):
                width = min(4, 13 - start)
                rows = xs[t, i, start : start + width].reshape(64 * width, 384)
                product = nt_dot(weights, rows)
                for a in range(3):
                    for b in range(3):
                        top = 16 * (3 * a + b)
                        acc[t, b, i + 2 - a, :, 64 * start : 64 * (start + width)] += product[top : top + 16]
        gather(i - 1)
        return carry

    def last(i, carry):
        finish(i - 2)
        gather(jnp.minimum(i - 1, 12))
        return carry

    lax.fori_loop(0, 13, line, 0)
    lax.fori_loop(13, 15, last, 0)
    for i in range(13):
        slope_copy(i).start()
    pooled = pool[1:7].reshape(36, 16, 128) * (1.0 / 9.0)
    pooled_out[...] = pooled
    pooled_copy = pltpu.make_async_copy(pooled_out, pooled_ref, out_sem.at[0])
    pooled_copy.start()
    mixed = own[None] * pooled + into[None] * swap_halves(pooled)
    flat_t = nn_dot(slab_order(0), mixed.reshape(576, 128).astype(BF16))
    flat_t_out[...] = flat_t.astype(BF16)
    flat_copy = pltpu.make_async_copy(flat_t_out, flat_t_ref, out_sem.at[1])
    flat_copy.start()
    flat = flat_t.T.astype(BF16)
    core = core_ref[0]
    copies_out = [pooled_copy, flat_copy]
    for t in range(2):
        w_copy(t).wait()
    for k, (ref, parity) in enumerate(((other_ref, 1 - core), (own_ref, core))):
        for q in range(8):
            at = pl.ds(pl.multiple_of((2 * q + parity) * 256, 256), 256)
            for t in range(2):
                parts[k, q, 64 * t : 64 * t + 64] = nn_dot(flat[64 * t : 64 * t + 64], ws[t, :, at]).astype(BF16)
            if q % 4 == 3:
                some = pl.ds(q - 3, 4)
                copy = pltpu.make_async_copy(parts.at[k, some], ref.at[some], out_sem.at[2 + 2 * k + q // 4])
                copy.start()
                copies_out.append(copy)
    for i in range(13):
        slope_copy(i).wait()
    for copy in copies_out:
        copy.wait()


VMEM = pl.BlockSpec(memory_space=pltpu.VMEM)
SMEM = pl.BlockSpec(memory_space=pltpu.SMEM)
ANY = pl.BlockSpec(memory_space=pl.ANY)


def front(core, x, w, kernels, bias, stitch):
    return pl.pallas_call(
        front_kernel,
        in_specs=[SMEM, ANY, ANY, VMEM, VMEM, VMEM],
        out_specs=[ANY] * 5,
        out_shape=[
            jax.ShapeDtypeStruct((13, 13, 16, 128), BF16),
            jax.ShapeDtypeStruct((36, 16, 128), F32),
            jax.ShapeDtypeStruct((576, 128), BF16),
            jax.ShapeDtypeStruct((8, 128, 256), BF16),
            jax.ShapeDtypeStruct((8, 128, 256), BF16),
        ],
        scratch_shapes=[
            pltpu.VMEM((2, 13, 13, 64, 384), BF16),
            pltpu.VMEM((2, 576, 4096), BF16),
            pltpu.VMEM((2, 3, 15, 16, 896), F32),
            pltpu.VMEM((2, 16, 896), F32),
            pltpu.VMEM((8, 6, 16, 128), F32),
            pltpu.VMEM((13, 13, 16, 128), BF16),
            pltpu.VMEM((36, 16, 128), F32),
            pltpu.VMEM((576, 128), BF16),
            pltpu.VMEM((2, 8, 128, 256), BF16),
            pltpu.SemaphoreType.DMA((13,)),
            pltpu.SemaphoreType.DMA((2,)),
            pltpu.SemaphoreType.DMA((13,)),
            pltpu.SemaphoreType.DMA((6,)),
        ],
        compiler_params=params(),
        cost_estimate=cost(10e9, 30e6),
        name="front",
    )(core, x, w, kernels, bias, stitch)


def hidden_kernel(counts_ref, parts_ref, bias_ref, stitch_ref, cot_ref, out_ref, grad_ref, sums_ref):
    live = counts_ref[0]
    for k in range(1, 8):
        live += counts_ref[k]
    mask = (lax.broadcasted_iota(jnp.int32, (64, 256), 0) < live).astype(F32)
    total = parts_ref[0].astype(F32)
    for k in range(1, 8):
        total += parts_ref[k].astype(F32)
    hidden, slope = [], []
    for t in range(2):
        act, der = gelu_parts(total[64 * t : 64 * t + 64] + bias_ref[t][None])
        hidden.append(act)
        slope.append(der)
    cots = [cot_ref[u].astype(F32) * mask for u in range(2)]
    stitch = [[stitch_ref[u, v][None] for v in range(2)] for u in range(2)]
    sums = []
    for u in range(2):
        out_ref[u] = (mask * (stitch[u][0] * hidden[0] + stitch[u][1] * hidden[1])).astype(BF16)
    for v in range(2):
        grad = (stitch[0][v] * cots[0] + stitch[1][v] * cots[1]) * slope[v]
        grad = grad.astype(BF16)
        for k in range(8):
            for half in range(2):
                top = 128 * half + 64 * v
                grad_ref[k, top : top + 64] = grad[:, 128 * half : 128 * half + 128]
        sums.append(jnp.sum(grad.astype(F32), axis=0, keepdims=True))
    for u in range(2):
        for v in range(2):
            sums.append(jnp.sum(cots[u] * hidden[v], axis=0, keepdims=True))
    sums_ref[...] = jnp.concatenate(sums + [jnp.zeros((2, 256), F32)], axis=0)


def hidden_layer(counts, parts, bias, stitch, cot):
    vmem = pl.BlockSpec(memory_space=pltpu.VMEM)
    return pl.pallas_call(
        hidden_kernel,
        in_specs=[pl.BlockSpec(memory_space=pltpu.SMEM), vmem, vmem, vmem, vmem],
        out_specs=[vmem, vmem, vmem],
        out_shape=[
            jax.ShapeDtypeStruct((2, 64, 256), BF16),
            jax.ShapeDtypeStruct((8, 256, 128), BF16),
            jax.ShapeDtypeStruct((8, 256), F32),
        ],
        compiler_params=params(SMALL),
        cost_estimate=cost(1e7, 3e6),
        name="hidden_layer",
    )(counts, parts, bias, stitch, cot)


def back_kernel(
    core_ref, own_ref, other_ref, w_ref, stitch_ref, pooled_ref, slope_ref,
    send_ref, pre_ref, stats_ref,
    ws, grads, pooled, slopes, sends, pres, w_sem, in_sem, send_sem, pre_sem,
):
    def w_copy(k):
        at = pl.ds(1024 * k, 1024)
        return pltpu.make_async_copy(w_ref.at[:, :, at], ws.at[:, :, at], w_sem.at[k])

    first_in = [
        pltpu.make_async_copy(own_ref, grads.at[0], in_sem.at[0]),
        pltpu.make_async_copy(other_ref, grads.at[1], in_sem.at[1]),
    ]
    later_in = [
        pltpu.make_async_copy(pooled_ref, pooled, in_sem.at[2]),
        pltpu.make_async_copy(slope_ref, slopes, in_sem.at[3]),
    ]
    for copy in first_in:
        copy.start()
    for k in range(4):
        w_copy(k).start()
    for copy in later_in:
        copy.start()
    first = core_ref[0] == 0
    perm = slab_order(1)
    own_slab, _, back_slab = stitch_slabs(stitch_ref)
    for copy in first_in:
        copy.wait()
    totals = [jnp.zeros((576, 128), F32)] * 2
    for k in range(4):
        w_copy(k).wait()
        blocks = []
        for q in (2 * k, 2 * k + 1):
            own, other = (jnp.concatenate([grads[p, q, 0:128], grads[p, q, 128:256]], axis=1) for p in range(2))
            blocks += [jnp.where(first, own, other), jnp.where(first, other, own)]
        rows = jnp.concatenate(blocks, axis=1)
        for t in range(2):
            totals[t] = totals[t] + nt_dot(ws[t, :, 1024 * k : 1024 * k + 1024], rows)
    flat_grad = jnp.where(first_half((576, 128)), totals[0], totals[1])
    high = flat_grad.astype(BF16)
    low = (flat_grad - high.astype(F32)).astype(BF16)
    mixed_grad = (nn_dot(perm, high) + nn_dot(perm, low)).reshape(36, 16, 128)
    swapped = swap_halves(mixed_grad)
    pooled_grad = own_slab[None] * mixed_grad + back_slab[None] * swapped
    pooled_grad = (pooled_grad * (1.0 / 9.0)).reshape(6, 6, 16, 128)
    for copy in later_in:
        copy.wait()
    lead = first_half((16, 128))
    bias_sum = jnp.zeros((16, 128), F32)
    zero = jnp.zeros((16, 128), F32)
    widened = []
    for p in range(6):
        line = []
        for j in range(13):
            terms = [pooled_grad[p, q] for q in range(6) if 2 * q <= j <= 2 * q + 2]
            line.append(terms[0] if len(terms) == 1 else terms[0] + terms[1])
        widened.append(line)
    copies_out = []
    for i in range(13):
        windows = [p for p in range(6) if 2 * p <= i <= 2 * p + 2]
        slabs = []
        for j in range(13):
            value = widened[windows[0]][j]
            if len(windows) == 2:
                value = value + widened[windows[1]][j]
            value = (value * slopes[i, j].astype(F32)).astype(BF16)
            pres[i, j] = value
            value = value.astype(F32)
            bias_sum = bias_sum + value
            slabs.append(value)
        slabs = exchange(slabs + [zero] * 3)
        at = pl.ds(128 * i, 128)
        for m in range(16):
            block = (m % 2) * 8 + m // 2
            sends[m, :, 128 * i : 128 * i + 128] = slabs[block].astype(BF16)
        copies_out.append(pltpu.make_async_copy(sends.at[:, :, at], send_ref.at[:, :, at], send_sem.at[i]))
        copies_out[-1].start()
        copies_out.append(pltpu.make_async_copy(pres.at[i], pre_ref.at[i], pre_sem.at[i]))
        copies_out[-1].start()
    pooled_in = pooled[...]
    own = jnp.sum(mixed_grad * pooled_in, axis=0)
    cross = jnp.sum(swapped * pooled_in, axis=0)
    lane = lax.broadcasted_iota(jnp.int32, (16, 128), 1)
    stats = jnp.zeros((16, 128), F32)
    for k, value in enumerate((own, cross, bias_sum)):
        for t in range(2):
            half = jnp.sum(jnp.where(lead == (t == 0), value, 0.0), axis=1, keepdims=True)
            stats = jnp.where(lane == 2 * k + t, half, stats)
    stats_ref[...] = stats
    for copy in copies_out:
        copy.wait()


def back_fc(core, own, other, w, stitch, pooled, slope):
    return pl.pallas_call(
        back_kernel,
        in_specs=[SMEM, ANY, ANY, ANY, VMEM, ANY, ANY],
        out_specs=[ANY, ANY, VMEM],
        out_shape=[
            jax.ShapeDtypeStruct((16, 16, 1664), BF16),
            jax.ShapeDtypeStruct((13, 13, 16, 128), BF16),
            jax.ShapeDtypeStruct((16, 128), F32),
        ],
        scratch_shapes=[
            pltpu.VMEM((2, 576, 4096), BF16),
            pltpu.VMEM((2, 8, 256, 128), BF16),
            pltpu.VMEM((36, 16, 128), F32),
            pltpu.VMEM((13, 13, 16, 128), BF16),
            pltpu.VMEM((16, 16, 1664), BF16),
            pltpu.VMEM((13, 13, 16, 128), BF16),
            pltpu.SemaphoreType.DMA((4,)),
            pltpu.SemaphoreType.DMA((4,)),
            pltpu.SemaphoreType.DMA((13,)),
            pltpu.SemaphoreType.DMA((13,)),
        ],
        compiler_params=params(),
        cost_estimate=cost(1e8, 1e6),
        name="back_fc",
    )(core, own, other, w, stitch, pooled, slope)


def weight_kernel(x_ref, pre_ref, sums_ref, stats_ref, out_ref, xs, lines, acc, x_sem):
    def x_copy(i):
        return pltpu.make_async_copy(x_ref.at[:, i], xs.at[:, i], x_sem.at[i])

    for i in range(13):
        x_copy(i).start()
    lines[...] = jnp.zeros_like(lines)
    acc[...] = jnp.zeros_like(acc)
    lead = first_half((16, 128))

    def merge(i, carry):
        zero = jnp.zeros((16, 128), F32)
        slabs = [pre_ref[i, j].astype(F32) for j in range(13)]
        turned = [swap_halves(slab) for slab in slabs]
        slabs = [zero] + slabs + [zero] * 2
        turned = [zero] + turned + [zero] * 2
        for first in range(-1, 14):
            left, right = first + 1, first + 2
            pair = (
                jnp.where(lead, slabs[left], turned[right]).astype(BF16),
                jnp.where(lead, turned[left], slabs[right]).astype(BF16),
            )
            for b in range(3):
                place = first + b - 1
                if place % 2 == 0 and 0 <= place <= 12:
                    for t in range(2):
                        lines[t, b, i + 1, :, 64 * place : 64 * place + 128] = pair[t]
        return carry

    lax.fori_loop(0, 13, merge, 0)

    def line(i, carry):
        x_copy(i).wait()
        for t in range(2):
            left = jnp.concatenate([lines[t, b, i + 2 - a] for a in range(3) for b in range(3)], axis=0)
            right = jnp.concatenate([xs[t, i].reshape(832, 384), jnp.zeros((64, 384), BF16)], axis=0)
            acc[144 * t : 144 * t + 144] += nn_dot(left, right)
        return carry

    lax.fori_loop(0, 13, line, 0)
    out_ref[0:288] = acc[...].astype(BF16)
    small = jnp.concatenate([sums_ref[...], jnp.zeros((8, 256), F32)], axis=0)
    out_ref[288:304] = jnp.concatenate([small, stats_ref[...]], axis=1).astype(BF16)


def weight_grad(x, pre, sums, stats):
    return pl.pallas_call(
        weight_kernel,
        in_specs=[ANY, VMEM, VMEM, VMEM],
        out_specs=VMEM,
        out_shape=jax.ShapeDtypeStruct((304, 384), BF16),
        scratch_shapes=[
            pltpu.VMEM((2, 13, 13, 64, 384), BF16),
            pltpu.VMEM((2, 3, 15, 16, 896), BF16),
            pltpu.VMEM((288, 384), F32),
            pltpu.SemaphoreType.DMA((13,)),
        ],
        compiler_params=params(),
        cost_estimate=cost(10e9, 20e6),
        name="weight_grad",
    )(x, pre, sums, stats)


def turn_kernel(core_ref, blocks_ref, out_ref, rows):
    core = core_ref[0]
    for k in range(8):
        for p, parity in ((0, core), (1, 1 - core)):
            at = pl.ds(pl.multiple_of(16 * (2 * k + parity), 16), 16)
            for tap in range(9):
                rows[tap, at] = blocks_ref[k, p, 16 * tap : 16 * tap + 16]
    for tap in range(9):
        out_ref[:, 256 * tap : 256 * tap + 256] = rows[tap].T


def turned(core, blocks):
    return pl.pallas_call(
        turn_kernel,
        in_specs=[SMEM, VMEM],
        out_specs=VMEM,
        out_shape=jax.ShapeDtypeStruct((384, 2304), BF16),
        scratch_shapes=[pltpu.VMEM((9, 256, 384), BF16)],
        compiler_params=params(SMALL),
        cost_estimate=cost(1e9, 4e6),
        name="turned_kernels",
    )(core, blocks)


def input_kernel(g_ref, w_ref, out_ref, taps):
    g = g_ref[...].reshape(256, 1664).astype(F32)
    zero = jnp.zeros((256, 128), BF16)
    for b in range(3):
        taps[b, :, 0:128] = zero
        taps[b, :, 1792:1920] = zero
        for i in range(13):
            row = g[:, 128 * i : 128 * i + 128]
            if b == 0:
                row = pltpu.roll(row, 120, 1)
            if b == 2:
                row = pltpu.roll(row, 8, 1)
            taps[b, :, 128 * i + 128 : 128 * i + 256] = row.astype(BF16)
    weights = w_ref[...]
    for start in range(0, 13, 2):
        width = 128 * min(2, 13 - start)
        right = jnp.concatenate(
            [
                taps[b, :, 128 * (start + 2 - a) : 128 * (start + 2 - a) + width]
                for a in range(3)
                for b in range(3)
            ],
            axis=0,
        )
        product = nn_dot(weights, right)
        for m in range(16):
            out_ref[m, :, 128 * start : 128 * start + width] = product[24 * m : 24 * m + 24].astype(BF16)


def input_grad_part(g, w):
    return pl.pallas_call(
        input_kernel,
        in_specs=[VMEM, VMEM],
        out_specs=VMEM,
        out_shape=jax.ShapeDtypeStruct((16, 24, 1664), BF16),
        scratch_shapes=[pltpu.VMEM((3, 256, 1920), BF16)],
        compiler_params=params(SMALL),
        cost_estimate=cost(4e9, 4e6),
        name="input_grad",
    )(g, w)


def place_kernel(part_ref, out_ref):
    for i in range(13):
        lanes = slice(128 * i, 128 * i + 128)
        slabs = [part_ref[2 * (block % 8) + block // 8, :, lanes].astype(F32) for block in range(16)]
        slabs = exchange(slabs)
        for j in range(13):
            out_ref[0, i, j] = slabs[j][:, 0:64].astype(BF16)
            out_ref[1, i, j] = swap_halves(slabs[j])[:, 0:64].astype(BF16)


def placed_back(parts):
    return pl.pallas_call(
        place_kernel,
        in_specs=[VMEM],
        out_specs=VMEM,
        out_shape=jax.ShapeDtypeStruct((2, 13, 13, 24, 64), BF16),
        compiler_params=params(SMALL),
        cost_estimate=cost(1e8, 3e6),
        name="placed_back",
    )(parts)


def fc_weight_kernel(place_ref, flat_0, flat_1, flat_2, flat_3, own_ref, other_ref, out_ref):
    core = place_ref[0]
    lead = first_half((576, 128))
    zero = jnp.zeros((576, 128), BF16)
    flats = [ref[h] for ref in (flat_0, flat_1, flat_2, flat_3) for h in range(2)]
    lefts = [
        jnp.concatenate([jnp.where(lead, flat, zero) for flat in flats], axis=1),
        jnp.concatenate([jnp.where(lead, zero, flat) for flat in flats], axis=1),
    ]
    for ref, parity in ((own_ref, core), (other_ref, 1 - core)):
        for half in range(2):
            right = jnp.concatenate(
                [ref[place_ref[1 + k], 128 * half : 128 * half + 128] for k in range(8)], axis=0
            )
            at = pl.ds(pl.multiple_of(parity * 256 + 128 * half, 128), 128)
            for t in range(2):
                out_ref[t, :, at] = nn_dot(lefts[t], right)


def fc_weight_grad_of(place, flats, own, other):
    return pl.pallas_call(
        fc_weight_kernel,
        in_specs=[SMEM] + [VMEM] * 6,
        out_specs=VMEM,
        out_shape=jax.ShapeDtypeStruct((2, 576, 512), F32),
        compiler_params=params(SMALL),
        cost_estimate=cost(3e9, 5e6),
        name="fc_weight_grad",
    )(place, *flats, own, other)


def row_of(column):
    size = column.shape[0]
    eye = lax.broadcasted_iota(jnp.int32, (size, size), 0) == lax.broadcasted_iota(jnp.int32, (size, size), 1)
    return jnp.sum(jnp.where(eye, column, 0.0), axis=0, keepdims=True)


def total_kernel(part_0, part_1, part_2, part_3, conv_ref, bias_ref, first_ref, fc_bias_ref, second_ref):
    total = (part_0[...].astype(F32) + part_1[...].astype(F32)) + (part_2[...].astype(F32) + part_3[...].astype(F32))
    conv_ref[...] = total[0:288]
    for t in range(2):
        fc_bias_ref[t : t + 1] = total[288 + t : 289 + t, 0:256]
        bias_ref[t : t + 1] = row_of(total[288:304, 260 + t : 261 + t])
    for u in range(2):
        for v in range(2):
            line = 290 + 2 * u + v
            second_ref[u, v : v + 1] = total[line : line + 1, 0:256]
            place = 256 + u if u == v else 258 + v
            first_ref[u, v : v + 1] = row_of(total[288:304, place : place + 1])


def summed(parts):
    return pl.pallas_call(
        total_kernel,
        in_specs=[VMEM] * 4,
        out_specs=[VMEM] * 5,
        out_shape=[
            jax.ShapeDtypeStruct((288, 384), F32),
            jax.ShapeDtypeStruct((2, 16), F32),
            jax.ShapeDtypeStruct((2, 2, 16), F32),
            jax.ShapeDtypeStruct((2, 256), F32),
            jax.ShapeDtypeStruct((2, 2, 256), F32),
        ],
        compiler_params=params(SMALL),
        cost_estimate=cost(1e7, 3e6),
        name="summed",
    )(*parts)


def mp_moves(z_step, y_step, core_step):
    return [
        ((z * 4 + y) * 2 + c, (((z + z_step) % 2) * 4 + (y + y_step) % 4) * 2 + (c + core_step) % 2)
        for z in range(2)
        for y in range(4)
        for c in range(2)
    ]


def dp_moves(x_step, z_step):
    return [(x * 2 + h, ((x + x_step) % 4) * 2 + (h + z_step) % 2) for x in range(4) for h in range(2)]


SAME_CORE = [[2 * k + c for k in range(8)] for c in range(2)]


def over_mp(array, z_step=0, y_step=0, core_step=0):
    return lax.ppermute(array, "mp", mp_moves(z_step, y_step, core_step))


def over_dp(array, x_step=0, z_step=0):
    return lax.ppermute(array, "dp", dp_moves(x_step, z_step))


def dealt(array, groups=None, axis="mp"):
    return lax.all_to_all(array, axis, 0, 0, tiled=True, axis_index_groups=groups)


def pick(array, index, axis):
    return lax.dynamic_index_in_dim(array, index, axis, keepdims=False)


def local(
    inputs,
    conv_weight,
    conv_bias,
    first_stitch,
    fc_weight,
    fc_bias,
    second_stitch,
    crop_counts,
    out_grad,
):
    x = jnp.transpose(inputs, (0, 2, 3, 1, 4))
    kernels = jnp.transpose(conv_weight, (0, 1, 2, 4, 3)).reshape(2, 144, 384)
    stitch_one = jnp.transpose(first_stitch, (1, 2, 0))
    mp_at, dp_at = lax.axis_index("mp"), lax.axis_index("dp")
    z_at, y_at, core = mp_at // 8, (mp_at // 2) % 4, mp_at % 2
    x_at, h_at = dp_at // 2, dp_at % 2
    core_arg = core.astype(jnp.int32).reshape(1)

    pair = jnp.stack([pick(kernels, core, 0), over_mp(pick(kernels, 1 - core, 0), core_step=1)])
    blocks = dealt(jnp.broadcast_to(pair[None], (8, 2, 144, 384)), SAME_CORE)
    slope, pooled, flat_t, own, other = front(
        core_arg, x, fc_weight, kernels.reshape(288, 384), conv_bias, stitch_one
    )
    own, blocks = lax.optimization_barrier((own, blocks))
    own = (own.astype(F32) + over_mp(other, core_step=1).astype(F32)).astype(BF16)
    parts = dealt(own, SAME_CORE)

    flat_z = over_dp(flat_t, z_step=1)
    parts, flat_z = lax.optimization_barrier((parts, flat_z))
    output, grad_copies, sums = hidden_layer(
        crop_counts,
        parts,
        fc_bias.T,
        jnp.transpose(second_stitch, (1, 2, 0)),
        jnp.transpose(out_grad, (1, 2, 0)),
    )
    grads_own = dealt(grad_copies, SAME_CORE)
    flat_pair = jnp.stack([flat_t, flat_z])
    flats = [flat_pair] + [over_dp(flat_pair, x_step=k) for k in range(1, 4)]
    grads_other = over_mp(grads_own, core_step=1)
    slice_own = dealt(grads_own, axis="dp")
    send, pre, stats = back_fc(core_arg, grads_own, grads_other, fc_weight, stitch_one, pooled, slope)
    send, slice_own, flats = lax.optimization_barrier((send, slice_own, flats))
    slice_other = over_mp(slice_own, core_step=1)
    pre_all = dealt(send)

    weight_part = weight_grad(x, pre, sums, stats)
    kernels_all = turned(core_arg, blocks)
    weight_z = over_dp(weight_part, z_step=1)
    pre_all, weight_part = lax.optimization_barrier((pre_all, weight_part))
    input_part = input_grad_part(pre_all, kernels_all)
    input_part, weight_z = lax.optimization_barrier((input_part, weight_z))
    weight_pair = (weight_part.astype(F32) + weight_z.astype(F32)).astype(BF16)
    part = dealt(input_part)

    conv_sum, conv_bias_grad, first_sum, fc_bias_sum, second_sum = summed(
        [weight_pair] + [over_dp(weight_pair, x_step=k) for k in range(1, 4)]
    )
    crops_place = jnp.stack(
        [core] + [(x_at + 4 - k) % 4 * 2 + (h_at + dh) % 2 for k in range(4) for dh in range(2)]
    ).astype(jnp.int32)
    fc_weight_grad = fc_weight_grad_of(crops_place, flats, slice_own, slice_other)
    input_grad = jnp.transpose(placed_back(part), (0, 4, 1, 2, 3))

    conv_weight_grad = jnp.transpose(conv_sum.reshape(2, 3, 3, 16, 384), (0, 1, 2, 4, 3))
    first_stitch_grad = jnp.transpose(first_sum, (2, 0, 1))
    fc_bias_grad = fc_bias_sum.T
    second_stitch_grad = jnp.transpose(second_sum, (2, 0, 1))
    return (
        jnp.transpose(output, (2, 0, 1)),
        input_grad,
        conv_weight_grad,
        conv_bias_grad,
        first_stitch_grad,
        fc_weight_grad,
        fc_bias_grad,
        second_stitch_grad,
    )


def solution(mesh):
    placed = (
        P(None, "dp", None, None, None),
        P(None, None, None, None, "mp"),
        P(None, "mp"),
        P("mp", None, None),
        P(None, "mp", None),
        P("mp", None),
        P("mp", None, None),
        P("dp"),
        P("mp", None, "dp"),
    )
    return jax.shard_map(
        local,
        mesh=mesh,
        in_specs=placed,
        out_specs=(
            P("mp", None, "dp"),
            P(None, "dp", None, None, "mp"),
            P(None, None, None, None, "mp"),
            P(None, "mp"),
            P("mp", None, None),
            P(None, "mp", "dp"),
            P("mp", None),
            P("mp", None, None),
        ),
        check_vma=False,
    )
```

time: 548 us -> 150 us (0.27)
  local copies, waits for them, and re-layouts: 234 us -> 8.8 us
  matrix products: 163 us -> 0 us
  Pallas kernels: 0 us -> 48.6 us
  other arithmetic: 23.7 us -> 3.06 us
  between operations: 16.4 us -> 0.83 us
  waiting for transfers between devices: 46 us -> 31.4 us
    pad x6 -> x0, local copies, waits for them, and re-layouts: 211 us -> none  [unpool_axis(): placed = lax.pad(values, jnp.float32(0.0), config)]
    conv_general_dilated x4 -> x0, matrix products: 90.3 us -> none  [the longest x2 61.4 us: local(): lax.conv_general_dilated(inputs[tower_index], conv_weight[tower_index], (...]
    dot_general x12 -> x0, matrix products: 72.5 us -> none  [the longest x9 54.1 us: local(): jnp.einsum('trijc,trijo->tco', window_in, pre_grad, preferred_element_typ...]
    pallas_call x0 -> x9, Pallas kernels: none -> 48.6 us  [the longest x1 14.5 us: front(): pl.pallas_call(front_kernel, in_specs=[SMEM, ANY, ANY, VMEM, VMEM, VMEM],...]
    all_to_all x7 -> x5, waiting for transfers between devices: 38.6 us -> 11.3 us  [dealt(): lax.all_to_all(array, axis, 0, 0, tiled=True, axis_index_groups=groups)]
    ppermute x0 -> x12, waiting for transfers between devices: none -> 20.1 us  [the longest x8 19.1 us: over_dp(): return lax.ppermute(array, 'dp', dp_moves(x_step, z_step))]
    all_to_all x7 -> x5, starting transfers between devices: 41.8 us -> 23.3 us  [dealt(): lax.all_to_all(array, axis, 0, 0, tiled=True, axis_index_groups=groups)]
    ppermute x0 -> x12, starting transfers between devices: none -> 17.2 us  [the longest x8 12.6 us: over_dp(): return lax.ppermute(array, 'dp', dp_moves(x_step, z_step))]
  transfers between devices with their start and end apart: 9 -> 17, of which waited for: 5 -> 8; matrix products, arithmetic and copies ran while one was open for 57% -> 1% of each run, Pallas kernels for 0% -> 30%
where the time goes in v2:
time: 150 us; the launch traced here: 149 us
  Pallas kernels  48.6 us (32%)
  starting transfers between devices  40.5 us (27%)
  waiting for transfers between devices  31.4 us (21%)
  blocking collectives  16.1 us (11%)
  local copies, waits for them, and re-layouts  8.8 us (6%)
  other arithmetic  3.06 us (2%)
    all_to_all x5, starting transfers between devices, dealt(): lax.all_to_all(array, axis, 0, 0, tiled=True, axis_index_groups=groups)  23.3 us
    ppermute x8, waiting for transfers between devices, over_dp(): return lax.ppermute(array, 'dp', dp_moves(x_step, z_step))  19.1 us
    all_to_all x1, blocking collectives, dealt(): lax.all_to_all(array, axis, 0, 0, tiled=True, axis_index_groups=groups)  16.1 us
    pallas_call x1, Pallas kernels, front(): pl.pallas_call(front_kernel, in_specs=[SMEM, ANY, ANY, VMEM, VMEM, VMEM],...  14.5 us
    ppermute x8, starting transfers between devices, over_dp(): return lax.ppermute(array, 'dp', dp_moves(x_step, z_step))  12.6 us
    all_to_all x5, waiting for transfers between devices, dealt(): lax.all_to_all(array, axis, 0, 0, tiled=True, axis_index_groups=groups)  11.3 us
    pallas_call x1, Pallas kernels, weight_grad(): pl.pallas_call(weight_kernel, in_specs=[ANY, VMEM, VMEM, VMEM], out_specs...  9.57 us
    pallas_call x1, Pallas kernels, back_fc(): pl.pallas_call(back_kernel, in_specs=[SMEM, ANY, ANY, ANY, VMEM, ANY, ANY...  9.43 us
  transfers between devices with their start and end apart: 17, of which 8 were waited for; matrix products, arithmetic and copies ran while one was open for 1% of the time, Pallas kernels for 30%

profile of v2, /device:TPU:1, one launch (start us, length us, event | category | flops | bytes accessed | tf_op | source)
XLA Modules:
  0.0 149.4 jit_solution(1659331270126206990)
XLA Ops:
  1.6 1.5 %collective-permute-start = (bf16[144,384]{1,0:T(8,128)(2,1)S(1)}, bf16[144,384]{1,0:T(8,128)(2,1)S(1)}, u32[]{:S(2)}, u32[]{:S(2)}) collective-permute-start(bf16[144,384]{1,0:T(8,128)(2,1)S(1)} %get-tuple-element.69), channel_id=1, source_target_pairs={{0,8},{8,0},{16,24},{24,16},{32,40},{40,32},{48,56},{56,48},{64,72... | collective-permute-start | bytes 331784 | tf_op jit(solution)/shard_map/ppermute | solution.py:635
  5.5 5.6 %all-to-all-start = ((bf16[8,2,144,384]{3,2,1,0:T(8,128)(2,1)}), bf16[8,2,144,384]{3,2,1,0:T(8,128)(2,1)S(1)}, u32[]{:S(2)}, u32[]{:S(2)}) async-start(bf16[8,2,144,384]{3,2,1,0:T(8,128)(2,1)} %broadcast_in_dim.2), calls=%async_computation | async-start | bytes 3538944 | tf_op jit(solution)/shard_map/all_to_all | solution.py:643
  11.1 14.5 %front.1 = (bf16[13,13,16,128]{3,2,1,0:T(8,128)(2,1)}, f32[36,16,128]{2,1,0:T(8,128)}, bf16[576,128]{1,0:T(8,128)(2,1)}, bf16[8,128,256]{2,1,0:T(8,128)(2,1)}, bf16[8,128,256]{2,1,0:T(8,128)(2,1)}) custom-call(s32[1]{0:T(128)} %bitcast.core_ref, bf16[2,13,13,64,384]{4,3,2,1,0:T(8,128)(2,1)} %bitcast.43, bf16[2,576,4096]{2,1,0:T(8,128)(2,1)} %w_ref.3, ...), custom_call_target="tpu_custom_call" | custom-call | flops 10000000000 | bytes 30000000 | tf_op jit(solution)/shard_map/front/pallas_call | solution.py:196
  26.4 8.3 %all-to-all-done.blocks_ref = bf16[8,2,144,384]{3,2,1,0:T(8,128)(2,1)S(1)} async-done(((bf16[8,2,144,384]{3,2,1,0:T(8,128)(2,1)}), bf16[8,2,144,384]{3,2,1,0:T(8,128)(2,1)S(1)}, u32[]{:S(2)}, u32[]{:S(2)}) %all-to-all-start) | async-done | bytes 1769504 | tf_op jit(solution)/shard_map/all_to_all | solution.py:643
  34.7 2.0 %add_convert_fusion = bf16[8,128,256]{2,1,0:T(8,128)(2,1)} fusion(bf16[8,128,256]{2,1,0:T(8,128)(2,1)S(1)} %collective-permute-done.1, bf16[8,128,256]{2,1,0:T(8,128)(2,1)} %get-tuple-element.39), kind=kLoop, calls=%fused_computation | loop fusion | flops 1048576 | bytes 1572864 | tf_op jit(solution)/shard_map/convert_element_type | solution.py:675
  36.7 4.2 %all-to-all-start.1 = ((bf16[8,128,256]{2,1,0:T(8,128)(2,1)}), bf16[8,128,256]{2,1,0:T(8,128)(2,1)S(1)}, u32[]{:S(2)}, u32[]{:S(2)}) async-start(bf16[8,128,256]{2,1,0:T(8,128)(2,1)} %add_convert_fusion), calls=%async_computation.1 | async-start | bytes 1048576 | tf_op jit(solution)/shard_map/all_to_all | solution.py:643
  40.8 3.4 %collective-permute-start.2 = (bf16[576,128]{1,0:T(8,128)(2,1)S(1)}, bf16[576,128]{1,0:T(8,128)(2,1)S(1)}, u32[]{:S(2)}, u32[]{:S(2)}) collective-permute-start(bf16[576,128]{1,0:T(8,128)(2,1)S(1)} %copy-done.13), channel_id=1, source_target_pairs={{0,1},{1,0},{2,3},{3,2},{4,5},{5,4},{6,7},{7,6},{8,9},{9,8},{10,11... | collective-permute-start | bytes 442376 | tf_op jit(solution)/shard_map/ppermute | solution.py:639
  44.2 6.7 %collective-permute-done.2 = bf16[576,128]{1,0:T(8,128)(2,1)S(1)} collective-permute-done((bf16[576,128]{1,0:T(8,128)(2,1)S(1)}, bf16[576,128]{1,0:T(8,128)(2,1)S(1)}, u32[]{:S(2)}, u32[]{:S(2)}) %collective-permute-start.2) | collective-permute-done | bytes 147488 | tf_op jit(solution)/shard_map/ppermute | solution.py:639
  53.0 16.1 %all_to_all.30.own_ref = bf16[8,256,128]{2,1,0:T(8,128)(2,1)} all-to-all(bf16[8,256,128]{2,1,0:T(8,128)(2,1)S(1)} %get-tuple-element.44), channel_id=1, replica_groups={{0,16,32,48,64,80,96,112},{8,24,40,56,72,88,104,120},{1,17,33,49,65,81,..., dimensions={0} | all-to-all | bytes 1048576 | tf_op jit(solution)/shard_map/all_to_all | solution.py:643
  69.2 2.2 %collective-permute-start.3 = (bf16[8,256,128]{2,1,0:T(8,128)(2,1)}, bf16[8,256,128]{2,1,0:T(8,128)(2,1)S(1)}, u32[]{:S(2)}, u32[]{:S(2)}) collective-permute-start(bf16[8,256,128]{2,1,0:T(8,128)(2,1)} %all_to_all.30.own_ref), channel_id=1, source_target_pairs={{0,8},{8,0},{16,24},{24,16},{32,40},{40,32},{48,56},{56,48},{64,72... | collective-permute-start | bytes 1572872 | tf_op jit(solution)/shard_map/ppermute | solution.py:635
  71.3 4.6 %all-to-all-start.3 = ((bf16[8,256,128]{2,1,0:T(8,128)(2,1)}), bf16[8,256,128]{2,1,0:T(8,128)(2,1)S(1)}, u32[]{:S(2)}, u32[]{:S(2)}) async-start(bf16[8,256,128]{2,1,0:T(8,128)(2,1)} %all_to_all.30.own_ref), calls=%async_computation.3 | async-start | bytes 1048576 | tf_op jit(solution)/shard_map/all_to_all | solution.py:643
  76.9 2.7 %collective-permute-start.6 = (bf16[2,576,128]{2,1,0:T(8,128)(2,1)S(1)}, bf16[2,576,128]{2,1,0:T(8,128)(2,1)S(1)}, u32[]{:S(2)}, u32[]{:S(2)}) collective-permute-start(bf16[2,576,128]{2,1,0:T(8,128)(2,1)S(1)} %pad_maximum_fusion.flat_0), channel_id=1, source_target_pairs={{0,6},{1,7},{2,0},{3,1},{4,2},{5,3},{6,4},{7,5},{8,14},{9,15},{10,... | collective-permute-start | bytes 884744 | tf_op jit(solution)/shard_map/ppermute | solution.py:639
  82.4 9.4 %back_fc.1 = (bf16[16,16,1664]{2,1,0:T(8,128)(2,1)}, bf16[13,13,16,128]{3,2,1,0:T(8,128)(2,1)}, f32[16,128]{1,0:T(8,128)}) custom-call(s32[1]{0:T(128)} %bitcast.core_ref, bf16[8,256,128]{2,1,0:T(8,128)(2,1)} %all_to_all.30.own_ref, bf16[8,256,128]{2,1,0:T(8,128)(2,1)} %copy-done.11, bf16[2,576,4096]{2,1,0:T(8,128)(2,1)} %w_ref.3, f32[2,2,16]{2,1,0:T(2,128)} %bitcast.42, ...), custom_call_target="tpu_custom_call" | custom-call | flops 100000000 | bytes 1000000 | tf_op jit(solution)/shard_map/back_fc/pallas_call | solution.py:371
  92.6 5.9 %collective-permute-done.4.flat_1 = bf16[2,576,128]{2,1,0:T(8,128)(2,1)S(1)} collective-permute-done((bf16[2,576,128]{2,1,0:T(8,128)(2,1)S(1)}, bf16[2,576,128]{2,1,0:T(8,128)(2,1)S(1)}, u32[]{:S(2)}, u32[]{:S(2)}) %collective-permute-start.4) | collective-permute-done | bytes 294944 | tf_op jit(solution)/shard_map/ppermute | solution.py:639
  99.2 3.9 %all-to-all-start.4 = ((bf16[16,16,1664]{2,1,0:T(8,128)(2,1)}), bf16[16,16,1664]{2,1,0:T(8,128)(2,1)S(1)}, u32[]{:S(2)}, u32[]{:S(2)}) async-start(bf16[16,16,1664]{2,1,0:T(8,128)(2,1)} %get-tuple-element.49), calls=%async_computation.4 | async-start | bytes 1703936 | tf_op jit(solution)/shard_map/all_to_all | solution.py:643
  103.1 9.6 %weight_grad.1 = bf16[304,384]{1,0:T(8,128)(2,1)} custom-call(bf16[2,13,13,64,384]{4,3,2,1,0:T(8,128)(2,1)} %bitcast.44, bf16[13,13,16,128]{3,2,1,0:T(8,128)(2,1)} %get-tuple-element.50.pre_ref, f32[8,256]{1,0:T(8,128)} %copy-done.8, f32[16,128]{1,0:T(8,128)} %get-tuple-element.52.stats_ref), custom_call_target="tpu_custom_call" | custom-call | flops 10000000000 | bytes 20000000 | tf_op jit(solution)/shard_map/weight_grad/pallas_call | solution.py:444
  112.7 2.5 %collective-permute-start.7 = (bf16[304,384]{1,0:T(8,128)(2,1)}, bf16[304,384]{1,0:T(8,128)(2,1)S(1)}, u32[]{:S(2)}, u32[]{:S(2)}) collective-permute-start(bf16[304,384]{1,0:T(8,128)(2,1)} %weight_grad.1), channel_id=1, source_target_pairs={{0,1},{1,0},{2,3},{3,2},{4,5},{5,4},{6,7},{7,6},{8,9},{9,8},{10,11... | collective-permute-start | bytes 700424 | tf_op jit(solution)/shard_map/ppermute | solution.py:639
  115.2 1.8 %all-to-all-done.4.g_ref = bf16[16,16,1664]{2,1,0:T(8,128)(2,1)S(1)} async-done(((bf16[16,16,1664]{2,1,0:T(8,128)(2,1)}), bf16[16,16,1664]{2,1,0:T(8,128)(2,1)S(1)}, u32[]{:S(2)}, u32[]{:S(2)}) %all-to-all-start.4) | async-done | bytes 852000 | tf_op jit(solution)/shard_map/all_to_all | solution.py:643
  118.5 4.5 %input_grad.1 = bf16[16,24,1664]{2,1,0:T(8,128)(2,1)} custom-call(bf16[16,16,1664]{2,1,0:T(8,128)(2,1)S(1)} %all-to-all-done.4.g_ref, bf16[384,2304]{1,0:T(8,128)(2,1)S(1)} %copy-done.10), custom_call_target="tpu_custom_call" | custom-call | flops 4000000000 | bytes 4000000 | tf_op jit(solution)/shard_map/input_grad/pallas_call | solution.py:515
  123.0 5.0 %all-to-all-start.5 = ((bf16[16,24,1664]{2,1,0:T(8,128)(2,1)}), bf16[16,24,1664]{2,1,0:T(8,128)(2,1)S(1)}, u32[]{:S(2)}, u32[]{:S(2)}) async-start(bf16[16,24,1664]{2,1,0:T(8,128)(2,1)} %input_grad.1), calls=%async_computation.5 | async-start | bytes 2555904 | tf_op jit(solution)/shard_map/all_to_all | solution.py:643
  128.4 1.7 %collective-permute-start.10 = (bf16[304,384]{1,0:T(8,128)(2,1)S(1)}, bf16[304,384]{1,0:T(8,128)(2,1)S(1)}, u32[]{:S(2)}, u32[]{:S(2)}) collective-permute-start(bf16[304,384]{1,0:T(8,128)(2,1)S(1)} %add_convert_fusion.1.part_0), channel_id=1, source_target_pairs={{0,6},{1,7},{2,0},{3,1},{4,2},{5,3},{6,4},{7,5},{8,14},{9,15},{10,... | collective-permute-start | bytes 700424 | tf_op jit(solution)/shard_map/ppermute | solution.py:639
  133.2 4.5 %fc_weight_grad.1 = f32[2,576,512]{2,1,0:T(8,128)} custom-call(s32[9]{0:T(128)S(1)} %stack.57.place_ref, bf16[2,576,128]{2,1,0:T(8,128)(2,1)S(1)} %pad_maximum_fusion.flat_0, bf16[2,576,128]{2,1,0:T(8,128)(2,1)S(1)} %copy-done.7, bf16[2,576,128]{2,1,0:T(8,128)(2,1)S(1)} %copy-done.5, bf16[2,576,128]{2,1,0:T(8,128)(2,1)S(1)} %collective-permute-done.6.flat_3, ...), custom_call_target="tpu_custom_call" | custom-call | flops 3000000000 | bytes 5000000 | tf_op jit(solution)/shard_map/fc_weight_grad/pallas_call | solution.py:569
  138.3 5.9 %collective-permute-done.8.part_1 = bf16[304,384]{1,0:T(8,128)(2,1)S(1)} collective-permute-done((bf16[304,384]{1,0:T(8,128)(2,1)S(1)}, bf16[304,384]{1,0:T(8,128)(2,1)S(1)}, u32[]{:S(2)}, u32[]{:S(2)}) %collective-permute-start.8) | collective-permute-done | bytes 233504 | tf_op jit(solution)/shard_map/ppermute | solution.py:639
  146.4 3.0 %placed_back.1 = bf16[2,13,13,24,64]{4,3,2,1,0:T(8,128)(2,1)} custom-call(bf16[16,24,1664]{2,1,0:T(8,128)(2,1)S(1)} %all-to-all-done.5.part_ref), custom_call_target="tpu_custom_call" | custom-call | flops 100000000 | bytes 3000000 | tf_op jit(solution)/shard_map/placed_back/pallas_call | solution.py:538
  (57 shorter events, 18.9 us)
Async XLA Ops:
  1.6 2.5 %collective-permute-start = (bf16[144,384]{1,0:T(8,128)(2,1)S(1)}, bf16[144,384]{1,0:T(8,128)(2,1)S(1)}, u32[]{:S(2)}, u32[]{:S(2)}) collective-permute-start(bf16[144,384]{1,0:T(8,128)(2,1)S(1)} %get-tuple-element.69), channel_id=1, source_target_pairs={{0,8},{8,0},{16,24},{24,16},{32,40},{40,32},{48,56},{56,48},{64,72... | collective-permute-start | bytes 331784 | tf_op jit(solution)/shard_map/ppermute | solution.py:635
  5.5 29.2 %all-to-all-start = ((bf16[8,2,144,384]{3,2,1,0:T(8,128)(2,1)}), bf16[8,2,144,384]{3,2,1,0:T(8,128)(2,1)S(1)}, u32[]{:S(2)}, u32[]{:S(2)}) async-start(bf16[8,2,144,384]{3,2,1,0:T(8,128)(2,1)} %broadcast_in_dim.2), calls=%async_computation | async-start | bytes 3538944 | tf_op jit(solution)/shard_map/all_to_all | solution.py:643
  25.6 15.2 %copy-start.13 = (bf16[576,128]{1,0:T(8,128)(2,1)S(1)}, bf16[576,128]{1,0:T(8,128)(2,1)}, u32[]{:S(2)}) copy-start(bf16[576,128]{1,0:T(8,128)(2,1)} %get-tuple-element.41) | copy-start | bytes 442372
  25.6 26.0 %copy-start = (bf16[256,2,64]{0,2,1:T(8,128)(2,1)S(1)}, bf16[256,2,64]{0,2,1:T(8,128)(2,1)}, u32[]{:S(2)}) copy-start(bf16[256,2,64]{0,2,1:T(8,128)(2,1)} %param.17) | copy-start | bytes 196612
  25.6 25.9 %copy-start.1 = (f32[256,2,2]{0,2,1:T(2,128)S(1)}, f32[256,2,2]{0,2,1:T(2,128)}, u32[]{:S(2)}) copy-start(f32[256,2,2]{0,2,1:T(2,128)} %param.15) | copy-start | bytes 12292
  25.6 25.9 %copy-start.2 = (f32[256,2]{0,1:T(2,128)S(1)}, f32[256,2]{0,1:T(2,128)}, u32[]{:S(2)}) copy-start(f32[256,2]{0,1:T(2,128)} %param.14) | copy-start | bytes 6148
  25.7 25.9 %copy-start.3 = (s32[8]{0:T(128)S(1)}, s32[8]{0:T(128)}, u32[]{:S(2)}) copy-start(s32[8]{0:T(128)} %counts_ref.1) | copy-start | bytes 100
  25.7 9.0 %collective-permute-start.1 = (bf16[8,128,256]{2,1,0:T(8,128)(2,1)}, bf16[8,128,256]{2,1,0:T(8,128)(2,1)S(1)}, u32[]{:S(2)}, u32[]{:S(2)}) collective-permute-start(bf16[8,128,256]{2,1,0:T(8,128)(2,1)} %get-tuple-element.40), channel_id=1, source_target_pairs={{0,8},{8,0},{16,24},{24,16},{32,40},{40,32},{48,56},{56,48},{64,72... | collective-permute-start | bytes 1572872 | tf_op jit(solution)/shard_map/ppermute | solution.py:635
  36.7 14.3 %all-to-all-start.1 = ((bf16[8,128,256]{2,1,0:T(8,128)(2,1)}), bf16[8,128,256]{2,1,0:T(8,128)(2,1)S(1)}, u32[]{:S(2)}, u32[]{:S(2)}) async-start(bf16[8,128,256]{2,1,0:T(8,128)(2,1)} %add_convert_fusion), calls=%async_computation.1 | async-start | bytes 1048576 | tf_op jit(solution)/shard_map/all_to_all | solution.py:643
  40.8 10.1 %collective-permute-start.2 = (bf16[576,128]{1,0:T(8,128)(2,1)S(1)}, bf16[576,128]{1,0:T(8,128)(2,1)S(1)}, u32[]{:S(2)}, u32[]{:S(2)}) collective-permute-start(bf16[576,128]{1,0:T(8,128)(2,1)S(1)} %copy-done.13), channel_id=1, source_target_pairs={{0,1},{1,0},{2,3},{3,2},{4,5},{5,4},{6,7},{7,6},{8,9},{9,8},{10,11... | collective-permute-start | bytes 442376 | tf_op jit(solution)/shard_map/ppermute | solution.py:639
  53.0 16.2 %copy-start.8 = (f32[8,256]{1,0:T(8,128)}, f32[8,256]{1,0:T(8,128)S(1)}, u32[]{:S(2)}) copy-start(f32[8,256]{1,0:T(8,128)S(1)} %get-tuple-element.51.sums_ref) | copy-start | bytes 24580
  69.2 12.4 %collective-permute-start.3 = (bf16[8,256,128]{2,1,0:T(8,128)(2,1)}, bf16[8,256,128]{2,1,0:T(8,128)(2,1)S(1)}, u32[]{:S(2)}, u32[]{:S(2)}) collective-permute-start(bf16[8,256,128]{2,1,0:T(8,128)(2,1)} %all_to_all.30.own_ref), channel_id=1, source_target_pairs={{0,8},{8,0},{16,24},{24,16},{32,40},{40,32},{48,56},{56,48},{64,72... | collective-permute-start | bytes 1572872 | tf_op jit(solution)/shard_map/ppermute | solution.py:635
  71.3 27.9 %all-to-all-start.3 = ((bf16[8,256,128]{2,1,0:T(8,128)(2,1)}), bf16[8,256,128]{2,1,0:T(8,128)(2,1)S(1)}, u32[]{:S(2)}, u32[]{:S(2)}) async-start(bf16[8,256,128]{2,1,0:T(8,128)(2,1)} %all_to_all.30.own_ref), calls=%async_computation.3 | async-start | bytes 1048576 | tf_op jit(solution)/shard_map/all_to_all | solution.py:643
  76.9 14.9 %collective-permute-start.6 = (bf16[2,576,128]{2,1,0:T(8,128)(2,1)S(1)}, bf16[2,576,128]{2,1,0:T(8,128)(2,1)S(1)}, u32[]{:S(2)}, u32[]{:S(2)}) collective-permute-start(bf16[2,576,128]{2,1,0:T(8,128)(2,1)S(1)} %pad_maximum_fusion.flat_0), channel_id=1, source_target_pairs={{0,6},{1,7},{2,0},{3,1},{4,2},{5,3},{6,4},{7,5},{8,14},{9,15},{10,... | collective-permute-start | bytes 884744 | tf_op jit(solution)/shard_map/ppermute | solution.py:639
  79.7 12.2 %collective-permute-start.5 = (bf16[2,576,128]{2,1,0:T(8,128)(2,1)S(1)}, bf16[2,576,128]{2,1,0:T(8,128)(2,1)S(1)}, u32[]{:S(2)}, u32[]{:S(2)}) collective-permute-start(bf16[2,576,128]{2,1,0:T(8,128)(2,1)S(1)} %pad_maximum_fusion.flat_0), channel_id=1, source_target_pairs={{0,4},{1,5},{2,6},{3,7},{4,0},{5,1},{6,2},{7,3},{8,12},{9,13},{10,... | collective-permute-start | bytes 884744 | tf_op jit(solution)/shard_map/ppermute | solution.py:639
  80.3 18.2 %collective-permute-start.4 = (bf16[2,576,128]{2,1,0:T(8,128)(2,1)S(1)}, bf16[2,576,128]{2,1,0:T(8,128)(2,1)S(1)}, u32[]{:S(2)}, u32[]{:S(2)}) collective-permute-start(bf16[2,576,128]{2,1,0:T(8,128)(2,1)S(1)} %pad_maximum_fusion.flat_0), channel_id=1, source_target_pairs={{0,2},{1,3},{2,4},{3,5},{4,6},{5,7},{6,0},{7,1},{8,10},{9,11},{10,... | collective-permute-start | bytes 884744 | tf_op jit(solution)/shard_map/ppermute | solution.py:639
  81.5 10.3 %copy-start.9 = (bf16[384,2304]{1,0:T(8,128)(2,1)}, bf16[384,2304]{1,0:T(8,128)(2,1)S(1)}, u32[]{:S(2)}) copy-start(bf16[384,2304]{1,0:T(8,128)(2,1)S(1)} %turned_kernels.1.w_ref) | copy-start | bytes 5308420
  99.2 17.8 %all-to-all-start.4 = ((bf16[16,16,1664]{2,1,0:T(8,128)(2,1)}), bf16[16,16,1664]{2,1,0:T(8,128)(2,1)S(1)}, u32[]{:S(2)}, u32[]{:S(2)}) async-start(bf16[16,16,1664]{2,1,0:T(8,128)(2,1)} %get-tuple-element.49), calls=%async_computation.4 | async-start | bytes 1703936 | tf_op jit(solution)/shard_map/all_to_all | solution.py:643
  112.7 10.3 %collective-permute-start.7 = (bf16[304,384]{1,0:T(8,128)(2,1)}, bf16[304,384]{1,0:T(8,128)(2,1)S(1)}, u32[]{:S(2)}, u32[]{:S(2)}) collective-permute-start(bf16[304,384]{1,0:T(8,128)(2,1)} %weight_grad.1), channel_id=1, source_target_pairs={{0,1},{1,0},{2,3},{3,2},{4,5},{5,4},{6,7},{7,6},{8,9},{9,8},{10,11... | collective-permute-start | bytes 700424 | tf_op jit(solution)/shard_map/ppermute | solution.py:639
  123.0 23.3 %all-to-all-start.5 = ((bf16[16,24,1664]{2,1,0:T(8,128)(2,1)}), bf16[16,24,1664]{2,1,0:T(8,128)(2,1)S(1)}, u32[]{:S(2)}, u32[]{:S(2)}) async-start(bf16[16,24,1664]{2,1,0:T(8,128)(2,1)} %input_grad.1), calls=%async_computation.5 | async-start | bytes 2555904 | tf_op jit(solution)/shard_map/all_to_all | solution.py:643
  128.0 3.2 %collective-permute-start.11 = (bf16[8,256,128]{2,1,0:T(8,128)(2,1)S(1)}, bf16[8,256,128]{2,1,0:T(8,128)(2,1)S(1)}, u32[]{:S(2)}, u32[]{:S(2)}) collective-permute-start(bf16[8,256,128]{2,1,0:T(8,128)(2,1)S(1)} %all-to-all-done.3.own_ref), channel_id=1, source_target_pairs={{0,8},{8,0},{16,24},{24,16},{32,40},{40,32},{48,56},{56,48},{64,72... | collective-permute-start | bytes 1572872 | tf_op jit(solution)/shard_map/ppermute | solution.py:635
  128.4 9.4 %collective-permute-start.10 = (bf16[304,384]{1,0:T(8,128)(2,1)S(1)}, bf16[304,384]{1,0:T(8,128)(2,1)S(1)}, u32[]{:S(2)}, u32[]{:S(2)}) collective-permute-start(bf16[304,384]{1,0:T(8,128)(2,1)S(1)} %add_convert_fusion.1.part_0), channel_id=1, source_target_pairs={{0,6},{1,7},{2,0},{3,1},{4,2},{5,3},{6,4},{7,5},{8,14},{9,15},{10,... | collective-permute-start | bytes 700424 | tf_op jit(solution)/shard_map/ppermute | solution.py:639
  130.1 8.2 %collective-permute-start.9 = (bf16[304,384]{1,0:T(8,128)(2,1)S(1)}, bf16[304,384]{1,0:T(8,128)(2,1)S(1)}, u32[]{:S(2)}, u32[]{:S(2)}) collective-permute-start(bf16[304,384]{1,0:T(8,128)(2,1)S(1)} %add_convert_fusion.1.part_0), channel_id=1, source_target_pairs={{0,4},{1,5},{2,6},{3,7},{4,0},{5,1},{6,2},{7,3},{8,12},{9,13},{10,... | collective-permute-start | bytes 700424 | tf_op jit(solution)/shard_map/ppermute | solution.py:639
  131.3 12.9 %collective-permute-start.8 = (bf16[304,384]{1,0:T(8,128)(2,1)S(1)}, bf16[304,384]{1,0:T(8,128)(2,1)S(1)}, u32[]{:S(2)}, u32[]{:S(2)}) collective-permute-start(bf16[304,384]{1,0:T(8,128)(2,1)S(1)} %add_convert_fusion.1.part_0), channel_id=1, source_target_pairs={{0,2},{1,3},{2,4},{3,5},{4,6},{5,7},{6,0},{7,1},{8,10},{9,11},{10,... | collective-permute-start | bytes 700424 | tf_op jit(solution)/shard_map/ppermute | solution.py:639
  (8 other events, 11.7 us)

commit v3 on v2

--- a/solution.py
+++ b/solution.py
@@ -7,7 +7,7 @@
 
 F32 = jnp.float32
 BF16 = jnp.bfloat16
-LARGE, SMALL = 58, 16
+LARGE, MEDIUM, SMALL = 56, 50, 16
 
 
 def params(mib=LARGE):
@@ -109,10 +109,11 @@
     own, into, _ = stitch_slabs(stitch_ref)
 
     def gather(row):
+        line = jnp.maximum(row + 1, 0)
         for t in range(2):
-            right = pltpu.roll(acc[t, 0, row + 1], 64, 1)
-            left = pltpu.roll(acc[t, 2, row + 1], 832, 1)
-            ready[t] = acc[t, 1, row + 1] + right + left
+            right = pltpu.roll(acc[t, 0, line], 64, 1)
+            left = pltpu.roll(acc[t, 2, line], 832, 1)
+            ready[t] = acc[t, 1, line] + right + left
 
     def finish(row):
         acts = []
@@ -129,12 +130,13 @@
         even = row % 2 == 0
         for q in range(6):
             total = acts[2 * q] + acts[2 * q + 1] + acts[2 * q + 2]
-            pool[(row + 2) // 2, q] += total
+            pool[jnp.maximum(row + 2, 0) // 2, q] += total
             pool[jnp.maximum(row, 0) // 2, q] += jnp.where(even, total, 0.0)
 
     def line(i, carry):
         x_copy(i).wait()
-        finish(i - 2)
+        finish(i - 3)
+        gather(i - 2)
         for t in range(2):
             weights = kernel_ref[144 * t : 144 * t + 144]
             for start in range(0, 13, 4):
@@ -145,16 +147,15 @@
                     for b in range(3):
                         top = 16 * (3 * a + b)
                         acc[t, b, i + 2 - a, :, 64 * start : 64 * (start + width)] += product[top : top + 16]
-        gather(i - 1)
         return carry
 
     def last(i, carry):
-        finish(i - 2)
-        gather(jnp.minimum(i - 1, 12))
+        finish(i - 3)
+        gather(jnp.minimum(i - 2, 12))
         return carry
 
     lax.fori_loop(0, 13, line, 0)
-    lax.fori_loop(13, 15, last, 0)
+    lax.fori_loop(13, 16, last, 0)
     for i in range(13):
         slope_copy(i).start()
     pooled = pool[1:7].reshape(36, 16, 128) * (1.0 / 9.0)
@@ -225,6 +226,52 @@
     )(core, x, w, kernels, bias, stitch)
 
 
+def pair_kernel(first_ref, second_ref, out_ref):
+    out_ref[...] = (first_ref[...].astype(F32) + second_ref[...].astype(F32)).astype(BF16)
+
+
+def pair_sum(first, second):
+    return pl.pallas_call(
+        pair_kernel,
+        in_specs=[VMEM, VMEM],
+        out_specs=VMEM,
+        out_shape=jax.ShapeDtypeStruct(first.shape, BF16),
+        compiler_params=params(SMALL),
+        cost_estimate=cost(1e6, 2e6),
+        name="pair_sum",
+    )(first, second)
+
+
+def fan_kernel(core_ref, near_ref, far_ref, out_ref, held, in_sem, out_sem):
+    core = core_ref[0]
+    for p, ref in enumerate((near_ref, far_ref)):
+        pltpu.make_async_copy(ref.at[core], held.at[p], in_sem.at[p]).start()
+    for p, ref in enumerate((near_ref, far_ref)):
+        pltpu.make_async_copy(ref.at[core], held.at[p], in_sem.at[p]).wait()
+    copies = [pltpu.make_async_copy(held, out_ref.at[k], out_sem.at[k]) for k in range(8)]
+    for copy in copies:
+        copy.start()
+    for copy in copies:
+        copy.wait()
+
+
+def fanned(core, near, far):
+    return pl.pallas_call(
+        fan_kernel,
+        in_specs=[SMEM, ANY, ANY],
+        out_specs=ANY,
+        out_shape=jax.ShapeDtypeStruct((8, 2, 144, 384), BF16),
+        scratch_shapes=[
+            pltpu.VMEM((2, 144, 384), BF16),
+            pltpu.SemaphoreType.DMA((2,)),
+            pltpu.SemaphoreType.DMA((8,)),
+        ],
+        compiler_params=params(SMALL),
+        cost_estimate=cost(1e6, 4e6),
+        name="fanned",
+    )(core, near, far)
+
+
 def hidden_kernel(counts_ref, parts_ref, bias_ref, stitch_ref, cot_ref, out_ref, grad_ref, sums_ref):
     live = counts_ref[0]
     for k in range(1, 8):
@@ -277,22 +324,16 @@
 def back_kernel(
     core_ref, own_ref, other_ref, w_ref, stitch_ref, pooled_ref, slope_ref,
     send_ref, pre_ref, stats_ref,
-    ws, grads, pooled, slopes, sends, pres, w_sem, in_sem, send_sem, pre_sem,
+    ws, pooled, slopes, sends, w_sem, in_sem, send_sem,
 ):
     def w_copy(k):
         at = pl.ds(1024 * k, 1024)
         return pltpu.make_async_copy(w_ref.at[:, :, at], ws.at[:, :, at], w_sem.at[k])
 
-    first_in = [
-        pltpu.make_async_copy(own_ref, grads.at[0], in_sem.at[0]),
-        pltpu.make_async_copy(other_ref, grads.at[1], in_sem.at[1]),
+    later_in = [
+        pltpu.make_async_copy(pooled_ref, pooled, in_sem.at[0]),
+        pltpu.make_async_copy(slope_ref, slopes, in_sem.at[1]),
     ]
-    later_in = [
-        pltpu.make_async_copy(pooled_ref, pooled, in_sem.at[2]),
-        pltpu.make_async_copy(slope_ref, slopes, in_sem.at[3]),
-    ]
-    for copy in first_in:
-        copy.start()
     for k in range(4):
         w_copy(k).start()
     for copy in later_in:
@@ -300,14 +341,12 @@
     first = core_ref[0] == 0
     perm = slab_order(1)
     own_slab, _, back_slab = stitch_slabs(stitch_ref)
-    for copy in first_in:
-        copy.wait()
     totals = [jnp.zeros((576, 128), F32)] * 2
     for k in range(4):
         w_copy(k).wait()
         blocks = []
         for q in (2 * k, 2 * k + 1):
-            own, other = (jnp.concatenate([grads[p, q, 0:128], grads[p, q, 128:256]], axis=1) for p in range(2))
+            own, other = (jnp.concatenate([ref[q, 0:128], ref[q, 128:256]], axis=1) for ref in (own_ref, other_ref))
             blocks += [jnp.where(first, own, other), jnp.where(first, other, own)]
         rows = jnp.concatenate(blocks, axis=1)
         for t in range(2):
@@ -340,7 +379,7 @@
             if len(windows) == 2:
                 value = value + widened[windows[1]][j]
             value = (value * slopes[i, j].astype(F32)).astype(BF16)
-            pres[i, j] = value
+            pre_ref[i, j] = value
             value = value.astype(F32)
             bias_sum = bias_sum + value
             slabs.append(value)
@@ -350,8 +389,6 @@
             block = (m % 2) * 8 + m // 2
             sends[m, :, 128 * i : 128 * i + 128] = slabs[block].astype(BF16)
         copies_out.append(pltpu.make_async_copy(sends.at[:, :, at], send_ref.at[:, :, at], send_sem.at[i]))
-        copies_out[-1].start()
-        copies_out.append(pltpu.make_async_copy(pres.at[i], pre_ref.at[i], pre_sem.at[i]))
         copies_out[-1].start()
     pooled_in = pooled[...]
     own = jnp.sum(mixed_grad * pooled_in, axis=0)
@@ -370,8 +407,8 @@
 def back_fc(core, own, other, w, stitch, pooled, slope):
     return pl.pallas_call(
         back_kernel,
-        in_specs=[SMEM, ANY, ANY, ANY, VMEM, ANY, ANY],
-        out_specs=[ANY, ANY, VMEM],
+        in_specs=[SMEM, VMEM, VMEM, ANY, VMEM, ANY, ANY],
+        out_specs=[ANY, VMEM, VMEM],
         out_shape=[
             jax.ShapeDtypeStruct((16, 16, 1664), BF16),
             jax.ShapeDtypeStruct((13, 13, 16, 128), BF16),
@@ -379,14 +416,11 @@
         ],
         scratch_shapes=[
             pltpu.VMEM((2, 576, 4096), BF16),
-            pltpu.VMEM((2, 8, 256, 128), BF16),
             pltpu.VMEM((36, 16, 128), F32),
             pltpu.VMEM((13, 13, 16, 128), BF16),
             pltpu.VMEM((16, 16, 1664), BF16),
-            pltpu.VMEM((13, 13, 16, 128), BF16),
             pltpu.SemaphoreType.DMA((4,)),
-            pltpu.SemaphoreType.DMA((4,)),
-            pltpu.SemaphoreType.DMA((13,)),
+            pltpu.SemaphoreType.DMA((2,)),
             pltpu.SemaphoreType.DMA((13,)),
         ],
         compiler_params=params(),
@@ -452,7 +486,7 @@
             pltpu.VMEM((288, 384), F32),
             pltpu.SemaphoreType.DMA((13,)),
         ],
-        compiler_params=params(),
+        compiler_params=params(MEDIUM),
         cost_estimate=cost(10e9, 20e6),
         name="weight_grad",
     )(x, pre, sums, stats)
@@ -524,33 +558,38 @@
     )(g, w)
 
 
-def place_kernel(part_ref, out_ref):
+def place_kernel(part_ref, out_ref, rows, sem):
+    copies = [pltpu.make_async_copy(rows.at[:, i], out_ref.at[:, i], sem.at[i]) for i in range(13)]
     for i in range(13):
         lanes = slice(128 * i, 128 * i + 128)
         slabs = [part_ref[2 * (block % 8) + block // 8, :, lanes].astype(F32) for block in range(16)]
         slabs = exchange(slabs)
         for j in range(13):
-            out_ref[0, i, j] = slabs[j][:, 0:64].astype(BF16)
-            out_ref[1, i, j] = swap_halves(slabs[j])[:, 0:64].astype(BF16)
+            rows[0, i, j] = slabs[j][:, 0:64].astype(BF16)
+            rows[1, i, j] = swap_halves(slabs[j])[:, 0:64].astype(BF16)
+        copies[i].start()
+    for copy in copies:
+        copy.wait()
 
 
 def placed_back(parts):
     return pl.pallas_call(
         place_kernel,
         in_specs=[VMEM],
-        out_specs=VMEM,
+        out_specs=ANY,
         out_shape=jax.ShapeDtypeStruct((2, 13, 13, 24, 64), BF16),
+        scratch_shapes=[pltpu.VMEM((2, 13, 13, 24, 64), BF16), pltpu.SemaphoreType.DMA((13,))],
         compiler_params=params(SMALL),
         cost_estimate=cost(1e8, 3e6),
         name="placed_back",
     )(parts)
 
 
-def fc_weight_kernel(place_ref, flat_0, flat_1, flat_2, flat_3, own_ref, other_ref, out_ref):
+def fc_weight_kernel(place_ref, flat_0, flat_1, flat_3, near_2, far_2, own_ref, other_ref, out_ref):
     core = place_ref[0]
     lead = first_half((576, 128))
     zero = jnp.zeros((576, 128), BF16)
-    flats = [ref[h] for ref in (flat_0, flat_1, flat_2, flat_3) for h in range(2)]
+    flats = [ref[h] for ref in (flat_0, flat_1, flat_3) for h in range(2)] + [near_2[...], far_2[...]]
     lefts = [
         jnp.concatenate([jnp.where(lead, flat, zero) for flat in flats], axis=1),
         jnp.concatenate([jnp.where(lead, zero, flat) for flat in flats], axis=1),
@@ -568,7 +607,7 @@
 def fc_weight_grad_of(place, flats, own, other):
     return pl.pallas_call(
         fc_weight_kernel,
-        in_specs=[SMEM] + [VMEM] * 6,
+        in_specs=[SMEM] + [VMEM] * 7,
         out_specs=VMEM,
         out_shape=jax.ShapeDtypeStruct((2, 576, 512), F32),
         compiler_params=params(SMALL),
@@ -666,17 +705,19 @@
     x_at, h_at = dp_at // 2, dp_at % 2
     core_arg = core.astype(jnp.int32).reshape(1)
 
-    pair = jnp.stack([pick(kernels, core, 0), over_mp(pick(kernels, 1 - core, 0), core_step=1)])
-    blocks = dealt(jnp.broadcast_to(pair[None], (8, 2, 144, 384)), SAME_CORE)
+    kernels_c = over_mp(kernels, core_step=1)
+    blocks = dealt(fanned(core_arg, kernels, kernels_c), SAME_CORE)
     slope, pooled, flat_t, own, other = front(
         core_arg, x, fc_weight, kernels.reshape(288, 384), conv_bias, stitch_one
     )
+    flat_z, flat_2 = over_dp(flat_t, z_step=1), over_dp(flat_t, x_step=2)
     own, blocks = lax.optimization_barrier((own, blocks))
-    own = (own.astype(F32) + over_mp(other, core_step=1).astype(F32)).astype(BF16)
+    own = pair_sum(own, over_mp(other, core_step=1))
+    own, flat_z, flat_2 = lax.optimization_barrier((own, flat_z, flat_2))
     parts = dealt(own, SAME_CORE)
 
-    flat_z = over_dp(flat_t, z_step=1)
-    parts, flat_z = lax.optimization_barrier((parts, flat_z))
+    flat_pair = jnp.stack([flat_t, flat_z])
+    flat_1, flat_3 = over_dp(flat_pair, x_step=1), over_dp(flat_pair, x_step=3)
     output, grad_copies, sums = hidden_layer(
         crop_counts,
         parts,
@@ -684,30 +725,31 @@
         jnp.transpose(second_stitch, (1, 2, 0)),
         jnp.transpose(out_grad, (1, 2, 0)),
     )
+    grad_copies, flat_1, flat_3 = lax.optimization_barrier((grad_copies, flat_1, flat_3))
     grads_own = dealt(grad_copies, SAME_CORE)
-    flat_pair = jnp.stack([flat_t, flat_z])
-    flats = [flat_pair] + [over_dp(flat_pair, x_step=k) for k in range(1, 4)]
+    flats = [flat_pair, flat_1, flat_3, flat_2, over_dp(flat_z, x_step=2)]
+    kernels_all = turned(core_arg, blocks)
+    grads_own, flats, kernels_all = lax.optimization_barrier((grads_own, flats, kernels_all))
     grads_other = over_mp(grads_own, core_step=1)
     slice_own = dealt(grads_own, axis="dp")
     send, pre, stats = back_fc(core_arg, grads_own, grads_other, fc_weight, stitch_one, pooled, slope)
-    send, slice_own, flats = lax.optimization_barrier((send, slice_own, flats))
+    send, slice_own = lax.optimization_barrier((send, slice_own))
     slice_other = over_mp(slice_own, core_step=1)
     pre_all = dealt(send)
 
     weight_part = weight_grad(x, pre, sums, stats)
-    kernels_all = turned(core_arg, blocks)
     weight_z = over_dp(weight_part, z_step=1)
     pre_all, weight_part = lax.optimization_barrier((pre_all, weight_part))
     input_part = input_grad_part(pre_all, kernels_all)
     input_part, weight_z = lax.optimization_barrier((input_part, weight_z))
-    weight_pair = (weight_part.astype(F32) + weight_z.astype(F32)).astype(BF16)
     part = dealt(input_part)
 
+    weight_pair = pair_sum(weight_part, weight_z)
     conv_sum, conv_bias_grad, first_sum, fc_bias_sum, second_sum = summed(
         [weight_pair] + [over_dp(weight_pair, x_step=k) for k in range(1, 4)]
     )
     crops_place = jnp.stack(
-        [core] + [(x_at + 4 - k) % 4 * 2 + (h_at + dh) % 2 for k in range(4) for dh in range(2)]
+        [core] + [(x_at + 4 - k) % 4 * 2 + (h_at + dh) % 2 for k in (0, 1, 3, 2) for dh in range(2)]
     ).astype(jnp.int32)
     fc_weight_grad = fc_weight_grad_of(crops_place, flats, slice_own, slice_other)
     input_grad = jnp.transpose(placed_back(part), (0, 4, 1, 2, 3))

time: 150 us -> 138 us (0.920)
  blocking collectives: 16.1 us -> 0 us
  starting transfers between devices: 40.5 us -> 44.9 us
  other arithmetic: 3.06 us -> 0.94 us
  local copies, waits for them, and re-layouts: 8.8 us -> 10.5 us
    all_to_all x1 -> x0, blocking collectives: 16.1 us -> none  [dealt(): lax.all_to_all(array, axis, 0, 0, tiled=True, axis_index_groups=groups)]
    ppermute x8 -> x9, waiting for transfers between devices: 19.1 us -> 12.7 us  [over_dp(): return lax.ppermute(array, 'dp', dp_moves(x_step, z_step))]
    all_to_all x5 -> x6, waiting for transfers between devices: 11.3 us -> 16.8 us  [dealt(): lax.all_to_all(array, axis, 0, 0, tiled=True, axis_index_groups=groups)]
    unnamed x30 -> x38, local copies, waits for them, and re-layouts: 6.38 us -> 10.4 us
    all_to_all x5 -> x6, starting transfers between devices: 23.3 us -> 26 us  [dealt(): lax.all_to_all(array, axis, 0, 0, tiled=True, axis_index_groups=groups)]
    ppermute x8 -> x9, starting transfers between devices: 12.6 us -> 15 us  [over_dp(): return lax.ppermute(array, 'dp', dp_moves(x_step, z_step))]
    pallas_call x3 -> x6, Pallas kernels: 17 us -> 19.1 us  [the longest x1 9.6 us: back_fc(): pl.pallas_call(back_kernel, in_specs=[SMEM, VMEM, VMEM, ANY, VMEM, ANY, A...]
    convert_element_type x2 -> x0, other arithmetic: 2.03 us -> none  [the longest x1 1.96 us: local(): (own.astype(F32) + over_mp(other, core_step=1).astype(F32)).astype(BF16)]
  transfers between devices with their start and end apart: 17 -> 19, of which waited for: 8 -> 10; matrix products, arithmetic and copies ran while one was open for 1% -> 1% of each run, Pallas kernels for 30% -> 33%
where the time goes in v3:
time: 138 us; the launch traced here: 137 us
  Pallas kernels  48.6 us (35%)
  starting transfers between devices  44.9 us (33%)
  waiting for transfers between devices  30.8 us (22%)
  local copies, waits for them, and re-layouts  10.5 us (8%)
    all_to_all x6, starting transfers between devices, dealt(): lax.all_to_all(array, axis, 0, 0, tiled=True, axis_index_groups=groups)  26 us
    all_to_all x6, waiting for transfers between devices, dealt(): lax.all_to_all(array, axis, 0, 0, tiled=True, axis_index_groups=groups)  16.8 us
    ppermute x9, starting transfers between devices, over_dp(): return lax.ppermute(array, 'dp', dp_moves(x_step, z_step))  15 us
    pallas_call x1, Pallas kernels, front(): pl.pallas_call(front_kernel, in_specs=[SMEM, ANY, ANY, VMEM, VMEM, VMEM],...  13.8 us
    ppermute x9, waiting for transfers between devices, over_dp(): return lax.ppermute(array, 'dp', dp_moves(x_step, z_step))  12.7 us
    unnamed x38, local copies, waits for them, and re-layouts  10.4 us
    pallas_call x1, Pallas kernels, back_fc(): pl.pallas_call(back_kernel, in_specs=[SMEM, VMEM, VMEM, ANY, VMEM, ANY, A...  9.6 us
    pallas_call x1, Pallas kernels, weight_grad(): pl.pallas_call(weight_kernel, in_specs=[ANY, VMEM, VMEM, VMEM], out_specs...  7.83 us
  transfers between devices with their start and end apart: 19, of which 10 were waited for; matrix products, arithmetic and copies ran while one was open for 1% of the time, Pallas kernels for 33%

profile of v3, /device:TPU:1, one launch (start us, length us, event | category | flops | bytes accessed | tf_op | source)
XLA Modules:
  0.0 136.7 jit_solution(1847032989810881492)
XLA Ops:
  5.9 5.6 %all-to-all-start = ((bf16[8,2,144,384]{3,2,1,0:T(8,128)(2,1)}), bf16[8,2,144,384]{3,2,1,0:T(8,128)(2,1)S(1)}, u32[]{:S(2)}, u32[]{:S(2)}) async-start(bf16[8,2,144,384]{3,2,1,0:T(8,128)(2,1)} %fanned.1), calls=%async_computation | async-start | bytes 3538944 | tf_op jit(solution)/shard_map/all_to_all | solution.py:682
  11.6 13.8 %front.1 = (bf16[13,13,16,128]{3,2,1,0:T(8,128)(2,1)}, f32[36,16,128]{2,1,0:T(8,128)}, bf16[576,128]{1,0:T(8,128)(2,1)}, bf16[8,128,256]{2,1,0:T(8,128)(2,1)}, bf16[8,128,256]{2,1,0:T(8,128)(2,1)}) custom-call(s32[1]{0:T(128)} %bitcast.core_ref, bf16[2,13,13,64,384]{4,3,2,1,0:T(8,128)(2,1)} %bitcast.40, bf16[2,576,4096]{2,1,0:T(8,128)(2,1)} %w_ref.3, ...), custom_call_target="tpu_custom_call" | custom-call | flops 10000000000 | bytes 30000000 | tf_op jit(solution)/shard_map/front/pallas_call | solution.py:197
  26.2 2.8 %collective-permute-start.3 = (bf16[576,128]{1,0:T(8,128)(2,1)}, bf16[576,128]{1,0:T(8,128)(2,1)S(1)}, u32[]{:S(2)}, u32[]{:S(2)}) collective-permute-start(bf16[576,128]{1,0:T(8,128)(2,1)} %get-tuple-element.48), channel_id=1, source_target_pairs={{0,4},{1,5},{2,6},{3,7},{4,0},{5,1},{6,2},{7,3},{8,12},{9,13},{10,... | collective-permute-start | bytes 442376 | tf_op jit(solution)/shard_map/ppermute | solution.py:678
  28.9 3.3 %collective-permute-start.2 = (bf16[576,128]{1,0:T(8,128)(2,1)}, bf16[576,128]{1,0:T(8,128)(2,1)S(1)}, u32[]{:S(2)}, u32[]{:S(2)}) collective-permute-start(bf16[576,128]{1,0:T(8,128)(2,1)} %get-tuple-element.48), channel_id=1, source_target_pairs={{0,1},{1,0},{2,3},{3,2},{4,5},{5,4},{6,7},{7,6},{8,9},{9,8},{10,11... | collective-permute-start | bytes 442376 | tf_op jit(solution)/shard_map/ppermute | solution.py:678
  32.2 2.9 %all-to-all-done.blocks_ref = bf16[8,2,144,384]{3,2,1,0:T(8,128)(2,1)S(1)} async-done(((bf16[8,2,144,384]{3,2,1,0:T(8,128)(2,1)}), bf16[8,2,144,384]{3,2,1,0:T(8,128)(2,1)S(1)}, u32[]{:S(2)}, u32[]{:S(2)}) %all-to-all-start) | async-done | bytes 1769504 | tf_op jit(solution)/shard_map/all_to_all | solution.py:682
  37.1 3.7 %collective-permute-done.2 = bf16[576,128]{1,0:T(8,128)(2,1)S(1)} collective-permute-done((bf16[576,128]{1,0:T(8,128)(2,1)}, bf16[576,128]{1,0:T(8,128)(2,1)S(1)}, u32[]{:S(2)}, u32[]{:S(2)}) %collective-permute-start.2) | collective-permute-done | bytes 147488 | tf_op jit(solution)/shard_map/ppermute | solution.py:678
  41.4 3.5 %all-to-all-start.1 = ((bf16[8,128,256]{2,1,0:T(8,128)(2,1)}), bf16[8,128,256]{2,1,0:T(8,128)(2,1)S(1)}, u32[]{:S(2)}, u32[]{:S(2)}) async-start(bf16[8,128,256]{2,1,0:T(8,128)(2,1)} %pair_sum.2), calls=%async_computation.1 | async-start | bytes 1048576 | tf_op jit(solution)/shard_map/all_to_all | solution.py:682
  47.4 7.7 %all-to-all-done.1.parts_ref = bf16[8,128,256]{2,1,0:T(8,128)(2,1)S(1)} async-done(((bf16[8,128,256]{2,1,0:T(8,128)(2,1)}), bf16[8,128,256]{2,1,0:T(8,128)(2,1)S(1)}, u32[]{:S(2)}, u32[]{:S(2)}) %all-to-all-start.1) | async-done | bytes 524320 | tf_op jit(solution)/shard_map/all_to_all | solution.py:682
  55.2 1.6 %hidden_layer.1 = (bf16[2,64,256]{2,1,0:T(8,128)(2,1)}, bf16[8,256,128]{2,1,0:T(8,128)(2,1)}, f32[8,256]{1,0:T(8,128)S(1)}) custom-call(s32[8]{0:T(128)S(1)} %copy-done.5, bf16[8,128,256]{2,1,0:T(8,128)(2,1)S(1)} %all-to-all-done.1.parts_ref, f32[2,256]{1,0:T(2,128)S(1)} %bitcast.34, f32[2,2,256]{2,1,0:T(2,128)S(1)} %bitcast.33, bf16[2,64,256]{2,1,0:T(8,128)(2,1)S(1)} %bitcast.32), custom_call_target="tpu_custom_call" | custom-call | flops 10000000 | bytes 3000000 | tf_op jit(solution)/shard_map/hidden_layer/pallas_call | solution.py:309
  57.4 4.1 %all-to-all-start.2 = ((bf16[8,256,128]{2,1,0:T(8,128)(2,1)}), bf16[8,256,128]{2,1,0:T(8,128)(2,1)}, u32[]{:S(2)}, u32[]{:S(2)}) async-start(bf16[8,256,128]{2,1,0:T(8,128)(2,1)} %get-tuple-element.53), calls=%async_computation.2 | async-start | bytes 1048576 | tf_op jit(solution)/shard_map/all_to_all | solution.py:682
  64.8 2.5 %collective-permute-done.6.far_2 = bf16[576,128]{1,0:T(8,128)(2,1)S(1)} collective-permute-done((bf16[576,128]{1,0:T(8,128)(2,1)}, bf16[576,128]{1,0:T(8,128)(2,1)S(1)}, u32[]{:S(2)}, u32[]{:S(2)}) %collective-permute-start.6) | collective-permute-done | bytes 147488 | tf_op jit(solution)/shard_map/ppermute | solution.py:678
  67.3 3.8 %all-to-all-done.2.own_ref = bf16[8,256,128]{2,1,0:T(8,128)(2,1)} async-done(((bf16[8,256,128]{2,1,0:T(8,128)(2,1)}), bf16[8,256,128]{2,1,0:T(8,128)(2,1)}, u32[]{:S(2)}, u32[]{:S(2)}) %all-to-all-start.2) | async-done | bytes 524320 | tf_op jit(solution)/shard_map/all_to_all | solution.py:682
  72.6 3.5 %all-to-all-start.3 = ((bf16[8,256,128]{2,1,0:T(8,128)(2,1)}), bf16[8,256,128]{2,1,0:T(8,128)(2,1)S(1)}, u32[]{:S(2)}, u32[]{:S(2)}) async-start(bf16[8,256,128]{2,1,0:T(8,128)(2,1)} %all-to-all-done.2.own_ref), calls=%async_computation.3 | async-start | bytes 1048576 | tf_op jit(solution)/shard_map/all_to_all | solution.py:682
  76.9 9.6 %back_fc.1 = (bf16[16,16,1664]{2,1,0:T(8,128)(2,1)}, bf16[13,13,16,128]{3,2,1,0:T(8,128)(2,1)}, f32[16,128]{1,0:T(8,128)}) custom-call(s32[1]{0:T(128)} %bitcast.core_ref, bf16[8,256,128]{2,1,0:T(8,128)(2,1)} %all-to-all-done.2.own_ref, bf16[8,256,128]{2,1,0:T(8,128)(2,1)} %copy-done.16, bf16[2,576,4096]{2,1,0:T(8,128)(2,1)} %w_ref.3, f32[2,2,16]{2,1,0:T(2,128)} %bitcast.39, ...), custom_call_target="tpu_custom_call" | custom-call | flops 100000000 | bytes 1000000 | tf_op jit(solution)/shard_map/back_fc/pallas_call | solution.py:408
  86.5 4.4 %all-to-all-start.4 = ((bf16[16,16,1664]{2,1,0:T(8,128)(2,1)}), bf16[16,16,1664]{2,1,0:T(8,128)(2,1)S(1)}, u32[]{:S(2)}, u32[]{:S(2)}) async-start(bf16[16,16,1664]{2,1,0:T(8,128)(2,1)} %get-tuple-element.62), calls=%async_computation.4 | async-start | bytes 1703936 | tf_op jit(solution)/shard_map/all_to_all | solution.py:682
  92.7 7.8 %weight_grad.1.first_ref = bf16[304,384]{1,0:T(8,128)(2,1)S(1)} custom-call(bf16[2,13,13,64,384]{4,3,2,1,0:T(8,128)(2,1)} %bitcast.41, bf16[13,13,16,128]{3,2,1,0:T(8,128)(2,1)S(1)} %copy-done.6, f32[8,256]{1,0:T(8,128)S(1)} %copy-done.12, f32[16,128]{1,0:T(8,128)S(1)} %copy-done.13), custom_call_target="tpu_custom_call" | custom-call | flops 10000000000 | bytes 20000000 | tf_op jit(solution)/shard_map/weight_grad/pallas_call | solution.py:478
  100.6 2.7 %collective-permute-start.8 = (bf16[304,384]{1,0:T(8,128)(2,1)S(1)}, bf16[304,384]{1,0:T(8,128)(2,1)S(1)}, u32[]{:S(2)}, u32[]{:S(2)}) collective-permute-start(bf16[304,384]{1,0:T(8,128)(2,1)S(1)} %weight_grad.1.first_ref), channel_id=1, source_target_pairs={{0,1},{1,0},{2,3},{3,2},{4,5},{5,4},{6,7},{7,6},{8,9},{9,8},{10,11... | collective-permute-start | bytes 700424 | tf_op jit(solution)/shard_map/ppermute | solution.py:678
  103.2 1.5 %all-to-all-done.4.g_ref = bf16[16,16,1664]{2,1,0:T(8,128)(2,1)S(1)} async-done(((bf16[16,16,1664]{2,1,0:T(8,128)(2,1)}), bf16[16,16,1664]{2,1,0:T(8,128)(2,1)S(1)}, u32[]{:S(2)}, u32[]{:S(2)}) %all-to-all-start.4) | async-done | bytes 852000 | tf_op jit(solution)/shard_map/all_to_all | solution.py:682
  106.3 4.6 %input_grad.1 = bf16[16,24,1664]{2,1,0:T(8,128)(2,1)} custom-call(bf16[16,16,1664]{2,1,0:T(8,128)(2,1)S(1)} %all-to-all-done.4.g_ref, bf16[384,2304]{1,0:T(8,128)(2,1)S(1)} %copy-done.15), custom_call_target="tpu_custom_call" | custom-call | flops 4000000000 | bytes 4000000 | tf_op jit(solution)/shard_map/input_grad/pallas_call | solution.py:549
  110.9 4.8 %all-to-all-start.5 = ((bf16[16,24,1664]{2,1,0:T(8,128)(2,1)}), bf16[16,24,1664]{2,1,0:T(8,128)(2,1)S(1)}, u32[]{:S(2)}, u32[]{:S(2)}) async-start(bf16[16,24,1664]{2,1,0:T(8,128)(2,1)} %input_grad.1), calls=%async_computation.5 | async-start | bytes 2555904 | tf_op jit(solution)/shard_map/all_to_all | solution.py:682
  116.0 2.1 %collective-permute-start.11 = (bf16[304,384]{1,0:T(8,128)(2,1)S(1)}, bf16[304,384]{1,0:T(8,128)(2,1)S(1)}, u32[]{:S(2)}, u32[]{:S(2)}) collective-permute-start(bf16[304,384]{1,0:T(8,128)(2,1)S(1)} %pair_sum.3.part_0), channel_id=1, source_target_pairs={{0,6},{1,7},{2,0},{3,1},{4,2},{5,3},{6,4},{7,5},{8,14},{9,15},{10,... | collective-permute-start | bytes 700424 | tf_op jit(solution)/shard_map/ppermute | solution.py:678
  121.2 4.5 %fc_weight_grad.1 = f32[2,576,512]{2,1,0:T(8,128)} custom-call(s32[9]{0:T(128)S(1)} %stack.48.place_ref, bf16[2,576,128]{2,1,0:T(8,128)(2,1)S(1)} %pad_maximum_fusion.flat_0, bf16[2,576,128]{2,1,0:T(8,128)(2,1)S(1)} %copy-done.8, bf16[2,576,128]{2,1,0:T(8,128)(2,1)S(1)} %collective-permute-done.5.flat_3, bf16[576,128]{1,0:T(8,128)(2,1)S(1)} %collective-permute-done.3.near_2, ...), custom_call_target="tpu_custom_call" | custom-call | flops 3000000000 | bytes 5000000 | tf_op jit(solution)/shard_map/fc_weight_grad/pallas_call | solution.py:608
  126.3 5.9 %collective-permute-done.9.part_1 = bf16[304,384]{1,0:T(8,128)(2,1)S(1)} collective-permute-done((bf16[304,384]{1,0:T(8,128)(2,1)S(1)}, bf16[304,384]{1,0:T(8,128)(2,1)S(1)}, u32[]{:S(2)}, u32[]{:S(2)}) %collective-permute-start.9) | collective-permute-done | bytes 233504 | tf_op jit(solution)/shard_map/ppermute | solution.py:678
  134.0 2.5 %placed_back.1 = bf16[2,13,13,24,64]{4,3,2,1,0:T(8,128)(2,1)} custom-call(bf16[16,24,1664]{2,1,0:T(8,128)(2,1)S(1)} %all-to-all-done.5.part_ref), custom_call_target="tpu_custom_call" | custom-call | flops 100000000 | bytes 3000000 | tf_op jit(solution)/shard_map/placed_back/pallas_call | solution.py:576
  (66 shorter events, 26.3 us)
Async XLA Ops:
  0.6 2.8 %collective-permute-start = (bf16[2,144,384]{2,1,0:T(8,128)(2,1)}, bf16[2,144,384]{2,1,0:T(8,128)(2,1)S(1)}, u32[]{:S(2)}, u32[]{:S(2)}) collective-permute-start(bf16[2,144,384]{2,1,0:T(8,128)(2,1)} %bitcast.29), channel_id=1, source_target_pairs={{0,8},{8,0},{16,24},{24,16},{32,40},{40,32},{48,56},{56,48},{64,72... | collective-permute-start | bytes 663560 | tf_op jit(solution)/shard_map/ppermute | solution.py:674
  5.9 29.2 %all-to-all-start = ((bf16[8,2,144,384]{3,2,1,0:T(8,128)(2,1)}), bf16[8,2,144,384]{3,2,1,0:T(8,128)(2,1)S(1)}, u32[]{:S(2)}, u32[]{:S(2)}) async-start(bf16[8,2,144,384]{3,2,1,0:T(8,128)(2,1)} %fanned.1), calls=%async_computation | async-start | bytes 3538944 | tf_op jit(solution)/shard_map/all_to_all | solution.py:682
  11.6 43.6 %copy-start.2 = (bf16[256,2,64]{0,2,1:T(8,128)(2,1)S(1)}, bf16[256,2,64]{0,2,1:T(8,128)(2,1)}, u32[]{:S(2)}) copy-start(bf16[256,2,64]{0,2,1:T(8,128)(2,1)} %param.17) | copy-start | bytes 196612
  11.6 43.6 %copy-start.4 = (f32[256,2]{0,1:T(2,128)S(1)}, f32[256,2]{0,1:T(2,128)}, u32[]{:S(2)}) copy-start(f32[256,2]{0,1:T(2,128)} %param.14) | copy-start | bytes 6148
  25.4 29.8 %copy-start.3 = (f32[256,2,2]{0,2,1:T(2,128)S(1)}, f32[256,2,2]{0,2,1:T(2,128)}, u32[]{:S(2)}) copy-start(f32[256,2,2]{0,2,1:T(2,128)} %param.15) | copy-start | bytes 12292
  25.4 29.7 %copy-start.5 = (s32[8]{0:T(128)S(1)}, s32[8]{0:T(128)}, u32[]{:S(2)}) copy-start(s32[8]{0:T(128)} %counts_ref.1) | copy-start | bytes 100
  25.4 9.7 %collective-permute-start.1 = (bf16[8,128,256]{2,1,0:T(8,128)(2,1)}, bf16[8,128,256]{2,1,0:T(8,128)(2,1)S(1)}, u32[]{:S(2)}, u32[]{:S(2)}) collective-permute-start(bf16[8,128,256]{2,1,0:T(8,128)(2,1)} %get-tuple-element.47), channel_id=1, source_target_pairs={{0,8},{8,0},{16,24},{24,16},{32,40},{40,32},{48,56},{56,48},{64,72... | collective-permute-start | bytes 1572872 | tf_op jit(solution)/shard_map/ppermute | solution.py:674
  26.2 11.0 %collective-permute-start.3 = (bf16[576,128]{1,0:T(8,128)(2,1)}, bf16[576,128]{1,0:T(8,128)(2,1)S(1)}, u32[]{:S(2)}, u32[]{:S(2)}) collective-permute-start(bf16[576,128]{1,0:T(8,128)(2,1)} %get-tuple-element.48), channel_id=1, source_target_pairs={{0,4},{1,5},{2,6},{3,7},{4,0},{5,1},{6,2},{7,3},{8,12},{9,13},{10,... | collective-permute-start | bytes 442376 | tf_op jit(solution)/shard_map/ppermute | solution.py:678
  28.9 11.8 %collective-permute-start.2 = (bf16[576,128]{1,0:T(8,128)(2,1)}, bf16[576,128]{1,0:T(8,128)(2,1)S(1)}, u32[]{:S(2)}, u32[]{:S(2)}) collective-permute-start(bf16[576,128]{1,0:T(8,128)(2,1)} %get-tuple-element.48), channel_id=1, source_target_pairs={{0,1},{1,0},{2,3},{3,2},{4,5},{5,4},{6,7},{7,6},{8,9},{9,8},{10,11... | collective-permute-start | bytes 442376 | tf_op jit(solution)/shard_map/ppermute | solution.py:678
  41.4 13.7 %all-to-all-start.1 = ((bf16[8,128,256]{2,1,0:T(8,128)(2,1)}), bf16[8,128,256]{2,1,0:T(8,128)(2,1)S(1)}, u32[]{:S(2)}, u32[]{:S(2)}) async-start(bf16[8,128,256]{2,1,0:T(8,128)(2,1)} %pair_sum.2), calls=%async_computation.1 | async-start | bytes 1048576 | tf_op jit(solution)/shard_map/all_to_all | solution.py:682
  45.9 10.9 %collective-permute-start.5 = (bf16[2,576,128]{2,1,0:T(8,128)(2,1)S(1)}, bf16[2,576,128]{2,1,0:T(8,128)(2,1)S(1)}, u32[]{:S(2)}, u32[]{:S(2)}) collective-permute-start(bf16[2,576,128]{2,1,0:T(8,128)(2,1)S(1)} %pad_maximum_fusion.flat_0), channel_id=1, source_target_pairs={{0,6},{1,7},{2,0},{3,1},{4,2},{5,3},{6,4},{7,5},{8,14},{9,15},{10,... | collective-permute-start | bytes 884744 | tf_op jit(solution)/shard_map/ppermute | solution.py:678
  47.2 9.5 %collective-permute-start.4 = (bf16[2,576,128]{2,1,0:T(8,128)(2,1)S(1)}, bf16[2,576,128]{2,1,0:T(8,128)(2,1)S(1)}, u32[]{:S(2)}, u32[]{:S(2)}) collective-permute-start(bf16[2,576,128]{2,1,0:T(8,128)(2,1)S(1)} %pad_maximum_fusion.flat_0), channel_id=1, source_target_pairs={{0,2},{1,3},{2,4},{3,5},{4,6},{5,7},{6,0},{7,1},{8,10},{9,11},{10,... | collective-permute-start | bytes 884744 | tf_op jit(solution)/shard_map/ppermute | solution.py:678
  57.4 13.7 %all-to-all-start.2 = ((bf16[8,256,128]{2,1,0:T(8,128)(2,1)}), bf16[8,256,128]{2,1,0:T(8,128)(2,1)}, u32[]{:S(2)}, u32[]{:S(2)}) async-start(bf16[8,256,128]{2,1,0:T(8,128)(2,1)} %get-tuple-element.53), calls=%async_computation.2 | async-start | bytes 1048576 | tf_op jit(solution)/shard_map/all_to_all | solution.py:682
  61.5 5.8 %collective-permute-start.6 = (bf16[576,128]{1,0:T(8,128)(2,1)}, bf16[576,128]{1,0:T(8,128)(2,1)S(1)}, u32[]{:S(2)}, u32[]{:S(2)}) collective-permute-start(bf16[576,128]{1,0:T(8,128)(2,1)} %copy-done.17), channel_id=1, source_target_pairs={{0,4},{1,5},{2,6},{3,7},{4,0},{5,1},{6,2},{7,3},{8,12},{9,13},{10,... | collective-permute-start | bytes 442376 | tf_op jit(solution)/shard_map/ppermute | solution.py:678
  67.3 19.2 %copy-start.9 = (bf16[576,128]{1,0:T(8,128)(2,1)}, bf16[576,128]{1,0:T(8,128)(2,1)S(1)}, u32[]{:S(2)}) copy-start(bf16[576,128]{1,0:T(8,128)(2,1)S(1)} %collective-permute-done.6.far_2) | copy-start | bytes 442372
  71.1 5.0 %collective-permute-start.7 = (bf16[8,256,128]{2,1,0:T(8,128)(2,1)}, bf16[8,256,128]{2,1,0:T(8,128)(2,1)S(1)}, u32[]{:S(2)}, u32[]{:S(2)}) collective-permute-start(bf16[8,256,128]{2,1,0:T(8,128)(2,1)} %all-to-all-done.2.own_ref), channel_id=1, source_target_pairs={{0,8},{8,0},{16,24},{24,16},{32,40},{40,32},{48,56},{56,48},{64,72... | collective-permute-start | bytes 1572872 | tf_op jit(solution)/shard_map/ppermute | solution.py:674
  72.6 13.9 %all-to-all-start.3 = ((bf16[8,256,128]{2,1,0:T(8,128)(2,1)}), bf16[8,256,128]{2,1,0:T(8,128)(2,1)S(1)}, u32[]{:S(2)}, u32[]{:S(2)}) async-start(bf16[8,256,128]{2,1,0:T(8,128)(2,1)} %all-to-all-done.2.own_ref), calls=%async_computation.3 | async-start | bytes 1048576 | tf_op jit(solution)/shard_map/all_to_all | solution.py:682
  86.5 18.3 %all-to-all-start.4 = ((bf16[16,16,1664]{2,1,0:T(8,128)(2,1)}), bf16[16,16,1664]{2,1,0:T(8,128)(2,1)S(1)}, u32[]{:S(2)}, u32[]{:S(2)}) async-start(bf16[16,16,1664]{2,1,0:T(8,128)(2,1)} %get-tuple-element.62), calls=%async_computation.4 | async-start | bytes 1703936 | tf_op jit(solution)/shard_map/all_to_all | solution.py:682
  100.6 10.3 %collective-permute-start.8 = (bf16[304,384]{1,0:T(8,128)(2,1)S(1)}, bf16[304,384]{1,0:T(8,128)(2,1)S(1)}, u32[]{:S(2)}, u32[]{:S(2)}) collective-permute-start(bf16[304,384]{1,0:T(8,128)(2,1)S(1)} %weight_grad.1.first_ref), channel_id=1, source_target_pairs={{0,1},{1,0},{2,3},{3,2},{4,5},{5,4},{6,7},{7,6},{8,9},{9,8},{10,11... | collective-permute-start | bytes 700424 | tf_op jit(solution)/shard_map/ppermute | solution.py:678
  110.9 23.1 %all-to-all-start.5 = ((bf16[16,24,1664]{2,1,0:T(8,128)(2,1)}), bf16[16,24,1664]{2,1,0:T(8,128)(2,1)S(1)}, u32[]{:S(2)}, u32[]{:S(2)}) async-start(bf16[16,24,1664]{2,1,0:T(8,128)(2,1)} %input_grad.1), calls=%async_computation.5 | async-start | bytes 2555904 | tf_op jit(solution)/shard_map/all_to_all | solution.py:682
  115.7 3.6 %collective-permute-start.12 = (bf16[8,256,128]{2,1,0:T(8,128)(2,1)S(1)}, bf16[8,256,128]{2,1,0:T(8,128)(2,1)S(1)}, u32[]{:S(2)}, u32[]{:S(2)}) collective-permute-start(bf16[8,256,128]{2,1,0:T(8,128)(2,1)S(1)} %all-to-all-done.3.own_ref), channel_id=1, source_target_pairs={{0,8},{8,0},{16,24},{24,16},{32,40},{40,32},{48,56},{56,48},{64,72... | collective-permute-start | bytes 1572872 | tf_op jit(solution)/shard_map/ppermute | solution.py:674
  116.0 9.7 %collective-permute-start.11 = (bf16[304,384]{1,0:T(8,128)(2,1)S(1)}, bf16[304,384]{1,0:T(8,128)(2,1)S(1)}, u32[]{:S(2)}, u32[]{:S(2)}) collective-permute-start(bf16[304,384]{1,0:T(8,128)(2,1)S(1)} %pair_sum.3.part_0), channel_id=1, source_target_pairs={{0,6},{1,7},{2,0},{3,1},{4,2},{5,3},{6,4},{7,5},{8,14},{9,15},{10,... | collective-permute-start | bytes 700424 | tf_op jit(solution)/shard_map/ppermute | solution.py:678
  118.2 8.2 %collective-permute-start.10 = (bf16[304,384]{1,0:T(8,128)(2,1)S(1)}, bf16[304,384]{1,0:T(8,128)(2,1)S(1)}, u32[]{:S(2)}, u32[]{:S(2)}) collective-permute-start(bf16[304,384]{1,0:T(8,128)(2,1)S(1)} %pair_sum.3.part_0), channel_id=1, source_target_pairs={{0,4},{1,5},{2,6},{3,7},{4,0},{5,1},{6,2},{7,3},{8,12},{9,13},{10,... | collective-permute-start | bytes 700424 | tf_op jit(solution)/shard_map/ppermute | solution.py:678
  118.7 13.5 %collective-permute-start.9 = (bf16[304,384]{1,0:T(8,128)(2,1)S(1)}, bf16[304,384]{1,0:T(8,128)(2,1)S(1)}, u32[]{:S(2)}, u32[]{:S(2)}) collective-permute-start(bf16[304,384]{1,0:T(8,128)(2,1)S(1)} %pair_sum.3.part_0), channel_id=1, source_target_pairs={{0,2},{1,3},{2,4},{3,5},{4,6},{5,7},{6,0},{7,1},{8,10},{9,11},{10,... | collective-permute-start | bytes 700424 | tf_op jit(solution)/shard_map/ppermute | solution.py:678
  (14 other events, 40.0 us)

commit v4 on v3

--- a/solution.py
+++ b/solution.py
@@ -86,7 +86,7 @@
 def front_kernel(
     core_ref, x_ref, w_ref, kernel_ref, bias_ref, stitch_ref,
     slope_ref, pooled_ref, flat_t_ref, own_ref, other_ref,
-    xs, ws, acc, ready, pool, slopes, pooled_out, flat_t_out, parts, x_sem, w_sem, slope_sem, out_sem,
+    xs, ws, acc, ready, pool, slopes, pooled_out, flat_t_out, x_sem, w_sem, slope_sem, out_sem,
 ):
     def x_copy(i):
         return pltpu.make_async_copy(x_ref.at[:, i], xs.at[:, i], x_sem.at[i])
@@ -172,16 +172,11 @@
     copies_out = [pooled_copy, flat_copy]
     for t in range(2):
         w_copy(t).wait()
-    for k, (ref, parity) in enumerate(((other_ref, 1 - core), (own_ref, core))):
+    for ref, parity in ((other_ref, 1 - core), (own_ref, core)):
         for q in range(8):
             at = pl.ds(pl.multiple_of((2 * q + parity) * 256, 256), 256)
             for t in range(2):
-                parts[k, q, 64 * t : 64 * t + 64] = nn_dot(flat[64 * t : 64 * t + 64], ws[t, :, at]).astype(BF16)
-            if q % 4 == 3:
-                some = pl.ds(q - 3, 4)
-                copy = pltpu.make_async_copy(parts.at[k, some], ref.at[some], out_sem.at[2 + 2 * k + q // 4])
-                copy.start()
-                copies_out.append(copy)
+                ref[q, 64 * t : 64 * t + 64] = nn_dot(flat[64 * t : 64 * t + 64], ws[t, :, at]).astype(BF16)
     for i in range(13):
         slope_copy(i).wait()
     for copy in copies_out:
@@ -197,7 +192,7 @@
     return pl.pallas_call(
         front_kernel,
         in_specs=[SMEM, ANY, ANY, VMEM, VMEM, VMEM],
-        out_specs=[ANY] * 5,
+        out_specs=[ANY, ANY, ANY, VMEM, VMEM],
         out_shape=[
             jax.ShapeDtypeStruct((13, 13, 16, 128), BF16),
             jax.ShapeDtypeStruct((36, 16, 128), F32),
@@ -214,11 +209,10 @@
             pltpu.VMEM((13, 13, 16, 128), BF16),
             pltpu.VMEM((36, 16, 128), F32),
             pltpu.VMEM((576, 128), BF16),
-            pltpu.VMEM((2, 8, 128, 256), BF16),
             pltpu.SemaphoreType.DMA((13,)),
             pltpu.SemaphoreType.DMA((2,)),
             pltpu.SemaphoreType.DMA((13,)),
-            pltpu.SemaphoreType.DMA((6,)),
+            pltpu.SemaphoreType.DMA((2,)),
         ],
         compiler_params=params(),
         cost_estimate=cost(10e9, 30e6),
@@ -240,36 +234,6 @@
         cost_estimate=cost(1e6, 2e6),
         name="pair_sum",
     )(first, second)
-
-
-def fan_kernel(core_ref, near_ref, far_ref, out_ref, held, in_sem, out_sem):
-    core = core_ref[0]
-    for p, ref in enumerate((near_ref, far_ref)):
-        pltpu.make_async_copy(ref.at[core], held.at[p], in_sem.at[p]).start()
-    for p, ref in enumerate((near_ref, far_ref)):
-        pltpu.make_async_copy(ref.at[core], held.at[p], in_sem.at[p]).wait()
-    copies = [pltpu.make_async_copy(held, out_ref.at[k], out_sem.at[k]) for k in range(8)]
-    for copy in copies:
-        copy.start()
-    for copy in copies:
-        copy.wait()
-
-
-def fanned(core, near, far):
-    return pl.pallas_call(
-        fan_kernel,
-        in_specs=[SMEM, ANY, ANY],
-        out_specs=ANY,
-        out_shape=jax.ShapeDtypeStruct((8, 2, 144, 384), BF16),
-        scratch_shapes=[
-            pltpu.VMEM((2, 144, 384), BF16),
-            pltpu.SemaphoreType.DMA((2,)),
-            pltpu.SemaphoreType.DMA((8,)),
-        ],
-        compiler_params=params(SMALL),
-        cost_estimate=cost(1e6, 4e6),
-        name="fanned",
-    )(core, near, far)
 
 
 def hidden_kernel(counts_ref, parts_ref, bias_ref, stitch_ref, cot_ref, out_ref, grad_ref, sums_ref):
@@ -352,9 +316,7 @@
         for t in range(2):
             totals[t] = totals[t] + nt_dot(ws[t, :, 1024 * k : 1024 * k + 1024], rows)
     flat_grad = jnp.where(first_half((576, 128)), totals[0], totals[1])
-    high = flat_grad.astype(BF16)
-    low = (flat_grad - high.astype(F32)).astype(BF16)
-    mixed_grad = (nn_dot(perm, high) + nn_dot(perm, low)).reshape(36, 16, 128)
+    mixed_grad = nn_dot(perm, flat_grad.astype(BF16)).reshape(36, 16, 128)
     swapped = swap_halves(mixed_grad)
     pooled_grad = own_slab[None] * mixed_grad + back_slab[None] * swapped
     pooled_grad = (pooled_grad * (1.0 / 9.0)).reshape(6, 6, 16, 128)
@@ -424,7 +386,7 @@
             pltpu.SemaphoreType.DMA((13,)),
         ],
         compiler_params=params(),
-        cost_estimate=cost(1e8, 1e6),
+        cost_estimate=cost(1e9, 30e6),
         name="back_fc",
     )(core, own, other, w, stitch, pooled, slope)
 
@@ -492,43 +454,48 @@
     )(x, pre, sums, stats)
 
 
-def turn_kernel(core_ref, blocks_ref, out_ref, rows):
-    core = core_ref[0]
-    for k in range(8):
-        for p, parity in ((0, core), (1, 1 - core)):
-            at = pl.ds(pl.multiple_of(16 * (2 * k + parity), 16), 16)
-            for tap in range(9):
-                rows[tap, at] = blocks_ref[k, p, 16 * tap : 16 * tap + 16]
+def turn_kernel(place_ref, same, same_a, same_b, other, other_a, other_b, out_ref, rows):
+    core, z = place_ref[0], place_ref[1]
+    for parity, refs in ((core, (same, same_a, same_b)), (1 - core, (other, other_a, other_b))):
+        for ref, near, first in zip(refs, (True, False, False), (0, 0, 2)):
+            for k in range(ref.shape[0]):
+                block = 8 * (z if near else 1 - z) + 2 * (first + k) + parity
+                at = pl.ds(pl.multiple_of(16 * block, 16), 16)
+                for tap in range(9):
+                    rows[tap, at] = ref[k, core, 16 * tap : 16 * tap + 16]
     for tap in range(9):
         out_ref[:, 256 * tap : 256 * tap + 256] = rows[tap].T
 
 
-def turned(core, blocks):
+def turned(place, parts):
     return pl.pallas_call(
         turn_kernel,
-        in_specs=[SMEM, VMEM],
+        in_specs=[SMEM] + [VMEM] * 6,
         out_specs=VMEM,
         out_shape=jax.ShapeDtypeStruct((384, 2304), BF16),
         scratch_shapes=[pltpu.VMEM((9, 256, 384), BF16)],
         compiler_params=params(SMALL),
         cost_estimate=cost(1e9, 4e6),
         name="turned_kernels",
-    )(core, blocks)
+    )(place, *parts)
 
 
 def input_kernel(g_ref, w_ref, out_ref, taps):
-    g = g_ref[...].reshape(256, 1664).astype(F32)
     zero = jnp.zeros((256, 128), BF16)
     for b in range(3):
         taps[b, :, 0:128] = zero
         taps[b, :, 1792:1920] = zero
-        for i in range(13):
-            row = g[:, 128 * i : 128 * i + 128]
-            if b == 0:
-                row = pltpu.roll(row, 120, 1)
-            if b == 2:
-                row = pltpu.roll(row, 8, 1)
-            taps[b, :, 128 * i + 128 : 128 * i + 256] = row.astype(BF16)
+
+    def widen(i):
+        row = g_ref[:, :, 128 * i : 128 * i + 128].reshape(256, 128)
+        at = slice(128 * i + 128, 128 * i + 256)
+        taps[1, :, at] = row
+        row = row.astype(F32)
+        taps[0, :, at] = pltpu.roll(row, 120, 1).astype(BF16)
+        taps[2, :, at] = pltpu.roll(row, 8, 1).astype(BF16)
+
+    for i in range(3):
+        widen(i)
     weights = w_ref[...]
     for start in range(0, 13, 2):
         width = 128 * min(2, 13 - start)
@@ -540,6 +507,8 @@
             ],
             axis=0,
         )
+        for i in range(start + 3, min(start + 5, 13)):
+            widen(i)
         product = nn_dot(weights, right)
         for m in range(16):
             out_ref[m, :, 128 * start : 128 * start + width] = product[24 * m : 24 * m + 24].astype(BF16)
@@ -585,11 +554,11 @@
     )(parts)
 
 
-def fc_weight_kernel(place_ref, flat_0, flat_1, flat_3, near_2, far_2, own_ref, other_ref, out_ref):
+def fc_weight_kernel(place_ref, flat_0, flat_1, flat_3, flat_2, own_ref, other_ref, out_ref):
     core = place_ref[0]
     lead = first_half((576, 128))
     zero = jnp.zeros((576, 128), BF16)
-    flats = [ref[h] for ref in (flat_0, flat_1, flat_3) for h in range(2)] + [near_2[...], far_2[...]]
+    flats = [ref[h] for ref in (flat_0, flat_1, flat_3, flat_2) for h in range(2)]
     lefts = [
         jnp.concatenate([jnp.where(lead, flat, zero) for flat in flats], axis=1),
         jnp.concatenate([jnp.where(lead, zero, flat) for flat in flats], axis=1),
@@ -607,7 +576,7 @@
 def fc_weight_grad_of(place, flats, own, other):
     return pl.pallas_call(
         fc_weight_kernel,
-        in_specs=[SMEM] + [VMEM] * 7,
+        in_specs=[SMEM] + [VMEM] * 6,
         out_specs=VMEM,
         out_shape=jax.ShapeDtypeStruct((2, 576, 512), F32),
         compiler_params=params(SMALL),
@@ -668,6 +637,7 @@
 
 
 SAME_CORE = [[2 * k + c for k in range(8)] for c in range(2)]
+SAME_Z_CORE = [[8 * z + 2 * y + c for y in range(4)] for z in range(2) for c in range(2)]
 
 
 def over_mp(array, z_step=0, y_step=0, core_step=0):
@@ -676,6 +646,18 @@
 
 def over_dp(array, x_step=0, z_step=0):
     return lax.ppermute(array, "dp", dp_moves(x_step, z_step))
+
+
+def over_far_z(array):
+    moves = [
+        (((z * 4 + y) * 2 + c) * 8 + x * 2 + h, (((1 - z) * 4 + y) * 2 + c) * 8 + x * 2 + 1 - h)
+        for z in range(2)
+        for y in range(4)
+        for c in range(2)
+        for x in range(4)
+        for h in range(2)
+    ]
+    return lax.ppermute(array, ("mp", "dp"), moves)
 
 
 def dealt(array, groups=None, axis="mp"):
@@ -705,19 +687,16 @@
     x_at, h_at = dp_at // 2, dp_at % 2
     core_arg = core.astype(jnp.int32).reshape(1)
 
-    kernels_c = over_mp(kernels, core_step=1)
-    blocks = dealt(fanned(core_arg, kernels, kernels_c), SAME_CORE)
+    blocks = dealt(jnp.broadcast_to(kernels[None], (4, 2, 144, 384)), SAME_Z_CORE)
     slope, pooled, flat_t, own, other = front(
         core_arg, x, fc_weight, kernels.reshape(288, 384), conv_bias, stitch_one
     )
-    flat_z, flat_2 = over_dp(flat_t, z_step=1), over_dp(flat_t, x_step=2)
     own, blocks = lax.optimization_barrier((own, blocks))
     own = pair_sum(own, over_mp(other, core_step=1))
-    own, flat_z, flat_2 = lax.optimization_barrier((own, flat_z, flat_2))
     parts = dealt(own, SAME_CORE)
 
-    flat_pair = jnp.stack([flat_t, flat_z])
-    flat_1, flat_3 = over_dp(flat_pair, x_step=1), over_dp(flat_pair, x_step=3)
+    flat_z = over_dp(flat_t, z_step=1)
+    blocks_a, blocks_b = over_mp(blocks[0:2], z_step=1), over_far_z(blocks[2:4])
     output, grad_copies, sums = hidden_layer(
         crop_counts,
         parts,
@@ -725,12 +704,16 @@
         jnp.transpose(second_stitch, (1, 2, 0)),
         jnp.transpose(out_grad, (1, 2, 0)),
     )
-    grad_copies, flat_1, flat_3 = lax.optimization_barrier((grad_copies, flat_1, flat_3))
     grads_own = dealt(grad_copies, SAME_CORE)
-    flats = [flat_pair, flat_1, flat_3, flat_2, over_dp(flat_z, x_step=2)]
-    kernels_all = turned(core_arg, blocks)
-    grads_own, flats, kernels_all = lax.optimization_barrier((grads_own, flats, kernels_all))
+    same = [blocks, blocks_a, blocks_b]
+    kernels_all = turned(
+        jnp.stack([core, z_at]).astype(jnp.int32), same + [over_mp(part, core_step=1) for part in same]
+    )
+    flat_pair = jnp.stack([flat_t, flat_z])
+    flat_1, flat_3 = over_dp(flat_pair, x_step=1), over_dp(flat_pair, x_step=3)
+    grads_own, flat_1, flat_3, kernels_all = lax.optimization_barrier((grads_own, flat_1, flat_3, kernels_all))
     grads_other = over_mp(grads_own, core_step=1)
+    flats = [flat_pair, flat_1, flat_3, over_dp(flat_pair, x_step=2)]
     slice_own = dealt(grads_own, axis="dp")
     send, pre, stats = back_fc(core_arg, grads_own, grads_other, fc_weight, stitch_one, pooled, slope)
     send, slice_own = lax.optimization_barrier((send, slice_own))

time: 138 us -> 134 us (0.971)
  waiting for transfers between devices: 30.8 us -> 19.2 us
  starting transfers between devices: 44.9 us -> 53.7 us
  local copies, waits for them, and re-layouts: 10.5 us -> 8.77 us
    all_to_all x6, waiting for transfers between devices: 16.8 us -> 6.05 us  [dealt(): lax.all_to_all(array, axis, 0, 0, tiled=True, axis_index_groups=groups)]
    all_to_all x6, starting transfers between devices: 26 us -> 31.8 us  [dealt(): lax.all_to_all(array, axis, 0, 0, tiled=True, axis_index_groups=groups)]
    unnamed x38 -> x28, local copies, waits for them, and re-layouts: 10.4 us -> 5.75 us
    ppermute x4 -> x7, starting transfers between devices: 3.88 us -> 7.82 us  [over_mp(): return lax.ppermute(array, 'mp', mp_moves(z_step, y_step, core_step))]
    ppermute x9 -> x8, starting transfers between devices: 15 us -> 11.8 us  [over_dp(): return lax.ppermute(array, 'dp', dp_moves(x_step, z_step))]
    ppermute x0 -> x1, starting transfers between devices: none -> 2.24 us  [over_far_z(): return lax.ppermute(array, ('mp', 'dp'), moves)]
    broadcast_in_dim x0 -> x1, local copies, waits for them, and re-layouts: none -> 1.92 us  [local(): jnp.broadcast_to(kernels[None], (4, 2, 144, 384))]
    ppermute x9 -> x8, waiting for transfers between devices: 12.7 us -> 11 us  [over_dp(): return lax.ppermute(array, 'dp', dp_moves(x_step, z_step))]
  transfers between devices with their start and end apart: 19 -> 22, of which waited for: 10 -> 10; matrix products, arithmetic and copies ran while one was open for 1% -> 2% of each run, Pallas kernels for 33% -> 35%
where the time goes in v4:
time: 134 us; the launch traced here: 133 us
  starting transfers between devices  53.7 us (40%)
  Pallas kernels  49.2 us (37%)
  waiting for transfers between devices  19.2 us (14%)
  local copies, waits for them, and re-layouts  8.77 us (7%)
    all_to_all x6, starting transfers between devices, dealt(): lax.all_to_all(array, axis, 0, 0, tiled=True, axis_index_groups=groups)  31.8 us
    pallas_call x1, Pallas kernels, front(): pl.pallas_call(front_kernel, in_specs=[SMEM, ANY, ANY, VMEM, VMEM, VMEM],...  14 us
    ppermute x8, starting transfers between devices, over_dp(): return lax.ppermute(array, 'dp', dp_moves(x_step, z_step))  11.8 us
    ppermute x8, waiting for transfers between devices, over_dp(): return lax.ppermute(array, 'dp', dp_moves(x_step, z_step))  11 us
    pallas_call x1, Pallas kernels, back_fc(): pl.pallas_call(back_kernel, in_specs=[SMEM, VMEM, VMEM, ANY, VMEM, ANY, A...  9.52 us
    ppermute x7, starting transfers between devices, over_mp(): return lax.ppermute(array, 'mp', mp_moves(z_step, y_step, core_step))  7.82 us
    pallas_call x1, Pallas kernels, weight_grad(): pl.pallas_call(weight_kernel, in_specs=[ANY, VMEM, VMEM, VMEM], out_specs...  7.77 us
    all_to_all x6, waiting for transfers between devices, dealt(): lax.all_to_all(array, axis, 0, 0, tiled=True, axis_index_groups=groups)  6.05 us
  transfers between devices with their start and end apart: 22, of which 10 were waited for; matrix products, arithmetic and copies ran while one was open for 2% of the time, Pallas kernels for 35%

profile of v4, /device:TPU:1, one launch (start us, length us, event | category | flops | bytes accessed | tf_op | source)
XLA Modules:
  0.0 132.8 jit_solution(1740690529140384219)
XLA Ops:
  0.6 1.9 %broadcast_in_dim.8 = bf16[4,2,144,384]{3,2,1,0:T(8,128)(2,1)} broadcast(bf16[2,144,384]{2,1,0:T(8,128)(2,1)} %bitcast.34), dimensions={1,2,3} | broadcast | bytes 1105920 | tf_op jit(solution)/shard_map/broadcast_in_dim | solution.py:690
  2.6 5.0 %all-to-all-start = ((bf16[4,2,144,384]{3,2,1,0:T(8,128)(2,1)}), bf16[4,2,144,384]{3,2,1,0:T(8,128)(2,1)S(1)}, u32[]{:S(2)}, u32[]{:S(2)}) async-start(bf16[4,2,144,384]{3,2,1,0:T(8,128)(2,1)} %broadcast_in_dim.8), calls=%async_computation | async-start | bytes 1769472 | tf_op jit(solution)/shard_map/all_to_all | solution.py:664
  7.6 14.0 %front.1 = (bf16[13,13,16,128]{3,2,1,0:T(8,128)(2,1)}, f32[36,16,128]{2,1,0:T(8,128)}, bf16[576,128]{1,0:T(8,128)(2,1)}, bf16[8,128,256]{2,1,0:T(8,128)(2,1)}, bf16[8,128,256]{2,1,0:T(8,128)(2,1)}) custom-call(s32[1]{0:T(128)} %bitcast.core_ref, bf16[2,13,13,64,384]{4,3,2,1,0:T(8,128)(2,1)} %bitcast.40, bf16[2,576,4096]{2,1,0:T(8,128)(2,1)} %w_ref.3, ...), custom_call_target="tpu_custom_call" | custom-call | flops 10000000000 | bytes 30000000 | tf_op jit(solution)/shard_map/front/pallas_call | solution.py:192
  23.8 1.6 %collective-permute-start.4 = (bf16[2,2,144,384]{3,2,1,0:T(8,128)(2,1)}, bf16[2,2,144,384]{3,2,1,0:T(8,128)(2,1)}, u32[]{:S(2)}, u32[]{:S(2)}) collective-permute-start(bf16[2,2,144,384]{3,2,1,0:T(8,128)(2,1)} %get-tuple-element.65), channel_id=1, source_target_pairs={{0,64},{8,72},{16,80},{24,88},{32,96},{40,104},{48,112},{56,120},{... | collective-permute-start | bytes 1327112 | tf_op jit(solution)/shard_map/ppermute | solution.py:644
  25.4 2.2 %collective-permute-start.5 = (bf16[2,2,144,384]{3,2,1,0:T(8,128)(2,1)}, bf16[2,2,144,384]{3,2,1,0:T(8,128)(2,1)}, u32[]{:S(2)}, u32[]{:S(2)}) collective-permute-start(bf16[2,2,144,384]{3,2,1,0:T(8,128)(2,1)} %get-tuple-element.64), channel_id=1, source_target_pairs={{0,65},{1,64},{2,67},{3,66},{4,69},{5,68},{6,71},{7,70},{8,73},{9,... | collective-permute-start | bytes 1327112 | tf_op jit(solution)/shard_map/ppermute | solution.py:660
  28.6 5.0 %all-to-all-start.1 = ((bf16[8,128,256]{2,1,0:T(8,128)(2,1)}), bf16[8,128,256]{2,1,0:T(8,128)(2,1)S(1)}, u32[]{:S(2)}, u32[]{:S(2)}) async-start(bf16[8,128,256]{2,1,0:T(8,128)(2,1)} %pair_sum.2), calls=%async_computation.1 | async-start | bytes 1048576 | tf_op jit(solution)/shard_map/all_to_all | solution.py:664
  37.9 2.0 %collective-permute-start.8 = (bf16[2,2,144,384]{3,2,1,0:T(8,128)(2,1)}, bf16[2,2,144,384]{3,2,1,0:T(8,128)(2,1)}, u32[]{:S(2)}, u32[]{:S(2)}) collective-permute-start(bf16[2,2,144,384]{3,2,1,0:T(8,128)(2,1)} %collective-permute-done.5.same_b), channel_id=1, source_target_pairs={{0,8},{8,0},{16,24},{24,16},{32,40},{40,32},{48,56},{56,48},{64,72... | collective-permute-start | bytes 1327112 | tf_op jit(solution)/shard_map/ppermute | solution.py:644
  39.9 3.9 %all-to-all-done.1.parts_ref = bf16[8,128,256]{2,1,0:T(8,128)(2,1)S(1)} async-done(((bf16[8,128,256]{2,1,0:T(8,128)(2,1)}), bf16[8,128,256]{2,1,0:T(8,128)(2,1)S(1)}, u32[]{:S(2)}, u32[]{:S(2)}) %all-to-all-start.1) | async-done | bytes 524320 | tf_op jit(solution)/shard_map/all_to_all | solution.py:664
  45.4 4.1 %all-to-all-start.2 = ((bf16[8,256,128]{2,1,0:T(8,128)(2,1)}), bf16[8,256,128]{2,1,0:T(8,128)(2,1)}, u32[]{:S(2)}, u32[]{:S(2)}) async-start(bf16[8,256,128]{2,1,0:T(8,128)(2,1)} %get-tuple-element.40), calls=%async_computation.2 | async-start | bytes 1048576 | tf_op jit(solution)/shard_map/all_to_all | solution.py:664
  55.4 2.0 %turned_kernels.1.w_ref = bf16[384,2304]{1,0:T(8,128)(2,1)S(1)} custom-call(s32[2]{0:T(128)S(1)} %pad_add_fusion.place_ref, bf16[4,2,144,384]{3,2,1,0:T(8,128)(2,1)S(1)} %all-to-all-done.same, bf16[2,2,144,384]{3,2,1,0:T(8,128)(2,1)} %collective-permute-done.4.same_a, bf16[2,2,144,384]{3,2,1,0:T(8,128)(2,1)} %collective-permute-done.5.same_b, ...), custom_call_target="tpu_custom_call" | custom-call | flops 1000000000 | bytes 4000000 | tf_op jit(solution)/shard_map/turned_kernels/pallas_call | solution.py:471
  59.6 1.7 %collective-permute-start.9 = (bf16[8,256,128]{2,1,0:T(8,128)(2,1)}, bf16[8,256,128]{2,1,0:T(8,128)(2,1)S(1)}, u32[]{:S(2)}, u32[]{:S(2)}) collective-permute-start(bf16[8,256,128]{2,1,0:T(8,128)(2,1)} %all-to-all-done.2.own_ref), channel_id=1, source_target_pairs={{0,8},{8,0},{16,24},{24,16},{32,40},{40,32},{48,56},{56,48},{64,72... | collective-permute-start | bytes 1572872 | tf_op jit(solution)/shard_map/ppermute | solution.py:644
  61.3 6.8 %all-to-all-start.3 = ((bf16[8,256,128]{2,1,0:T(8,128)(2,1)}), bf16[8,256,128]{2,1,0:T(8,128)(2,1)}, u32[]{:S(2)}, u32[]{:S(2)}) async-start(bf16[8,256,128]{2,1,0:T(8,128)(2,1)} %all-to-all-done.2.own_ref), calls=%async_computation.3 | async-start | bytes 1048576 | tf_op jit(solution)/shard_map/all_to_all | solution.py:664
  68.9 9.5 %back_fc.1 = (bf16[16,16,1664]{2,1,0:T(8,128)(2,1)}, bf16[13,13,16,128]{3,2,1,0:T(8,128)(2,1)}, f32[16,128]{1,0:T(8,128)}) custom-call(s32[1]{0:T(128)} %bitcast.core_ref, bf16[8,256,128]{2,1,0:T(8,128)(2,1)} %all-to-all-done.2.own_ref, bf16[8,256,128]{2,1,0:T(8,128)(2,1)} %copy-done.12, bf16[2,576,4096]{2,1,0:T(8,128)(2,1)} %w_ref.3, f32[2,2,16]{2,1,0:T(2,128)} %bitcast.39, ...), custom_call_target="tpu_custom_call" | custom-call | flops 1000000000 | bytes 30000000 | tf_op jit(solution)/shard_map/back_fc/pallas_call | solution.py:370
  78.7 5.9 %all-to-all-start.4 = ((bf16[16,16,1664]{2,1,0:T(8,128)(2,1)}), bf16[16,16,1664]{2,1,0:T(8,128)(2,1)}, u32[]{:S(2)}, u32[]{:S(2)}) async-start(bf16[16,16,1664]{2,1,0:T(8,128)(2,1)} %get-tuple-element.47), calls=%async_computation.4 | async-start | bytes 1703936 | tf_op jit(solution)/shard_map/all_to_all | solution.py:664
  86.4 7.8 %weight_grad.1.first_ref = bf16[304,384]{1,0:T(8,128)(2,1)S(1)} custom-call(bf16[2,13,13,64,384]{4,3,2,1,0:T(8,128)(2,1)} %bitcast.41, bf16[13,13,16,128]{3,2,1,0:T(8,128)(2,1)S(1)} %copy-done.10, f32[8,256]{1,0:T(8,128)S(1)} %get-tuple-element.49.sums_ref, f32[16,128]{1,0:T(8,128)S(1)} %copy-done.11), custom_call_target="tpu_custom_call" | custom-call | flops 10000000000 | bytes 20000000 | tf_op jit(solution)/shard_map/weight_grad/pallas_call | solution.py:440
  94.2 2.9 %collective-permute-start.10 = (bf16[304,384]{1,0:T(8,128)(2,1)S(1)}, bf16[304,384]{1,0:T(8,128)(2,1)S(1)}, u32[]{:S(2)}, u32[]{:S(2)}) collective-permute-start(bf16[304,384]{1,0:T(8,128)(2,1)S(1)} %weight_grad.1.first_ref), channel_id=1, source_target_pairs={{0,1},{1,0},{2,3},{3,2},{4,5},{5,4},{6,7},{7,6},{8,9},{9,8},{10,11... | collective-permute-start | bytes 700424 | tf_op jit(solution)/shard_map/ppermute | solution.py:648
  98.5 4.7 %input_grad.1 = bf16[16,24,1664]{2,1,0:T(8,128)(2,1)S(1)} custom-call(bf16[16,16,1664]{2,1,0:T(8,128)(2,1)} %all-to-all-done.4.g_ref, bf16[384,2304]{1,0:T(8,128)(2,1)S(1)} %turned_kernels.1.w_ref), custom_call_target="tpu_custom_call" | custom-call | flops 4000000000 | bytes 4000000 | tf_op jit(solution)/shard_map/input_grad/pallas_call | solution.py:518
  104.2 5.0 %all-to-all-start.5 = ((bf16[16,24,1664]{2,1,0:T(8,128)(2,1)}), bf16[16,24,1664]{2,1,0:T(8,128)(2,1)S(1)}, u32[]{:S(2)}, u32[]{:S(2)}) async-start(bf16[16,24,1664]{2,1,0:T(8,128)(2,1)} %copy-done), calls=%async_computation.5 | async-start | bytes 2555904 | tf_op jit(solution)/shard_map/all_to_all | solution.py:664
  109.4 2.2 %collective-permute-start.14 = (bf16[2,576,128]{2,1,0:T(8,128)(2,1)S(1)}, bf16[2,576,128]{2,1,0:T(8,128)(2,1)S(1)}, u32[]{:S(2)}, u32[]{:S(2)}) collective-permute-start(bf16[2,576,128]{2,1,0:T(8,128)(2,1)S(1)} %copy-done.5), channel_id=1, source_target_pairs={{0,4},{1,5},{2,6},{3,7},{4,0},{5,1},{6,2},{7,3},{8,12},{9,13},{10,... | collective-permute-start | bytes 884744 | tf_op jit(solution)/shard_map/ppermute | solution.py:648
  112.2 1.8 %collective-permute-start.12 = (bf16[304,384]{1,0:T(8,128)(2,1)S(1)}, bf16[304,384]{1,0:T(8,128)(2,1)S(1)}, u32[]{:S(2)}, u32[]{:S(2)}) collective-permute-start(bf16[304,384]{1,0:T(8,128)(2,1)S(1)} %pair_sum.3.part_0), channel_id=1, source_target_pairs={{0,4},{1,5},{2,6},{3,7},{4,0},{5,1},{6,2},{7,3},{8,12},{9,13},{10,... | collective-permute-start | bytes 700424 | tf_op jit(solution)/shard_map/ppermute | solution.py:648
  114.7 4.5 %collective-permute-done.14.flat_2 = bf16[2,576,128]{2,1,0:T(8,128)(2,1)S(1)} collective-permute-done((bf16[2,576,128]{2,1,0:T(8,128)(2,1)S(1)}, bf16[2,576,128]{2,1,0:T(8,128)(2,1)S(1)}, u32[]{:S(2)}, u32[]{:S(2)}) %collective-permute-start.14) | collective-permute-done | bytes 294944 | tf_op jit(solution)/shard_map/ppermute | solution.py:648
  119.2 5.2 %fc_weight_grad.1 = f32[2,576,512]{2,1,0:T(8,128)} custom-call(s32[9]{0:T(128)S(1)} %stack.57.place_ref, bf16[2,576,128]{2,1,0:T(8,128)(2,1)S(1)} %copy-done.5, bf16[2,576,128]{2,1,0:T(8,128)(2,1)} %collective-permute-done.2.flat_1, bf16[2,576,128]{2,1,0:T(8,128)(2,1)} %collective-permute-done.3.flat_3, ...), custom_call_target="tpu_custom_call" | custom-call | flops 3000000000 | bytes 5000000 | tf_op jit(solution)/shard_map/fc_weight_grad/pallas_call | solution.py:577
  125.5 3.8 %collective-permute-done.12.part_2 = bf16[304,384]{1,0:T(8,128)(2,1)S(1)} collective-permute-done((bf16[304,384]{1,0:T(8,128)(2,1)S(1)}, bf16[304,384]{1,0:T(8,128)(2,1)S(1)}, u32[]{:S(2)}, u32[]{:S(2)}) %collective-permute-start.12) | collective-permute-done | bytes 233504 | tf_op jit(solution)/shard_map/ppermute | solution.py:648
  130.2 2.5 %placed_back.1 = bf16[2,13,13,24,64]{4,3,2,1,0:T(8,128)(2,1)} custom-call(bf16[16,24,1664]{2,1,0:T(8,128)(2,1)S(1)} %all-to-all-done.5.part_ref), custom_call_target="tpu_custom_call" | custom-call | flops 100000000 | bytes 3000000 | tf_op jit(solution)/shard_map/placed_back/pallas_call | solution.py:545
  (64 shorter events, 25.7 us)
Async XLA Ops:
  2.6 20.1 %all-to-all-start = ((bf16[4,2,144,384]{3,2,1,0:T(8,128)(2,1)}), bf16[4,2,144,384]{3,2,1,0:T(8,128)(2,1)S(1)}, u32[]{:S(2)}, u32[]{:S(2)}) async-start(bf16[4,2,144,384]{3,2,1,0:T(8,128)(2,1)} %broadcast_in_dim.8), calls=%async_computation | async-start | bytes 1769472 | tf_op jit(solution)/shard_map/all_to_all | solution.py:664
  21.6 6.1 %collective-permute-start = (bf16[8,128,256]{2,1,0:T(8,128)(2,1)}, bf16[8,128,256]{2,1,0:T(8,128)(2,1)S(1)}, u32[]{:S(2)}, u32[]{:S(2)}) collective-permute-start(bf16[8,128,256]{2,1,0:T(8,128)(2,1)} %get-tuple-element.38), channel_id=1, source_target_pairs={{0,8},{8,0},{16,24},{24,16},{32,40},{40,32},{48,56},{56,48},{64,72... | collective-permute-start | bytes 1572872 | tf_op jit(solution)/shard_map/ppermute | solution.py:644
  22.6 21.1 %copy-start.7 = (f32[256,2,2]{0,2,1:T(2,128)S(1)}, f32[256,2,2]{0,2,1:T(2,128)}, u32[]{:S(2)}) copy-start(f32[256,2,2]{0,2,1:T(2,128)} %param.15) | copy-start | bytes 12292
  22.7 30.7 %collective-permute-start.6 = (bf16[4,2,144,384]{3,2,1,0:T(8,128)(2,1)S(1)}, bf16[4,2,144,384]{3,2,1,0:T(8,128)(2,1)S(1)}, u32[]{:S(2)}, u32[]{:S(2)}) collective-permute-start(bf16[4,2,144,384]{3,2,1,0:T(8,128)(2,1)S(1)} %all-to-all-done.same), channel_id=1, source_target_pairs={{0,8},{8,0},{16,24},{24,16},{32,40},{40,32},{48,56},{56,48},{64,72... | collective-permute-start | bytes 2654216 | tf_op jit(solution)/shard_map/ppermute | solution.py:644
  23.8 12.0 %collective-permute-start.4 = (bf16[2,2,144,384]{3,2,1,0:T(8,128)(2,1)}, bf16[2,2,144,384]{3,2,1,0:T(8,128)(2,1)}, u32[]{:S(2)}, u32[]{:S(2)}) collective-permute-start(bf16[2,2,144,384]{3,2,1,0:T(8,128)(2,1)} %get-tuple-element.65), channel_id=1, source_target_pairs={{0,64},{8,72},{16,80},{24,88},{32,96},{40,104},{48,112},{56,120},{... | collective-permute-start | bytes 1327112 | tf_op jit(solution)/shard_map/ppermute | solution.py:644
  25.4 12.5 %collective-permute-start.5 = (bf16[2,2,144,384]{3,2,1,0:T(8,128)(2,1)}, bf16[2,2,144,384]{3,2,1,0:T(8,128)(2,1)}, u32[]{:S(2)}, u32[]{:S(2)}) collective-permute-start(bf16[2,2,144,384]{3,2,1,0:T(8,128)(2,1)} %get-tuple-element.64), channel_id=1, source_target_pairs={{0,65},{1,64},{2,67},{3,66},{4,69},{5,68},{6,71},{7,70},{8,73},{9,... | collective-permute-start | bytes 1327112 | tf_op jit(solution)/shard_map/ppermute | solution.py:660
  28.6 15.2 %all-to-all-start.1 = ((bf16[8,128,256]{2,1,0:T(8,128)(2,1)}), bf16[8,128,256]{2,1,0:T(8,128)(2,1)S(1)}, u32[]{:S(2)}, u32[]{:S(2)}) async-start(bf16[8,128,256]{2,1,0:T(8,128)(2,1)} %pair_sum.2), calls=%async_computation.1 | async-start | bytes 1048576 | tf_op jit(solution)/shard_map/all_to_all | solution.py:664
  33.6 16.0 %collective-permute-start.1 = (bf16[576,128]{1,0:T(8,128)(2,1)S(1)}, bf16[576,128]{1,0:T(8,128)(2,1)S(1)}, u32[]{:S(2)}, u32[]{:S(2)}) collective-permute-start(bf16[576,128]{1,0:T(8,128)(2,1)S(1)} %copy-done.13), channel_id=1, source_target_pairs={{0,1},{1,0},{2,3},{3,2},{4,5},{5,4},{6,7},{7,6},{8,9},{9,8},{10,11... | collective-permute-start | bytes 442376 | tf_op jit(solution)/shard_map/ppermute | solution.py:648
  35.8 18.5 %collective-permute-start.7 = (bf16[2,2,144,384]{3,2,1,0:T(8,128)(2,1)}, bf16[2,2,144,384]{3,2,1,0:T(8,128)(2,1)S(1)}, u32[]{:S(2)}, u32[]{:S(2)}) collective-permute-start(bf16[2,2,144,384]{3,2,1,0:T(8,128)(2,1)} %collective-permute-done.4.same_a), channel_id=1, source_target_pairs={{0,8},{8,0},{16,24},{24,16},{32,40},{40,32},{48,56},{56,48},{64,72... | collective-permute-start | bytes 1327112 | tf_op jit(solution)/shard_map/ppermute | solution.py:644
  37.9 16.4 %collective-permute-start.8 = (bf16[2,2,144,384]{3,2,1,0:T(8,128)(2,1)}, bf16[2,2,144,384]{3,2,1,0:T(8,128)(2,1)}, u32[]{:S(2)}, u32[]{:S(2)}) collective-permute-start(bf16[2,2,144,384]{3,2,1,0:T(8,128)(2,1)} %collective-permute-done.5.same_b), channel_id=1, source_target_pairs={{0,8},{8,0},{16,24},{24,16},{32,40},{40,32},{48,56},{56,48},{64,72... | collective-permute-start | bytes 1327112 | tf_op jit(solution)/shard_map/ppermute | solution.py:644
  45.4 14.2 %all-to-all-start.2 = ((bf16[8,256,128]{2,1,0:T(8,128)(2,1)}), bf16[8,256,128]{2,1,0:T(8,128)(2,1)}, u32[]{:S(2)}, u32[]{:S(2)}) async-start(bf16[8,256,128]{2,1,0:T(8,128)(2,1)} %get-tuple-element.40), calls=%async_computation.2 | async-start | bytes 1048576 | tf_op jit(solution)/shard_map/all_to_all | solution.py:664
  50.5 28.0 %copy-start.4 = (bf16[2,576,128]{2,1,0:T(8,128)(2,1)}, bf16[2,576,128]{2,1,0:T(8,128)(2,1)S(1)}, u32[]{:S(2)}) copy-start(bf16[2,576,128]{2,1,0:T(8,128)(2,1)S(1)} %pad_maximum_fusion.flat_0) | copy-start | bytes 884740
  50.5 8.5 %collective-permute-start.2 = (bf16[2,576,128]{2,1,0:T(8,128)(2,1)S(1)}, bf16[2,576,128]{2,1,0:T(8,128)(2,1)}, u32[]{:S(2)}, u32[]{:S(2)}) collective-permute-start(bf16[2,576,128]{2,1,0:T(8,128)(2,1)S(1)} %pad_maximum_fusion.flat_0), channel_id=1, source_target_pairs={{0,2},{1,3},{2,4},{3,5},{4,6},{5,7},{6,0},{7,1},{8,10},{9,11},{10,... | collective-permute-start | bytes 884744 | tf_op jit(solution)/shard_map/ppermute | solution.py:648
  51.8 7.2 %collective-permute-start.3 = (bf16[2,576,128]{2,1,0:T(8,128)(2,1)S(1)}, bf16[2,576,128]{2,1,0:T(8,128)(2,1)}, u32[]{:S(2)}, u32[]{:S(2)}) collective-permute-start(bf16[2,576,128]{2,1,0:T(8,128)(2,1)S(1)} %pad_maximum_fusion.flat_0), channel_id=1, source_target_pairs={{0,6},{1,7},{2,0},{3,1},{4,2},{5,3},{6,4},{7,5},{8,14},{9,15},{10,... | collective-permute-start | bytes 884744 | tf_op jit(solution)/shard_map/ppermute | solution.py:648
  59.6 8.5 %collective-permute-start.9 = (bf16[8,256,128]{2,1,0:T(8,128)(2,1)}, bf16[8,256,128]{2,1,0:T(8,128)(2,1)S(1)}, u32[]{:S(2)}, u32[]{:S(2)}) collective-permute-start(bf16[8,256,128]{2,1,0:T(8,128)(2,1)} %all-to-all-done.2.own_ref), channel_id=1, source_target_pairs={{0,8},{8,0},{16,24},{24,16},{32,40},{40,32},{48,56},{56,48},{64,72... | collective-permute-start | bytes 1572872 | tf_op jit(solution)/shard_map/ppermute | solution.py:644
  61.3 17.4 %all-to-all-start.3 = ((bf16[8,256,128]{2,1,0:T(8,128)(2,1)}), bf16[8,256,128]{2,1,0:T(8,128)(2,1)}, u32[]{:S(2)}, u32[]{:S(2)}) async-start(bf16[8,256,128]{2,1,0:T(8,128)(2,1)} %all-to-all-done.2.own_ref), calls=%async_computation.3 | async-start | bytes 1048576 | tf_op jit(solution)/shard_map/all_to_all | solution.py:664
  78.7 19.7 %all-to-all-start.4 = ((bf16[16,16,1664]{2,1,0:T(8,128)(2,1)}), bf16[16,16,1664]{2,1,0:T(8,128)(2,1)}, u32[]{:S(2)}, u32[]{:S(2)}) async-start(bf16[16,16,1664]{2,1,0:T(8,128)(2,1)} %get-tuple-element.47), calls=%async_computation.4 | async-start | bytes 1703936 | tf_op jit(solution)/shard_map/all_to_all | solution.py:664
  94.2 10.0 %collective-permute-start.10 = (bf16[304,384]{1,0:T(8,128)(2,1)S(1)}, bf16[304,384]{1,0:T(8,128)(2,1)S(1)}, u32[]{:S(2)}, u32[]{:S(2)}) collective-permute-start(bf16[304,384]{1,0:T(8,128)(2,1)S(1)} %weight_grad.1.first_ref), channel_id=1, source_target_pairs={{0,1},{1,0},{2,3},{3,2},{4,5},{5,4},{6,7},{7,6},{8,9},{9,8},{10,11... | collective-permute-start | bytes 700424 | tf_op jit(solution)/shard_map/ppermute | solution.py:648
  104.2 26.0 %all-to-all-start.5 = ((bf16[16,24,1664]{2,1,0:T(8,128)(2,1)}), bf16[16,24,1664]{2,1,0:T(8,128)(2,1)S(1)}, u32[]{:S(2)}, u32[]{:S(2)}) async-start(bf16[16,24,1664]{2,1,0:T(8,128)(2,1)} %copy-done), calls=%async_computation.5 | async-start | bytes 2555904 | tf_op jit(solution)/shard_map/all_to_all | solution.py:664
  109.2 10.0 %collective-permute-start.15 = (bf16[8,256,128]{2,1,0:T(8,128)(2,1)}, bf16[8,256,128]{2,1,0:T(8,128)(2,1)S(1)}, u32[]{:S(2)}, u32[]{:S(2)}) collective-permute-start(bf16[8,256,128]{2,1,0:T(8,128)(2,1)} %all-to-all-done.3.own_ref), channel_id=1, source_target_pairs={{0,8},{8,0},{16,24},{24,16},{32,40},{40,32},{48,56},{56,48},{64,72... | collective-permute-start | bytes 1572872 | tf_op jit(solution)/shard_map/ppermute | solution.py:644
  109.4 9.8 %collective-permute-start.14 = (bf16[2,576,128]{2,1,0:T(8,128)(2,1)S(1)}, bf16[2,576,128]{2,1,0:T(8,128)(2,1)S(1)}, u32[]{:S(2)}, u32[]{:S(2)}) collective-permute-start(bf16[2,576,128]{2,1,0:T(8,128)(2,1)S(1)} %copy-done.5), channel_id=1, source_target_pairs={{0,4},{1,5},{2,6},{3,7},{4,0},{5,1},{6,2},{7,3},{8,12},{9,13},{10,... | collective-permute-start | bytes 884744 | tf_op jit(solution)/shard_map/ppermute | solution.py:648
  111.8 13.7 %collective-permute-start.11 = (bf16[304,384]{1,0:T(8,128)(2,1)S(1)}, bf16[304,384]{1,0:T(8,128)(2,1)S(1)}, u32[]{:S(2)}, u32[]{:S(2)}) collective-permute-start(bf16[304,384]{1,0:T(8,128)(2,1)S(1)} %pair_sum.3.part_0), channel_id=1, source_target_pairs={{0,2},{1,3},{2,4},{3,5},{4,6},{5,7},{6,0},{7,1},{8,10},{9,11},{10,... | collective-permute-start | bytes 700424 | tf_op jit(solution)/shard_map/ppermute | solution.py:648
  112.2 17.1 %collective-permute-start.12 = (bf16[304,384]{1,0:T(8,128)(2,1)S(1)}, bf16[304,384]{1,0:T(8,128)(2,1)S(1)}, u32[]{:S(2)}, u32[]{:S(2)}) collective-permute-start(bf16[304,384]{1,0:T(8,128)(2,1)S(1)} %pair_sum.3.part_0), channel_id=1, source_target_pairs={{0,4},{1,5},{2,6},{3,7},{4,0},{5,1},{6,2},{7,3},{8,12},{9,13},{10,... | collective-permute-start | bytes 700424 | tf_op jit(solution)/shard_map/ppermute | solution.py:648
  113.9 15.3 %collective-permute-start.13 = (bf16[304,384]{1,0:T(8,128)(2,1)S(1)}, bf16[304,384]{1,0:T(8,128)(2,1)S(1)}, u32[]{:S(2)}, u32[]{:S(2)}) collective-permute-start(bf16[304,384]{1,0:T(8,128)(2,1)S(1)} %pair_sum.3.part_0), channel_id=1, source_target_pairs={{0,6},{1,7},{2,0},{3,1},{4,2},{5,3},{6,4},{7,5},{8,14},{9,15},{10,... | collective-permute-start | bytes 700424 | tf_op jit(solution)/shard_map/ppermute | solution.py:648
  (12 other events, 91.4 us)

commit v5 on v4

--- a/solution.py
+++ b/solution.py
@@ -454,12 +454,14 @@
     )(x, pre, sums, stats)
 
 
-def turn_kernel(place_ref, same, same_a, same_b, other, other_a, other_b, out_ref, rows):
-    core, z = place_ref[0], place_ref[1]
-    for parity, refs in ((core, (same, same_a, same_b)), (1 - core, (other, other_a, other_b))):
-        for ref, near, first in zip(refs, (True, False, False), (0, 0, 2)):
-            for k in range(ref.shape[0]):
-                block = 8 * (z if near else 1 - z) + 2 * (first + k) + parity
+def turn_kernel(place_ref, *refs):
+    out_ref, rows = refs[8:]
+    core, z, y = place_ref[0], place_ref[1], place_ref[2]
+    for parity, group in ((core, refs[0:4]), (1 - core, refs[4:8])):
+        for part, ref in enumerate(group):
+            for k in range(2):
+                from_y = lax.rem(y + 4 - (2 * (part % 2) + k), 4)
+                block = 8 * (z if part < 2 else 1 - z) + 2 * from_y + parity
                 at = pl.ds(pl.multiple_of(16 * block, 16), 16)
                 for tap in range(9):
                     rows[tap, at] = ref[k, core, 16 * tap : 16 * tap + 16]
@@ -470,11 +472,11 @@
 def turned(place, parts):
     return pl.pallas_call(
         turn_kernel,
-        in_specs=[SMEM] + [VMEM] * 6,
+        in_specs=[SMEM] + [VMEM] * 8,
         out_specs=VMEM,
         out_shape=jax.ShapeDtypeStruct((384, 2304), BF16),
         scratch_shapes=[pltpu.VMEM((9, 256, 384), BF16)],
-        compiler_params=params(SMALL),
+        compiler_params=params(63),
         cost_estimate=cost(1e9, 4e6),
         name="turned_kernels",
     )(place, *parts)
@@ -687,16 +689,17 @@
     x_at, h_at = dp_at // 2, dp_at % 2
     core_arg = core.astype(jnp.int32).reshape(1)
 
-    blocks = dealt(jnp.broadcast_to(kernels[None], (4, 2, 144, 384)), SAME_Z_CORE)
+    column = [kernels] + [over_mp(kernels, y_step=k) for k in range(1, 4)]
     slope, pooled, flat_t, own, other = front(
         core_arg, x, fc_weight, kernels.reshape(288, 384), conv_bias, stitch_one
     )
-    own, blocks = lax.optimization_barrier((own, blocks))
+    own, column = lax.optimization_barrier((own, column))
     own = pair_sum(own, over_mp(other, core_step=1))
     parts = dealt(own, SAME_CORE)
 
     flat_z = over_dp(flat_t, z_step=1)
-    blocks_a, blocks_b = over_mp(blocks[0:2], z_step=1), over_far_z(blocks[2:4])
+    blocks_a, blocks_b = jnp.stack(column[0:2]), jnp.stack(column[2:4])
+    far_a, far_b = over_mp(blocks_a, z_step=1), over_far_z(blocks_b)
     output, grad_copies, sums = hidden_layer(
         crop_counts,
         parts,
@@ -705,15 +708,15 @@
         jnp.transpose(out_grad, (1, 2, 0)),
     )
     grads_own = dealt(grad_copies, SAME_CORE)
-    same = [blocks, blocks_a, blocks_b]
+    same = [blocks_a, blocks_b, far_a, far_b]
     kernels_all = turned(
-        jnp.stack([core, z_at]).astype(jnp.int32), same + [over_mp(part, core_step=1) for part in same]
+        jnp.stack([core, z_at, y_at]).astype(jnp.int32), same + [over_mp(part, core_step=1) for part in same]
     )
     flat_pair = jnp.stack([flat_t, flat_z])
     flat_1, flat_3 = over_dp(flat_pair, x_step=1), over_dp(flat_pair, x_step=3)
     grads_own, flat_1, flat_3, kernels_all = lax.optimization_barrier((grads_own, flat_1, flat_3, kernels_all))
     grads_other = over_mp(grads_own, core_step=1)
-    flats = [flat_pair, flat_1, flat_3, over_dp(flat_pair, x_step=2)]
+    flat_2 = over_dp(flat_pair, x_step=2)
     slice_own = dealt(grads_own, axis="dp")
     send, pre, stats = back_fc(core_arg, grads_own, grads_other, fc_weight, stitch_one, pooled, slope)
     send, slice_own = lax.optimization_barrier((send, slice_own))
@@ -724,7 +727,8 @@
     weight_z = over_dp(weight_part, z_step=1)
     pre_all, weight_part = lax.optimization_barrier((pre_all, weight_part))
     input_part = input_grad_part(pre_all, kernels_all)
-    input_part, weight_z = lax.optimization_barrier((input_part, weight_z))
+    input_part, weight_z, flat_2 = lax.optimization_barrier((input_part, weight_z, flat_2))
+    flats = [flat_pair, flat_1, flat_3, flat_2]
     part = dealt(input_part)
 
     weight_pair = pair_sum(weight_part, weight_z)

time: 134 us -> 131 us (0.978)
  local copies, waits for them, and re-layouts: 8.77 us -> 3.46 us
  Pallas kernels: 49.2 us -> 52.5 us
  starting transfers between devices: 53.7 us -> 52 us
  waiting for transfers between devices: 19.2 us -> 20.8 us
    all_to_all x6 -> x5, starting transfers between devices: 31.8 us -> 22 us  [dealt(): lax.all_to_all(array, axis, 0, 0, tiled=True, axis_index_groups=groups)]
    ppermute x7 -> x11, starting transfers between devices: 7.82 us -> 12.4 us  [over_mp(): return lax.ppermute(array, 'mp', mp_moves(z_step, y_step, core_step))]
    ppermute x7 -> x11, waiting for transfers between devices: 1.23 us -> 4.71 us  [over_mp(): return lax.ppermute(array, 'mp', mp_moves(z_step, y_step, core_step))]
    ppermute x1, waiting for transfers between devices: 0.99 us -> 3.84 us  [over_far_z(): return lax.ppermute(array, ('mp', 'dp'), moves)]
    all_to_all x6 -> x5, waiting for transfers between devices: 6.05 us -> 3.43 us  [dealt(): lax.all_to_all(array, axis, 0, 0, tiled=True, axis_index_groups=groups)]
    unnamed x28 -> x34, local copies, waits for them, and re-layouts: 5.75 us -> 3.37 us
    ppermute x8, waiting for transfers between devices: 11 us -> 8.79 us  [over_dp(): return lax.ppermute(array, 'dp', dp_moves(x_step, z_step))]
    ppermute x8, starting transfers between devices: 11.8 us -> 13.8 us  [over_dp(): return lax.ppermute(array, 'dp', dp_moves(x_step, z_step))]
  transfers between devices with their start and end apart: 22 -> 25, of which waited for: 10 -> 10; matrix products, arithmetic and copies ran while one was open for 2% -> 1% of each run, Pallas kernels for 35% -> 38%
where the time goes in v5:
time: 131 us
  Pallas kernels  52.5 us (40%)
  starting transfers between devices  52 us (40%)
  waiting for transfers between devices  20.8 us (16%)
  local copies, waits for them, and re-layouts  3.46 us (3%)
    all_to_all x5, starting transfers between devices, dealt(): lax.all_to_all(array, axis, 0, 0, tiled=True, axis_index_groups=groups)  22 us
    pallas_call x1, Pallas kernels, front(): pl.pallas_call(front_kernel, in_specs=[SMEM, ANY, ANY, VMEM, VMEM, VMEM],...  14 us
    ppermute x8, starting transfers between devices, over_dp(): return lax.ppermute(array, 'dp', dp_moves(x_step, z_step))  13.8 us
    ppermute x11, starting transfers between devices, over_mp(): return lax.ppermute(array, 'mp', mp_moves(z_step, y_step, core_step))  12.4 us
    pallas_call x1, Pallas kernels, back_fc(): pl.pallas_call(back_kernel, in_specs=[SMEM, VMEM, VMEM, ANY, VMEM, ANY, A...  9.52 us
    ppermute x8, waiting for transfers between devices, over_dp(): return lax.ppermute(array, 'dp', dp_moves(x_step, z_step))  8.79 us
    pallas_call x1, Pallas kernels, weight_grad(): pl.pallas_call(weight_kernel, in_specs=[ANY, VMEM, VMEM, VMEM], out_specs...  8.46 us
    pallas_call x1, Pallas kernels, fc_weight_grad_of(): pl.pallas_call(fc_weight_kernel, in_specs=[SMEM] + [VMEM] * 6, out_specs=...  5.07 us
  transfers between devices with their start and end apart: 25, of which 10 were waited for; matrix products, arithmetic and copies ran while one was open for 1% of the time, Pallas kernels for 38%

profile of v5, /device:TPU:1, one launch (start us, length us, event | category | flops | bytes accessed | tf_op | source)
XLA Modules:
  0.0 130.5 jit_solution(6816782496158613999)
XLA Ops:
  0.6 2.2 %collective-permute-start = (bf16[2,144,384]{2,1,0:T(8,128)(2,1)}, bf16[2,144,384]{2,1,0:T(8,128)(2,1)S(1)}, u32[]{:S(2)}, u32[]{:S(2)}) collective-permute-start(bf16[2,144,384]{2,1,0:T(8,128)(2,1)} %bitcast.39), channel_id=1, source_target_pairs={{0,16},{8,24},{16,32},{24,40},{32,48},{40,56},{48,0},{56,8},{64,80... | collective-permute-start | bytes 663560 | tf_op jit(solution)/shard_map/ppermute | solution.py:646
  2.8 2.6 %collective-permute-start.1 = (bf16[2,144,384]{2,1,0:T(8,128)(2,1)}, bf16[2,144,384]{2,1,0:T(8,128)(2,1)S(1)}, u32[]{:S(2)}, u32[]{:S(2)}) collective-permute-start(bf16[2,144,384]{2,1,0:T(8,128)(2,1)} %bitcast.40), channel_id=1, source_target_pairs={{0,32},{8,40},{16,48},{24,56},{32,0},{40,8},{48,16},{56,24},{64,96... | collective-permute-start | bytes 663560 | tf_op jit(solution)/shard_map/ppermute | solution.py:646
  6.5 14.0 %front.1 = (bf16[13,13,16,128]{3,2,1,0:T(8,128)(2,1)}, f32[36,16,128]{2,1,0:T(8,128)}, bf16[576,128]{1,0:T(8,128)(2,1)}, bf16[8,128,256]{2,1,0:T(8,128)(2,1)}, bf16[8,128,256]{2,1,0:T(8,128)(2,1)}) custom-call(s32[1]{0:T(128)} %bitcast.core_ref, bf16[2,13,13,64,384]{4,3,2,1,0:T(8,128)(2,1)} %bitcast.51, bf16[2,576,4096]{2,1,0:T(8,128)(2,1)} %w_ref.3, ...), custom_call_target="tpu_custom_call" | custom-call | flops 10000000000 | bytes 30000000 | tf_op jit(solution)/shard_map/front/pallas_call | solution.py:192
  22.3 3.8 %collective-permute-start.8 = (bf16[2,2,144,384]{3,2,1,0:T(8,128)(2,1)S(1)}, bf16[2,2,144,384]{3,2,1,0:T(8,128)(2,1)S(1)}, u32[]{:S(2)}, u32[]{:S(2)}) collective-permute-start(bf16[2,2,144,384]{3,2,1,0:T(8,128)(2,1)S(1)} %pad_maximum_fusion.1.refs_1_), channel_id=1, source_target_pairs={{0,65},{1,64},{2,67},{3,66},{4,69},{5,68},{6,71},{7,70},{8,73},{9,... | collective-permute-start | bytes 1327112 | tf_op jit(solution)/shard_map/ppermute | solution.py:662
  27.2 3.5 %all-to-all-start = ((bf16[8,128,256]{2,1,0:T(8,128)(2,1)}), bf16[8,128,256]{2,1,0:T(8,128)(2,1)S(1)}, u32[]{:S(2)}, u32[]{:S(2)}) async-start(bf16[8,128,256]{2,1,0:T(8,128)(2,1)} %pair_sum.2), calls=%async_computation | async-start | bytes 1048576 | tf_op jit(solution)/shard_map/all_to_all | solution.py:666
  32.8 3.8 %collective-permute-done.8.refs_3_ = bf16[2,2,144,384]{3,2,1,0:T(8,128)(2,1)S(1)} collective-permute-done((bf16[2,2,144,384]{3,2,1,0:T(8,128)(2,1)S(1)}, bf16[2,2,144,384]{3,2,1,0:T(8,128)(2,1)S(1)}, u32[]{:S(2)}, u32[]{:S(2)}) %collective-permute-start.8) | collective-permute-done | bytes 442400 | tf_op jit(solution)/shard_map/ppermute | solution.py:662
  37.3 4.7 %collective-permute-done.7.refs_2_ = bf16[2,2,144,384]{3,2,1,0:T(8,128)(2,1)S(1)} collective-permute-done((bf16[2,2,144,384]{3,2,1,0:T(8,128)(2,1)S(1)}, bf16[2,2,144,384]{3,2,1,0:T(8,128)(2,1)S(1)}, u32[]{:S(2)}, u32[]{:S(2)}) %collective-permute-start.7) | collective-permute-done | bytes 442400 | tf_op jit(solution)/shard_map/ppermute | solution.py:646
  42.0 1.9 %collective-permute-start.11 = (bf16[2,2,144,384]{3,2,1,0:T(8,128)(2,1)S(1)}, bf16[2,2,144,384]{3,2,1,0:T(8,128)(2,1)}, u32[]{:S(2)}, u32[]{:S(2)}) collective-permute-start(bf16[2,2,144,384]{3,2,1,0:T(8,128)(2,1)S(1)} %collective-permute-done.7.refs_2_), channel_id=1, source_target_pairs={{0,8},{8,0},{16,24},{24,16},{32,40},{40,32},{48,56},{56,48},{64,72... | collective-permute-start | bytes 1327112 | tf_op jit(solution)/shard_map/ppermute | solution.py:646
  45.5 4.2 %all-to-all-start.1 = ((bf16[8,256,128]{2,1,0:T(8,128)(2,1)}), bf16[8,256,128]{2,1,0:T(8,128)(2,1)}, u32[]{:S(2)}, u32[]{:S(2)}) async-start(bf16[8,256,128]{2,1,0:T(8,128)(2,1)} %get-tuple-element.44), calls=%async_computation.1 | async-start | bytes 1048576 | tf_op jit(solution)/shard_map/all_to_all | solution.py:666
  53.0 3.8 %turned_kernels.1.w_ref = bf16[384,2304]{1,0:T(8,128)(2,1)} custom-call(s32[3]{0:T(128)} %pad_add_fusion.place_ref, bf16[2,2,144,384]{3,2,1,0:T(8,128)(2,1)} %copy-done.11, bf16[2,2,144,384]{3,2,1,0:T(8,128)(2,1)} %copy-done.10, bf16[2,2,144,384]{3,2,1,0:T(8,128)(2,1)} %copy-done.14, bf16[2,2,144,384]{3,2,1,0:T(8,128)(2,1)} %copy-done.13, ...), custom_call_target="tpu_custom_call" | custom-call | flops 1000000000 | bytes 4000000 | tf_op jit(solution)/shard_map/turned_kernels/pallas_call | solution.py:473
  61.1 3.6 %all-to-all-start.2 = ((bf16[8,256,128]{2,1,0:T(8,128)(2,1)}), bf16[8,256,128]{2,1,0:T(8,128)(2,1)S(1)}, u32[]{:S(2)}, u32[]{:S(2)}) async-start(bf16[8,256,128]{2,1,0:T(8,128)(2,1)} %all-to-all-done.1.own_ref), calls=%async_computation.2 | async-start | bytes 1048576 | tf_op jit(solution)/shard_map/all_to_all | solution.py:666
  64.7 3.0 %collective-permute-start.15 = (bf16[2,576,128]{2,1,0:T(8,128)(2,1)S(1)}, bf16[2,576,128]{2,1,0:T(8,128)(2,1)}, u32[]{:S(2)}, u32[]{:S(2)}) collective-permute-start(bf16[2,576,128]{2,1,0:T(8,128)(2,1)S(1)} %pad_maximum_fusion.2.flat_0), channel_id=1, source_target_pairs={{0,4},{1,5},{2,6},{3,7},{4,0},{5,1},{6,2},{7,3},{8,12},{9,13},{10,... | collective-permute-start | bytes 884744 | tf_op jit(solution)/shard_map/ppermute | solution.py:650
  68.5 9.5 %back_fc.1 = (bf16[16,16,1664]{2,1,0:T(8,128)(2,1)}, bf16[13,13,16,128]{3,2,1,0:T(8,128)(2,1)}, f32[16,128]{1,0:T(8,128)}) custom-call(s32[1]{0:T(128)} %bitcast.core_ref, bf16[8,256,128]{2,1,0:T(8,128)(2,1)} %all-to-all-done.1.own_ref, bf16[8,256,128]{2,1,0:T(8,128)(2,1)} %copy-done.12, bf16[2,576,4096]{2,1,0:T(8,128)(2,1)} %w_ref.3, f32[2,2,16]{2,1,0:T(2,128)} %bitcast.50, ...), custom_call_target="tpu_custom_call" | custom-call | flops 1000000000 | bytes 30000000 | tf_op jit(solution)/shard_map/back_fc/pallas_call | solution.py:370
  78.0 5.9 %all-to-all-start.3 = ((bf16[16,16,1664]{2,1,0:T(8,128)(2,1)}), bf16[16,16,1664]{2,1,0:T(8,128)(2,1)S(1)}, u32[]{:S(2)}, u32[]{:S(2)}) async-start(bf16[16,16,1664]{2,1,0:T(8,128)(2,1)} %get-tuple-element.54), calls=%async_computation.3 | async-start | bytes 1703936 | tf_op jit(solution)/shard_map/all_to_all | solution.py:666
  85.7 8.5 %weight_grad.1.first_ref = bf16[304,384]{1,0:T(8,128)(2,1)} custom-call(bf16[2,13,13,64,384]{4,3,2,1,0:T(8,128)(2,1)} %bitcast.52, bf16[13,13,16,128]{3,2,1,0:T(8,128)(2,1)S(1)} %copy-done.6, f32[8,256]{1,0:T(8,128)S(1)} %get-tuple-element.56.sums_ref, f32[16,128]{1,0:T(8,128)S(1)} %copy-done.9), custom_call_target="tpu_custom_call" | custom-call | flops 10000000000 | bytes 20000000 | tf_op jit(solution)/shard_map/weight_grad/pallas_call | solution.py:440
  94.2 3.4 %collective-permute-start.14 = (bf16[304,384]{1,0:T(8,128)(2,1)}, bf16[304,384]{1,0:T(8,128)(2,1)}, u32[]{:S(2)}, u32[]{:S(2)}) collective-permute-start(bf16[304,384]{1,0:T(8,128)(2,1)} %weight_grad.1.first_ref), channel_id=1, source_target_pairs={{0,1},{1,0},{2,3},{3,2},{4,5},{5,4},{6,7},{7,6},{8,9},{9,8},{10,11... | collective-permute-start | bytes 700424 | tf_op jit(solution)/shard_map/ppermute | solution.py:650
  97.7 4.6 %input_grad.1 = bf16[16,24,1664]{2,1,0:T(8,128)(2,1)} custom-call(bf16[16,16,1664]{2,1,0:T(8,128)(2,1)S(1)} %all-to-all-done.3.g_ref, bf16[384,2304]{1,0:T(8,128)(2,1)S(1)} %copy-done), custom_call_target="tpu_custom_call" | custom-call | flops 4000000000 | bytes 4000000 | tf_op jit(solution)/shard_map/input_grad/pallas_call | solution.py:520
  102.3 2.5 %collective-permute-done.14.second_ref = bf16[304,384]{1,0:T(8,128)(2,1)} collective-permute-done((bf16[304,384]{1,0:T(8,128)(2,1)}, bf16[304,384]{1,0:T(8,128)(2,1)}, u32[]{:S(2)}, u32[]{:S(2)}) %collective-permute-start.14) | collective-permute-done | bytes 233504 | tf_op jit(solution)/shard_map/ppermute | solution.py:650
  104.7 4.8 %all-to-all-start.4 = ((bf16[16,24,1664]{2,1,0:T(8,128)(2,1)}), bf16[16,24,1664]{2,1,0:T(8,128)(2,1)S(1)}, u32[]{:S(2)}, u32[]{:S(2)}) async-start(bf16[16,24,1664]{2,1,0:T(8,128)(2,1)} %input_grad.1), calls=%async_computation.4 | async-start | bytes 2555904 | tf_op jit(solution)/shard_map/all_to_all | solution.py:666
  111.3 1.8 %collective-permute-start.17 = (bf16[304,384]{1,0:T(8,128)(2,1)S(1)}, bf16[304,384]{1,0:T(8,128)(2,1)S(1)}, u32[]{:S(2)}, u32[]{:S(2)}) collective-permute-start(bf16[304,384]{1,0:T(8,128)(2,1)S(1)} %pair_sum.3.part_0), channel_id=1, source_target_pairs={{0,4},{1,5},{2,6},{3,7},{4,0},{5,1},{6,2},{7,3},{8,12},{9,13},{10,... | collective-permute-start | bytes 700424 | tf_op jit(solution)/shard_map/ppermute | solution.py:650
  114.4 5.1 %fc_weight_grad.1 = f32[2,576,512]{2,1,0:T(8,128)} custom-call(s32[9]{0:T(128)S(1)} %stack.85.place_ref, bf16[2,576,128]{2,1,0:T(8,128)(2,1)S(1)} %pad_maximum_fusion.2.flat_0, bf16[2,576,128]{2,1,0:T(8,128)(2,1)S(1)} %copy-done.8, bf16[2,576,128]{2,1,0:T(8,128)(2,1)} %collective-permute-done.6.flat_3, bf16[2,576,128]{2,1,0:T(8,128)(2,1)} %collective-permute-done.15.flat_2, ...), custom_call_target="tpu_custom_call" | custom-call | flops 3000000000 | bytes 5000000 | tf_op jit(solution)/shard_map/fc_weight_grad/pallas_call | solution.py:579
  119.8 3.8 %collective-permute-done.17.part_2 = bf16[304,384]{1,0:T(8,128)(2,1)S(1)} collective-permute-done((bf16[304,384]{1,0:T(8,128)(2,1)S(1)}, bf16[304,384]{1,0:T(8,128)(2,1)S(1)}, u32[]{:S(2)}, u32[]{:S(2)}) %collective-permute-start.17) | collective-permute-done | bytes 233504 | tf_op jit(solution)/shard_map/ppermute | solution.py:650
  125.4 2.5 %all-to-all-done.4.part_ref = bf16[16,24,1664]{2,1,0:T(8,128)(2,1)S(1)} async-done(((bf16[16,24,1664]{2,1,0:T(8,128)(2,1)}), bf16[16,24,1664]{2,1,0:T(8,128)(2,1)S(1)}, u32[]{:S(2)}, u32[]{:S(2)}) %all-to-all-start.4) | async-done | bytes 1277984 | tf_op jit(solution)/shard_map/all_to_all | solution.py:666
  127.9 2.5 %placed_back.1 = bf16[2,13,13,24,64]{4,3,2,1,0:T(8,128)(2,1)} custom-call(bf16[16,24,1664]{2,1,0:T(8,128)(2,1)S(1)} %all-to-all-done.4.part_ref), custom_call_target="tpu_custom_call" | custom-call | flops 100000000 | bytes 3000000 | tf_op jit(solution)/shard_map/placed_back/pallas_call | solution.py:547
  (76 shorter events, 23.6 us)
Async XLA Ops:
  0.6 21.5 %collective-permute-start = (bf16[2,144,384]{2,1,0:T(8,128)(2,1)}, bf16[2,144,384]{2,1,0:T(8,128)(2,1)S(1)}, u32[]{:S(2)}, u32[]{:S(2)}) collective-permute-start(bf16[2,144,384]{2,1,0:T(8,128)(2,1)} %bitcast.39), channel_id=1, source_target_pairs={{0,16},{8,24},{16,32},{24,40},{32,48},{40,56},{48,0},{56,8},{64,80... | collective-permute-start | bytes 663560 | tf_op jit(solution)/shard_map/ppermute | solution.py:646
  2.8 19.3 %collective-permute-start.1 = (bf16[2,144,384]{2,1,0:T(8,128)(2,1)}, bf16[2,144,384]{2,1,0:T(8,128)(2,1)S(1)}, u32[]{:S(2)}, u32[]{:S(2)}) collective-permute-start(bf16[2,144,384]{2,1,0:T(8,128)(2,1)} %bitcast.40), channel_id=1, source_target_pairs={{0,32},{8,40},{16,48},{24,56},{32,0},{40,8},{48,16},{56,24},{64,96... | collective-permute-start | bytes 663560 | tf_op jit(solution)/shard_map/ppermute | solution.py:646
  5.4 16.7 %collective-permute-start.2 = (bf16[2,144,384]{2,1,0:T(8,128)(2,1)}, bf16[2,144,384]{2,1,0:T(8,128)(2,1)S(1)}, u32[]{:S(2)}, u32[]{:S(2)}) collective-permute-start(bf16[2,144,384]{2,1,0:T(8,128)(2,1)} %bitcast.41), channel_id=1, source_target_pairs={{0,48},{8,56},{16,0},{24,8},{32,16},{40,24},{48,32},{56,40},{64,11... | collective-permute-start | bytes 663560 | tf_op jit(solution)/shard_map/ppermute | solution.py:646
  20.6 5.7 %collective-permute-start.3 = (bf16[8,128,256]{2,1,0:T(8,128)(2,1)}, bf16[8,128,256]{2,1,0:T(8,128)(2,1)S(1)}, u32[]{:S(2)}, u32[]{:S(2)}) collective-permute-start(bf16[8,128,256]{2,1,0:T(8,128)(2,1)} %get-tuple-element.42), channel_id=1, source_target_pairs={{0,8},{8,0},{16,24},{24,16},{32,40},{40,32},{48,56},{56,48},{64,72... | collective-permute-start | bytes 1572872 | tf_op jit(solution)/shard_map/ppermute | solution.py:646
  22.3 14.3 %collective-permute-start.8 = (bf16[2,2,144,384]{3,2,1,0:T(8,128)(2,1)S(1)}, bf16[2,2,144,384]{3,2,1,0:T(8,128)(2,1)S(1)}, u32[]{:S(2)}, u32[]{:S(2)}) collective-permute-start(bf16[2,2,144,384]{3,2,1,0:T(8,128)(2,1)S(1)} %pad_maximum_fusion.1.refs_1_), channel_id=1, source_target_pairs={{0,65},{1,64},{2,67},{3,66},{4,69},{5,68},{6,71},{7,70},{8,73},{9,... | collective-permute-start | bytes 1327112 | tf_op jit(solution)/shard_map/ppermute | solution.py:662
  26.2 15.7 %collective-permute-start.7 = (bf16[2,2,144,384]{3,2,1,0:T(8,128)(2,1)S(1)}, bf16[2,2,144,384]{3,2,1,0:T(8,128)(2,1)S(1)}, u32[]{:S(2)}, u32[]{:S(2)}) collective-permute-start(bf16[2,2,144,384]{3,2,1,0:T(8,128)(2,1)S(1)} %pad_maximum_fusion.refs_0_), channel_id=1, source_target_pairs={{0,64},{8,72},{16,80},{24,88},{32,96},{40,104},{48,112},{56,120},{... | collective-permute-start | bytes 1327112 | tf_op jit(solution)/shard_map/ppermute | solution.py:646
  27.2 16.6 %all-to-all-start = ((bf16[8,128,256]{2,1,0:T(8,128)(2,1)}), bf16[8,128,256]{2,1,0:T(8,128)(2,1)S(1)}, u32[]{:S(2)}, u32[]{:S(2)}) async-start(bf16[8,128,256]{2,1,0:T(8,128)(2,1)} %pair_sum.2), calls=%async_computation | async-start | bytes 1048576 | tf_op jit(solution)/shard_map/all_to_all | solution.py:666
  30.8 20.2 %collective-permute-start.10 = (bf16[2,2,144,384]{3,2,1,0:T(8,128)(2,1)S(1)}, bf16[2,2,144,384]{3,2,1,0:T(8,128)(2,1)}, u32[]{:S(2)}, u32[]{:S(2)}) collective-permute-start(bf16[2,2,144,384]{3,2,1,0:T(8,128)(2,1)S(1)} %pad_maximum_fusion.1.refs_1_), channel_id=1, source_target_pairs={{0,8},{8,0},{16,24},{24,16},{32,40},{40,32},{48,56},{56,48},{64,72... | collective-permute-start | bytes 1327112 | tf_op jit(solution)/shard_map/ppermute | solution.py:646
  31.1 18.5 %collective-permute-start.4 = (bf16[576,128]{1,0:T(8,128)(2,1)S(1)}, bf16[576,128]{1,0:T(8,128)(2,1)S(1)}, u32[]{:S(2)}, u32[]{:S(2)}) collective-permute-start(bf16[576,128]{1,0:T(8,128)(2,1)S(1)} %copy-done.16), channel_id=1, source_target_pairs={{0,1},{1,0},{2,3},{3,2},{4,5},{5,4},{6,7},{7,6},{8,9},{9,8},{10,11... | collective-permute-start | bytes 442376 | tf_op jit(solution)/shard_map/ppermute | solution.py:650
  32.4 20.6 %collective-permute-start.9 = (bf16[2,2,144,384]{3,2,1,0:T(8,128)(2,1)S(1)}, bf16[2,2,144,384]{3,2,1,0:T(8,128)(2,1)}, u32[]{:S(2)}, u32[]{:S(2)}) collective-permute-start(bf16[2,2,144,384]{3,2,1,0:T(8,128)(2,1)S(1)} %pad_maximum_fusion.refs_0_), channel_id=1, source_target_pairs={{0,8},{8,0},{16,24},{24,16},{32,40},{40,32},{48,56},{56,48},{64,72... | collective-permute-start | bytes 1327112 | tf_op jit(solution)/shard_map/ppermute | solution.py:646
  36.7 16.4 %collective-permute-start.12 = (bf16[2,2,144,384]{3,2,1,0:T(8,128)(2,1)S(1)}, bf16[2,2,144,384]{3,2,1,0:T(8,128)(2,1)}, u32[]{:S(2)}, u32[]{:S(2)}) collective-permute-start(bf16[2,2,144,384]{3,2,1,0:T(8,128)(2,1)S(1)} %collective-permute-done.8.refs_3_), channel_id=1, source_target_pairs={{0,8},{8,0},{16,24},{24,16},{32,40},{40,32},{48,56},{56,48},{64,72... | collective-permute-start | bytes 1327112 | tf_op jit(solution)/shard_map/ppermute | solution.py:646
  42.0 11.1 %collective-permute-start.11 = (bf16[2,2,144,384]{3,2,1,0:T(8,128)(2,1)S(1)}, bf16[2,2,144,384]{3,2,1,0:T(8,128)(2,1)}, u32[]{:S(2)}, u32[]{:S(2)}) collective-permute-start(bf16[2,2,144,384]{3,2,1,0:T(8,128)(2,1)S(1)} %collective-permute-done.7.refs_2_), channel_id=1, source_target_pairs={{0,8},{8,0},{16,24},{24,16},{32,40},{40,32},{48,56},{56,48},{64,72... | collective-permute-start | bytes 1327112 | tf_op jit(solution)/shard_map/ppermute | solution.py:646
  45.5 14.3 %all-to-all-start.1 = ((bf16[8,256,128]{2,1,0:T(8,128)(2,1)}), bf16[8,256,128]{2,1,0:T(8,128)(2,1)}, u32[]{:S(2)}, u32[]{:S(2)}) async-start(bf16[8,256,128]{2,1,0:T(8,128)(2,1)} %get-tuple-element.44), calls=%async_computation.1 | async-start | bytes 1048576 | tf_op jit(solution)/shard_map/all_to_all | solution.py:666
  49.7 8.5 %collective-permute-start.5 = (bf16[2,576,128]{2,1,0:T(8,128)(2,1)S(1)}, bf16[2,576,128]{2,1,0:T(8,128)(2,1)S(1)}, u32[]{:S(2)}, u32[]{:S(2)}) collective-permute-start(bf16[2,576,128]{2,1,0:T(8,128)(2,1)S(1)} %pad_maximum_fusion.2.flat_0), channel_id=1, source_target_pairs={{0,2},{1,3},{2,4},{3,5},{4,6},{5,7},{6,0},{7,1},{8,10},{9,11},{10,... | collective-permute-start | bytes 884744 | tf_op jit(solution)/shard_map/ppermute | solution.py:650
  51.0 7.9 %collective-permute-start.6 = (bf16[2,576,128]{2,1,0:T(8,128)(2,1)S(1)}, bf16[2,576,128]{2,1,0:T(8,128)(2,1)}, u32[]{:S(2)}, u32[]{:S(2)}) collective-permute-start(bf16[2,576,128]{2,1,0:T(8,128)(2,1)S(1)} %pad_maximum_fusion.2.flat_0), channel_id=1, source_target_pairs={{0,6},{1,7},{2,0},{3,1},{4,2},{5,3},{6,4},{7,5},{8,14},{9,15},{10,... | collective-permute-start | bytes 884744 | tf_op jit(solution)/shard_map/ppermute | solution.py:650
  59.8 7.9 %collective-permute-start.13 = (bf16[8,256,128]{2,1,0:T(8,128)(2,1)}, bf16[8,256,128]{2,1,0:T(8,128)(2,1)S(1)}, u32[]{:S(2)}, u32[]{:S(2)}) collective-permute-start(bf16[8,256,128]{2,1,0:T(8,128)(2,1)} %all-to-all-done.1.own_ref), channel_id=1, source_target_pairs={{0,8},{8,0},{16,24},{24,16},{32,40},{40,32},{48,56},{56,48},{64,72... | collective-permute-start | bytes 1572872 | tf_op jit(solution)/shard_map/ppermute | solution.py:646
  61.1 16.9 %all-to-all-start.2 = ((bf16[8,256,128]{2,1,0:T(8,128)(2,1)}), bf16[8,256,128]{2,1,0:T(8,128)(2,1)S(1)}, u32[]{:S(2)}, u32[]{:S(2)}) async-start(bf16[8,256,128]{2,1,0:T(8,128)(2,1)} %all-to-all-done.1.own_ref), calls=%async_computation.2 | async-start | bytes 1048576 | tf_op jit(solution)/shard_map/all_to_all | solution.py:666
  64.7 37.6 %collective-permute-start.15 = (bf16[2,576,128]{2,1,0:T(8,128)(2,1)S(1)}, bf16[2,576,128]{2,1,0:T(8,128)(2,1)}, u32[]{:S(2)}, u32[]{:S(2)}) collective-permute-start(bf16[2,576,128]{2,1,0:T(8,128)(2,1)S(1)} %pad_maximum_fusion.2.flat_0), channel_id=1, source_target_pairs={{0,4},{1,5},{2,6},{3,7},{4,0},{5,1},{6,2},{7,3},{8,12},{9,13},{10,... | collective-permute-start | bytes 884744 | tf_op jit(solution)/shard_map/ppermute | solution.py:650
  78.0 19.7 %all-to-all-start.3 = ((bf16[16,16,1664]{2,1,0:T(8,128)(2,1)}), bf16[16,16,1664]{2,1,0:T(8,128)(2,1)S(1)}, u32[]{:S(2)}, u32[]{:S(2)}) async-start(bf16[16,16,1664]{2,1,0:T(8,128)(2,1)} %get-tuple-element.54), calls=%async_computation.3 | async-start | bytes 1703936 | tf_op jit(solution)/shard_map/all_to_all | solution.py:666
  94.2 10.5 %collective-permute-start.14 = (bf16[304,384]{1,0:T(8,128)(2,1)}, bf16[304,384]{1,0:T(8,128)(2,1)}, u32[]{:S(2)}, u32[]{:S(2)}) collective-permute-start(bf16[304,384]{1,0:T(8,128)(2,1)} %weight_grad.1.first_ref), channel_id=1, source_target_pairs={{0,1},{1,0},{2,3},{3,2},{4,5},{5,4},{6,7},{7,6},{8,9},{9,8},{10,11... | collective-permute-start | bytes 700424 | tf_op jit(solution)/shard_map/ppermute | solution.py:650
  104.7 23.1 %all-to-all-start.4 = ((bf16[16,24,1664]{2,1,0:T(8,128)(2,1)}), bf16[16,24,1664]{2,1,0:T(8,128)(2,1)S(1)}, u32[]{:S(2)}, u32[]{:S(2)}) async-start(bf16[16,24,1664]{2,1,0:T(8,128)(2,1)} %input_grad.1), calls=%async_computation.4 | async-start | bytes 2555904 | tf_op jit(solution)/shard_map/all_to_all | solution.py:666
  110.9 8.8 %collective-permute-start.16 = (bf16[304,384]{1,0:T(8,128)(2,1)S(1)}, bf16[304,384]{1,0:T(8,128)(2,1)S(1)}, u32[]{:S(2)}, u32[]{:S(2)}) collective-permute-start(bf16[304,384]{1,0:T(8,128)(2,1)S(1)} %pair_sum.3.part_0), channel_id=1, source_target_pairs={{0,2},{1,3},{2,4},{3,5},{4,6},{5,7},{6,0},{7,1},{8,10},{9,11},{10,... | collective-permute-start | bytes 700424 | tf_op jit(solution)/shard_map/ppermute | solution.py:650
  111.3 12.3 %collective-permute-start.17 = (bf16[304,384]{1,0:T(8,128)(2,1)S(1)}, bf16[304,384]{1,0:T(8,128)(2,1)S(1)}, u32[]{:S(2)}, u32[]{:S(2)}) collective-permute-start(bf16[304,384]{1,0:T(8,128)(2,1)S(1)} %pair_sum.3.part_0), channel_id=1, source_target_pairs={{0,4},{1,5},{2,6},{3,7},{4,0},{5,1},{6,2},{7,3},{8,12},{9,13},{10,... | collective-permute-start | bytes 700424 | tf_op jit(solution)/shard_map/ppermute | solution.py:650
  113.1 11.4 %collective-permute-start.18 = (bf16[304,384]{1,0:T(8,128)(2,1)S(1)}, bf16[304,384]{1,0:T(8,128)(2,1)S(1)}, u32[]{:S(2)}, u32[]{:S(2)}) collective-permute-start(bf16[304,384]{1,0:T(8,128)(2,1)S(1)} %pair_sum.3.part_0), channel_id=1, source_target_pairs={{0,6},{1,7},{2,0},{3,1},{4,2},{5,3},{6,4},{7,5},{8,14},{9,15},{10,... | collective-permute-start | bytes 700424 | tf_op jit(solution)/shard_map/ppermute | solution.py:650
  (18 other events, 222.9 us)

commit v6 on v5

--- a/solution.py
+++ b/solution.py
@@ -524,7 +524,7 @@
         out_shape=jax.ShapeDtypeStruct((16, 24, 1664), BF16),
         scratch_shapes=[pltpu.VMEM((3, 256, 1920), BF16)],
         compiler_params=params(SMALL),
-        cost_estimate=cost(4e9, 4e6),
+        cost_estimate=cost(4e9, 20e6),
         name="input_grad",
     )(g, w)
 

time: 131 us -> 131 us (level)
  no operation moved by 1% of the time
where the time goes in v6:
time: 131 us
  Pallas kernels  52.5 us (40%)
  starting transfers between devices  52 us (40%)
  waiting for transfers between devices  20.8 us (16%)
  local copies, waits for them, and re-layouts  3.46 us (3%)
    all_to_all x5, starting transfers between devices, dealt(): lax.all_to_all(array, axis, 0, 0, tiled=True, axis_index_groups=groups)  22 us
    pallas_call x1, Pallas kernels, front(): pl.pallas_call(front_kernel, in_specs=[SMEM, ANY, ANY, VMEM, VMEM, VMEM],...  14 us
    ppermute x8, starting transfers between devices, over_dp(): return lax.ppermute(array, 'dp', dp_moves(x_step, z_step))  13.8 us
    ppermute x11, starting transfers between devices, over_mp(): return lax.ppermute(array, 'mp', mp_moves(z_step, y_step, core_step))  12.4 us
    pallas_call x1, Pallas kernels, back_fc(): pl.pallas_call(back_kernel, in_specs=[SMEM, VMEM, VMEM, ANY, VMEM, ANY, A...  9.52 us
    ppermute x8, waiting for transfers between devices, over_dp(): return lax.ppermute(array, 'dp', dp_moves(x_step, z_step))  8.79 us
    pallas_call x1, Pallas kernels, weight_grad(): pl.pallas_call(weight_kernel, in_specs=[ANY, VMEM, VMEM, VMEM], out_specs...  8.46 us
    pallas_call x1, Pallas kernels, fc_weight_grad_of(): pl.pallas_call(fc_weight_kernel, in_specs=[SMEM] + [VMEM] * 6, out_specs=...  5.07 us
  transfers between devices with their start and end apart: 25, of which 10 were waited for; matrix products, arithmetic and copies ran while one was open for 1% of the time, Pallas kernels for 38%

profile of v6, /device:TPU:1, one launch (start us, length us, event | category | flops | bytes accessed | tf_op | source)
XLA Modules:
  0.0 130.5 jit_solution(6816782496158613999)
XLA Ops:
  0.6 2.2 %collective-permute-start = (bf16[2,144,384]{2,1,0:T(8,128)(2,1)}, bf16[2,144,384]{2,1,0:T(8,128)(2,1)S(1)}, u32[]{:S(2)}, u32[]{:S(2)}) collective-permute-start(bf16[2,144,384]{2,1,0:T(8,128)(2,1)} %bitcast.39), channel_id=1, source_target_pairs={{0,16},{8,24},{16,32},{24,40},{32,48},{40,56},{48,0},{56,8},{64,80... | collective-permute-start | bytes 663560 | tf_op jit(solution)/shard_map/ppermute | solution.py:646
  2.8 2.6 %collective-permute-start.1 = (bf16[2,144,384]{2,1,0:T(8,128)(2,1)}, bf16[2,144,384]{2,1,0:T(8,128)(2,1)S(1)}, u32[]{:S(2)}, u32[]{:S(2)}) collective-permute-start(bf16[2,144,384]{2,1,0:T(8,128)(2,1)} %bitcast.40), channel_id=1, source_target_pairs={{0,32},{8,40},{16,48},{24,56},{32,0},{40,8},{48,16},{56,24},{64,96... | collective-permute-start | bytes 663560 | tf_op jit(solution)/shard_map/ppermute | solution.py:646
  6.5 14.0 %front.1 = (bf16[13,13,16,128]{3,2,1,0:T(8,128)(2,1)}, f32[36,16,128]{2,1,0:T(8,128)}, bf16[576,128]{1,0:T(8,128)(2,1)}, bf16[8,128,256]{2,1,0:T(8,128)(2,1)}, bf16[8,128,256]{2,1,0:T(8,128)(2,1)}) custom-call(s32[1]{0:T(128)} %bitcast.core_ref, bf16[2,13,13,64,384]{4,3,2,1,0:T(8,128)(2,1)} %bitcast.51, bf16[2,576,4096]{2,1,0:T(8,128)(2,1)} %w_ref.3, ...), custom_call_target="tpu_custom_call" | custom-call | flops 10000000000 | bytes 30000000 | tf_op jit(solution)/shard_map/front/pallas_call | solution.py:192
  22.3 3.8 %collective-permute-start.8 = (bf16[2,2,144,384]{3,2,1,0:T(8,128)(2,1)S(1)}, bf16[2,2,144,384]{3,2,1,0:T(8,128)(2,1)S(1)}, u32[]{:S(2)}, u32[]{:S(2)}) collective-permute-start(bf16[2,2,144,384]{3,2,1,0:T(8,128)(2,1)S(1)} %pad_maximum_fusion.1.refs_1_), channel_id=1, source_target_pairs={{0,65},{1,64},{2,67},{3,66},{4,69},{5,68},{6,71},{7,70},{8,73},{9,... | collective-permute-start | bytes 1327112 | tf_op jit(solution)/shard_map/ppermute | solution.py:662
  27.2 3.5 %all-to-all-start = ((bf16[8,128,256]{2,1,0:T(8,128)(2,1)}), bf16[8,128,256]{2,1,0:T(8,128)(2,1)S(1)}, u32[]{:S(2)}, u32[]{:S(2)}) async-start(bf16[8,128,256]{2,1,0:T(8,128)(2,1)} %pair_sum.2), calls=%async_computation | async-start | bytes 1048576 | tf_op jit(solution)/shard_map/all_to_all | solution.py:666
  32.8 3.8 %collective-permute-done.8.refs_3_ = bf16[2,2,144,384]{3,2,1,0:T(8,128)(2,1)S(1)} collective-permute-done((bf16[2,2,144,384]{3,2,1,0:T(8,128)(2,1)S(1)}, bf16[2,2,144,384]{3,2,1,0:T(8,128)(2,1)S(1)}, u32[]{:S(2)}, u32[]{:S(2)}) %collective-permute-start.8) | collective-permute-done | bytes 442400 | tf_op jit(solution)/shard_map/ppermute | solution.py:662
  37.3 4.7 %collective-permute-done.7.refs_2_ = bf16[2,2,144,384]{3,2,1,0:T(8,128)(2,1)S(1)} collective-permute-done((bf16[2,2,144,384]{3,2,1,0:T(8,128)(2,1)S(1)}, bf16[2,2,144,384]{3,2,1,0:T(8,128)(2,1)S(1)}, u32[]{:S(2)}, u32[]{:S(2)}) %collective-permute-start.7) | collective-permute-done | bytes 442400 | tf_op jit(solution)/shard_map/ppermute | solution.py:646
  42.0 1.9 %collective-permute-start.11 = (bf16[2,2,144,384]{3,2,1,0:T(8,128)(2,1)S(1)}, bf16[2,2,144,384]{3,2,1,0:T(8,128)(2,1)}, u32[]{:S(2)}, u32[]{:S(2)}) collective-permute-start(bf16[2,2,144,384]{3,2,1,0:T(8,128)(2,1)S(1)} %collective-permute-done.7.refs_2_), channel_id=1, source_target_pairs={{0,8},{8,0},{16,24},{24,16},{32,40},{40,32},{48,56},{56,48},{64,72... | collective-permute-start | bytes 1327112 | tf_op jit(solution)/shard_map/ppermute | solution.py:646
  45.5 4.2 %all-to-all-start.1 = ((bf16[8,256,128]{2,1,0:T(8,128)(2,1)}), bf16[8,256,128]{2,1,0:T(8,128)(2,1)}, u32[]{:S(2)}, u32[]{:S(2)}) async-start(bf16[8,256,128]{2,1,0:T(8,128)(2,1)} %get-tuple-element.44), calls=%async_computation.1 | async-start | bytes 1048576 | tf_op jit(solution)/shard_map/all_to_all | solution.py:666
  53.0 3.8 %turned_kernels.1.w_ref = bf16[384,2304]{1,0:T(8,128)(2,1)} custom-call(s32[3]{0:T(128)} %pad_add_fusion.place_ref, bf16[2,2,144,384]{3,2,1,0:T(8,128)(2,1)} %copy-done.11, bf16[2,2,144,384]{3,2,1,0:T(8,128)(2,1)} %copy-done.10, bf16[2,2,144,384]{3,2,1,0:T(8,128)(2,1)} %copy-done.14, bf16[2,2,144,384]{3,2,1,0:T(8,128)(2,1)} %copy-done.13, ...), custom_call_target="tpu_custom_call" | custom-call | flops 1000000000 | bytes 4000000 | tf_op jit(solution)/shard_map/turned_kernels/pallas_call | solution.py:473
  61.1 3.6 %all-to-all-start.2 = ((bf16[8,256,128]{2,1,0:T(8,128)(2,1)}), bf16[8,256,128]{2,1,0:T(8,128)(2,1)S(1)}, u32[]{:S(2)}, u32[]{:S(2)}) async-start(bf16[8,256,128]{2,1,0:T(8,128)(2,1)} %all-to-all-done.1.own_ref), calls=%async_computation.2 | async-start | bytes 1048576 | tf_op jit(solution)/shard_map/all_to_all | solution.py:666
  64.7 3.0 %collective-permute-start.15 = (bf16[2,576,128]{2,1,0:T(8,128)(2,1)S(1)}, bf16[2,576,128]{2,1,0:T(8,128)(2,1)}, u32[]{:S(2)}, u32[]{:S(2)}) collective-permute-start(bf16[2,576,128]{2,1,0:T(8,128)(2,1)S(1)} %pad_maximum_fusion.2.flat_0), channel_id=1, source_target_pairs={{0,4},{1,5},{2,6},{3,7},{4,0},{5,1},{6,2},{7,3},{8,12},{9,13},{10,... | collective-permute-start | bytes 884744 | tf_op jit(solution)/shard_map/ppermute | solution.py:650
  68.5 9.5 %back_fc.1 = (bf16[16,16,1664]{2,1,0:T(8,128)(2,1)}, bf16[13,13,16,128]{3,2,1,0:T(8,128)(2,1)}, f32[16,128]{1,0:T(8,128)}) custom-call(s32[1]{0:T(128)} %bitcast.core_ref, bf16[8,256,128]{2,1,0:T(8,128)(2,1)} %all-to-all-done.1.own_ref, bf16[8,256,128]{2,1,0:T(8,128)(2,1)} %copy-done.12, bf16[2,576,4096]{2,1,0:T(8,128)(2,1)} %w_ref.3, f32[2,2,16]{2,1,0:T(2,128)} %bitcast.50, ...), custom_call_target="tpu_custom_call" | custom-call | flops 1000000000 | bytes 30000000 | tf_op jit(solution)/shard_map/back_fc/pallas_call | solution.py:370
  78.0 5.9 %all-to-all-start.3 = ((bf16[16,16,1664]{2,1,0:T(8,128)(2,1)}), bf16[16,16,1664]{2,1,0:T(8,128)(2,1)S(1)}, u32[]{:S(2)}, u32[]{:S(2)}) async-start(bf16[16,16,1664]{2,1,0:T(8,128)(2,1)} %get-tuple-element.54), calls=%async_computation.3 | async-start | bytes 1703936 | tf_op jit(solution)/shard_map/all_to_all | solution.py:666
  85.7 8.5 %weight_grad.1.first_ref = bf16[304,384]{1,0:T(8,128)(2,1)} custom-call(bf16[2,13,13,64,384]{4,3,2,1,0:T(8,128)(2,1)} %bitcast.52, bf16[13,13,16,128]{3,2,1,0:T(8,128)(2,1)S(1)} %copy-done.6, f32[8,256]{1,0:T(8,128)S(1)} %get-tuple-element.56.sums_ref, f32[16,128]{1,0:T(8,128)S(1)} %copy-done.9), custom_call_target="tpu_custom_call" | custom-call | flops 10000000000 | bytes 20000000 | tf_op jit(solution)/shard_map/weight_grad/pallas_call | solution.py:440
  94.2 3.4 %collective-permute-start.14 = (bf16[304,384]{1,0:T(8,128)(2,1)}, bf16[304,384]{1,0:T(8,128)(2,1)}, u32[]{:S(2)}, u32[]{:S(2)}) collective-permute-start(bf16[304,384]{1,0:T(8,128)(2,1)} %weight_grad.1.first_ref), channel_id=1, source_target_pairs={{0,1},{1,0},{2,3},{3,2},{4,5},{5,4},{6,7},{7,6},{8,9},{9,8},{10,11... | collective-permute-start | bytes 700424 | tf_op jit(solution)/shard_map/ppermute | solution.py:650
  97.7 4.6 %input_grad.1 = bf16[16,24,1664]{2,1,0:T(8,128)(2,1)} custom-call(bf16[16,16,1664]{2,1,0:T(8,128)(2,1)S(1)} %all-to-all-done.3.g_ref, bf16[384,2304]{1,0:T(8,128)(2,1)S(1)} %copy-done), custom_call_target="tpu_custom_call" | custom-call | flops 4000000000 | bytes 20000000 | tf_op jit(solution)/shard_map/input_grad/pallas_call | solution.py:520
  102.3 2.5 %collective-permute-done.14.second_ref = bf16[304,384]{1,0:T(8,128)(2,1)} collective-permute-done((bf16[304,384]{1,0:T(8,128)(2,1)}, bf16[304,384]{1,0:T(8,128)(2,1)}, u32[]{:S(2)}, u32[]{:S(2)}) %collective-permute-start.14) | collective-permute-done | bytes 233504 | tf_op jit(solution)/shard_map/ppermute | solution.py:650
  104.7 4.8 %all-to-all-start.4 = ((bf16[16,24,1664]{2,1,0:T(8,128)(2,1)}), bf16[16,24,1664]{2,1,0:T(8,128)(2,1)S(1)}, u32[]{:S(2)}, u32[]{:S(2)}) async-start(bf16[16,24,1664]{2,1,0:T(8,128)(2,1)} %input_grad.1), calls=%async_computation.4 | async-start | bytes 2555904 | tf_op jit(solution)/shard_map/all_to_all | solution.py:666
  111.3 1.8 %collective-permute-start.17 = (bf16[304,384]{1,0:T(8,128)(2,1)S(1)}, bf16[304,384]{1,0:T(8,128)(2,1)S(1)}, u32[]{:S(2)}, u32[]{:S(2)}) collective-permute-start(bf16[304,384]{1,0:T(8,128)(2,1)S(1)} %pair_sum.3.part_0), channel_id=1, source_target_pairs={{0,4},{1,5},{2,6},{3,7},{4,0},{5,1},{6,2},{7,3},{8,12},{9,13},{10,... | collective-permute-start | bytes 700424 | tf_op jit(solution)/shard_map/ppermute | solution.py:650
  114.4 5.1 %fc_weight_grad.1 = f32[2,576,512]{2,1,0:T(8,128)} custom-call(s32[9]{0:T(128)S(1)} %stack.85.place_ref, bf16[2,576,128]{2,1,0:T(8,128)(2,1)S(1)} %pad_maximum_fusion.2.flat_0, bf16[2,576,128]{2,1,0:T(8,128)(2,1)S(1)} %copy-done.8, bf16[2,576,128]{2,1,0:T(8,128)(2,1)} %collective-permute-done.6.flat_3, bf16[2,576,128]{2,1,0:T(8,128)(2,1)} %collective-permute-done.15.flat_2, ...), custom_call_target="tpu_custom_call" | custom-call | flops 3000000000 | bytes 5000000 | tf_op jit(solution)/shard_map/fc_weight_grad/pallas_call | solution.py:579
  119.8 3.8 %collective-permute-done.17.part_2 = bf16[304,384]{1,0:T(8,128)(2,1)S(1)} collective-permute-done((bf16[304,384]{1,0:T(8,128)(2,1)S(1)}, bf16[304,384]{1,0:T(8,128)(2,1)S(1)}, u32[]{:S(2)}, u32[]{:S(2)}) %collective-permute-start.17) | collective-permute-done | bytes 233504 | tf_op jit(solution)/shard_map/ppermute | solution.py:650
  125.4 2.5 %all-to-all-done.4.part_ref = bf16[16,24,1664]{2,1,0:T(8,128)(2,1)S(1)} async-done(((bf16[16,24,1664]{2,1,0:T(8,128)(2,1)}), bf16[16,24,1664]{2,1,0:T(8,128)(2,1)S(1)}, u32[]{:S(2)}, u32[]{:S(2)}) %all-to-all-start.4) | async-done | bytes 1277984 | tf_op jit(solution)/shard_map/all_to_all | solution.py:666
  127.9 2.5 %placed_back.1 = bf16[2,13,13,24,64]{4,3,2,1,0:T(8,128)(2,1)} custom-call(bf16[16,24,1664]{2,1,0:T(8,128)(2,1)S(1)} %all-to-all-done.4.part_ref), custom_call_target="tpu_custom_call" | custom-call | flops 100000000 | bytes 3000000 | tf_op jit(solution)/shard_map/placed_back/pallas_call | solution.py:547
  (76 shorter events, 23.6 us)
Async XLA Ops:
  0.6 21.5 %collective-permute-start = (bf16[2,144,384]{2,1,0:T(8,128)(2,1)}, bf16[2,144,384]{2,1,0:T(8,128)(2,1)S(1)}, u32[]{:S(2)}, u32[]{:S(2)}) collective-permute-start(bf16[2,144,384]{2,1,0:T(8,128)(2,1)} %bitcast.39), channel_id=1, source_target_pairs={{0,16},{8,24},{16,32},{24,40},{32,48},{40,56},{48,0},{56,8},{64,80... | collective-permute-start | bytes 663560 | tf_op jit(solution)/shard_map/ppermute | solution.py:646
  2.8 19.3 %collective-permute-start.1 = (bf16[2,144,384]{2,1,0:T(8,128)(2,1)}, bf16[2,144,384]{2,1,0:T(8,128)(2,1)S(1)}, u32[]{:S(2)}, u32[]{:S(2)}) collective-permute-start(bf16[2,144,384]{2,1,0:T(8,128)(2,1)} %bitcast.40), channel_id=1, source_target_pairs={{0,32},{8,40},{16,48},{24,56},{32,0},{40,8},{48,16},{56,24},{64,96... | collective-permute-start | bytes 663560 | tf_op jit(solution)/shard_map/ppermute | solution.py:646
  5.4 16.7 %collective-permute-start.2 = (bf16[2,144,384]{2,1,0:T(8,128)(2,1)}, bf16[2,144,384]{2,1,0:T(8,128)(2,1)S(1)}, u32[]{:S(2)}, u32[]{:S(2)}) collective-permute-start(bf16[2,144,384]{2,1,0:T(8,128)(2,1)} %bitcast.41), channel_id=1, source_target_pairs={{0,48},{8,56},{16,0},{24,8},{32,16},{40,24},{48,32},{56,40},{64,11... | collective-permute-start | bytes 663560 | tf_op jit(solution)/shard_map/ppermute | solution.py:646
  20.6 5.7 %collective-permute-start.3 = (bf16[8,128,256]{2,1,0:T(8,128)(2,1)}, bf16[8,128,256]{2,1,0:T(8,128)(2,1)S(1)}, u32[]{:S(2)}, u32[]{:S(2)}) collective-permute-start(bf16[8,128,256]{2,1,0:T(8,128)(2,1)} %get-tuple-element.42), channel_id=1, source_target_pairs={{0,8},{8,0},{16,24},{24,16},{32,40},{40,32},{48,56},{56,48},{64,72... | collective-permute-start | bytes 1572872 | tf_op jit(solution)/shard_map/ppermute | solution.py:646
  22.3 14.3 %collective-permute-start.8 = (bf16[2,2,144,384]{3,2,1,0:T(8,128)(2,1)S(1)}, bf16[2,2,144,384]{3,2,1,0:T(8,128)(2,1)S(1)}, u32[]{:S(2)}, u32[]{:S(2)}) collective-permute-start(bf16[2,2,144,384]{3,2,1,0:T(8,128)(2,1)S(1)} %pad_maximum_fusion.1.refs_1_), channel_id=1, source_target_pairs={{0,65},{1,64},{2,67},{3,66},{4,69},{5,68},{6,71},{7,70},{8,73},{9,... | collective-permute-start | bytes 1327112 | tf_op jit(solution)/shard_map/ppermute | solution.py:662
  26.2 15.7 %collective-permute-start.7 = (bf16[2,2,144,384]{3,2,1,0:T(8,128)(2,1)S(1)}, bf16[2,2,144,384]{3,2,1,0:T(8,128)(2,1)S(1)}, u32[]{:S(2)}, u32[]{:S(2)}) collective-permute-start(bf16[2,2,144,384]{3,2,1,0:T(8,128)(2,1)S(1)} %pad_maximum_fusion.refs_0_), channel_id=1, source_target_pairs={{0,64},{8,72},{16,80},{24,88},{32,96},{40,104},{48,112},{56,120},{... | collective-permute-start | bytes 1327112 | tf_op jit(solution)/shard_map/ppermute | solution.py:646
  27.2 16.6 %all-to-all-start = ((bf16[8,128,256]{2,1,0:T(8,128)(2,1)}), bf16[8,128,256]{2,1,0:T(8,128)(2,1)S(1)}, u32[]{:S(2)}, u32[]{:S(2)}) async-start(bf16[8,128,256]{2,1,0:T(8,128)(2,1)} %pair_sum.2), calls=%async_computation | async-start | bytes 1048576 | tf_op jit(solution)/shard_map/all_to_all | solution.py:666
  30.8 20.2 %collective-permute-start.10 = (bf16[2,2,144,384]{3,2,1,0:T(8,128)(2,1)S(1)}, bf16[2,2,144,384]{3,2,1,0:T(8,128)(2,1)}, u32[]{:S(2)}, u32[]{:S(2)}) collective-permute-start(bf16[2,2,144,384]{3,2,1,0:T(8,128)(2,1)S(1)} %pad_maximum_fusion.1.refs_1_), channel_id=1, source_target_pairs={{0,8},{8,0},{16,24},{24,16},{32,40},{40,32},{48,56},{56,48},{64,72... | collective-permute-start | bytes 1327112 | tf_op jit(solution)/shard_map/ppermute | solution.py:646
  31.1 18.5 %collective-permute-start.4 = (bf16[576,128]{1,0:T(8,128)(2,1)S(1)}, bf16[576,128]{1,0:T(8,128)(2,1)S(1)}, u32[]{:S(2)}, u32[]{:S(2)}) collective-permute-start(bf16[576,128]{1,0:T(8,128)(2,1)S(1)} %copy-done.16), channel_id=1, source_target_pairs={{0,1},{1,0},{2,3},{3,2},{4,5},{5,4},{6,7},{7,6},{8,9},{9,8},{10,11... | collective-permute-start | bytes 442376 | tf_op jit(solution)/shard_map/ppermute | solution.py:650
  32.4 20.6 %collective-permute-start.9 = (bf16[2,2,144,384]{3,2,1,0:T(8,128)(2,1)S(1)}, bf16[2,2,144,384]{3,2,1,0:T(8,128)(2,1)}, u32[]{:S(2)}, u32[]{:S(2)}) collective-permute-start(bf16[2,2,144,384]{3,2,1,0:T(8,128)(2,1)S(1)} %pad_maximum_fusion.refs_0_), channel_id=1, source_target_pairs={{0,8},{8,0},{16,24},{24,16},{32,40},{40,32},{48,56},{56,48},{64,72... | collective-permute-start | bytes 1327112 | tf_op jit(solution)/shard_map/ppermute | solution.py:646
  36.7 16.4 %collective-permute-start.12 = (bf16[2,2,144,384]{3,2,1,0:T(8,128)(2,1)S(1)}, bf16[2,2,144,384]{3,2,1,0:T(8,128)(2,1)}, u32[]{:S(2)}, u32[]{:S(2)}) collective-permute-start(bf16[2,2,144,384]{3,2,1,0:T(8,128)(2,1)S(1)} %collective-permute-done.8.refs_3_), channel_id=1, source_target_pairs={{0,8},{8,0},{16,24},{24,16},{32,40},{40,32},{48,56},{56,48},{64,72... | collective-permute-start | bytes 1327112 | tf_op jit(solution)/shard_map/ppermute | solution.py:646
  42.0 11.1 %collective-permute-start.11 = (bf16[2,2,144,384]{3,2,1,0:T(8,128)(2,1)S(1)}, bf16[2,2,144,384]{3,2,1,0:T(8,128)(2,1)}, u32[]{:S(2)}, u32[]{:S(2)}) collective-permute-start(bf16[2,2,144,384]{3,2,1,0:T(8,128)(2,1)S(1)} %collective-permute-done.7.refs_2_), channel_id=1, source_target_pairs={{0,8},{8,0},{16,24},{24,16},{32,40},{40,32},{48,56},{56,48},{64,72... | collective-permute-start | bytes 1327112 | tf_op jit(solution)/shard_map/ppermute | solution.py:646
  45.5 14.3 %all-to-all-start.1 = ((bf16[8,256,128]{2,1,0:T(8,128)(2,1)}), bf16[8,256,128]{2,1,0:T(8,128)(2,1)}, u32[]{:S(2)}, u32[]{:S(2)}) async-start(bf16[8,256,128]{2,1,0:T(8,128)(2,1)} %get-tuple-element.44), calls=%async_computation.1 | async-start | bytes 1048576 | tf_op jit(solution)/shard_map/all_to_all | solution.py:666
  49.7 8.5 %collective-permute-start.5 = (bf16[2,576,128]{2,1,0:T(8,128)(2,1)S(1)}, bf16[2,576,128]{2,1,0:T(8,128)(2,1)S(1)}, u32[]{:S(2)}, u32[]{:S(2)}) collective-permute-start(bf16[2,576,128]{2,1,0:T(8,128)(2,1)S(1)} %pad_maximum_fusion.2.flat_0), channel_id=1, source_target_pairs={{0,2},{1,3},{2,4},{3,5},{4,6},{5,7},{6,0},{7,1},{8,10},{9,11},{10,... | collective-permute-start | bytes 884744 | tf_op jit(solution)/shard_map/ppermute | solution.py:650
  51.0 7.9 %collective-permute-start.6 = (bf16[2,576,128]{2,1,0:T(8,128)(2,1)S(1)}, bf16[2,576,128]{2,1,0:T(8,128)(2,1)}, u32[]{:S(2)}, u32[]{:S(2)}) collective-permute-start(bf16[2,576,128]{2,1,0:T(8,128)(2,1)S(1)} %pad_maximum_fusion.2.flat_0), channel_id=1, source_target_pairs={{0,6},{1,7},{2,0},{3,1},{4,2},{5,3},{6,4},{7,5},{8,14},{9,15},{10,... | collective-permute-start | bytes 884744 | tf_op jit(solution)/shard_map/ppermute | solution.py:650
  59.8 7.9 %collective-permute-start.13 = (bf16[8,256,128]{2,1,0:T(8,128)(2,1)}, bf16[8,256,128]{2,1,0:T(8,128)(2,1)S(1)}, u32[]{:S(2)}, u32[]{:S(2)}) collective-permute-start(bf16[8,256,128]{2,1,0:T(8,128)(2,1)} %all-to-all-done.1.own_ref), channel_id=1, source_target_pairs={{0,8},{8,0},{16,24},{24,16},{32,40},{40,32},{48,56},{56,48},{64,72... | collective-permute-start | bytes 1572872 | tf_op jit(solution)/shard_map/ppermute | solution.py:646
  61.1 16.9 %all-to-all-start.2 = ((bf16[8,256,128]{2,1,0:T(8,128)(2,1)}), bf16[8,256,128]{2,1,0:T(8,128)(2,1)S(1)}, u32[]{:S(2)}, u32[]{:S(2)}) async-start(bf16[8,256,128]{2,1,0:T(8,128)(2,1)} %all-to-all-done.1.own_ref), calls=%async_computation.2 | async-start | bytes 1048576 | tf_op jit(solution)/shard_map/all_to_all | solution.py:666
  64.7 37.6 %collective-permute-start.15 = (bf16[2,576,128]{2,1,0:T(8,128)(2,1)S(1)}, bf16[2,576,128]{2,1,0:T(8,128)(2,1)}, u32[]{:S(2)}, u32[]{:S(2)}) collective-permute-start(bf16[2,576,128]{2,1,0:T(8,128)(2,1)S(1)} %pad_maximum_fusion.2.flat_0), channel_id=1, source_target_pairs={{0,4},{1,5},{2,6},{3,7},{4,0},{5,1},{6,2},{7,3},{8,12},{9,13},{10,... | collective-permute-start | bytes 884744 | tf_op jit(solution)/shard_map/ppermute | solution.py:650
  78.0 19.7 %all-to-all-start.3 = ((bf16[16,16,1664]{2,1,0:T(8,128)(2,1)}), bf16[16,16,1664]{2,1,0:T(8,128)(2,1)S(1)}, u32[]{:S(2)}, u32[]{:S(2)}) async-start(bf16[16,16,1664]{2,1,0:T(8,128)(2,1)} %get-tuple-element.54), calls=%async_computation.3 | async-start | bytes 1703936 | tf_op jit(solution)/shard_map/all_to_all | solution.py:666
  94.2 10.5 %collective-permute-start.14 = (bf16[304,384]{1,0:T(8,128)(2,1)}, bf16[304,384]{1,0:T(8,128)(2,1)}, u32[]{:S(2)}, u32[]{:S(2)}) collective-permute-start(bf16[304,384]{1,0:T(8,128)(2,1)} %weight_grad.1.first_ref), channel_id=1, source_target_pairs={{0,1},{1,0},{2,3},{3,2},{4,5},{5,4},{6,7},{7,6},{8,9},{9,8},{10,11... | collective-permute-start | bytes 700424 | tf_op jit(solution)/shard_map/ppermute | solution.py:650
  104.7 23.1 %all-to-all-start.4 = ((bf16[16,24,1664]{2,1,0:T(8,128)(2,1)}), bf16[16,24,1664]{2,1,0:T(8,128)(2,1)S(1)}, u32[]{:S(2)}, u32[]{:S(2)}) async-start(bf16[16,24,1664]{2,1,0:T(8,128)(2,1)} %input_grad.1), calls=%async_computation.4 | async-start | bytes 2555904 | tf_op jit(solution)/shard_map/all_to_all | solution.py:666
  110.9 8.8 %collective-permute-start.16 = (bf16[304,384]{1,0:T(8,128)(2,1)S(1)}, bf16[304,384]{1,0:T(8,128)(2,1)S(1)}, u32[]{:S(2)}, u32[]{:S(2)}) collective-permute-start(bf16[304,384]{1,0:T(8,128)(2,1)S(1)} %pair_sum.3.part_0), channel_id=1, source_target_pairs={{0,2},{1,3},{2,4},{3,5},{4,6},{5,7},{6,0},{7,1},{8,10},{9,11},{10,... | collective-permute-start | bytes 700424 | tf_op jit(solution)/shard_map/ppermute | solution.py:650
  111.3 12.3 %collective-permute-start.17 = (bf16[304,384]{1,0:T(8,128)(2,1)S(1)}, bf16[304,384]{1,0:T(8,128)(2,1)S(1)}, u32[]{:S(2)}, u32[]{:S(2)}) collective-permute-start(bf16[304,384]{1,0:T(8,128)(2,1)S(1)} %pair_sum.3.part_0), channel_id=1, source_target_pairs={{0,4},{1,5},{2,6},{3,7},{4,0},{5,1},{6,2},{7,3},{8,12},{9,13},{10,... | collective-permute-start | bytes 700424 | tf_op jit(solution)/shard_map/ppermute | solution.py:650
  113.1 11.4 %collective-permute-start.18 = (bf16[304,384]{1,0:T(8,128)(2,1)S(1)}, bf16[304,384]{1,0:T(8,128)(2,1)S(1)}, u32[]{:S(2)}, u32[]{:S(2)}) collective-permute-start(bf16[304,384]{1,0:T(8,128)(2,1)S(1)} %pair_sum.3.part_0), channel_id=1, source_target_pairs={{0,6},{1,7},{2,0},{3,1},{4,2},{5,3},{6,4},{7,5},{8,14},{9,15},{10,... | collective-permute-start | bytes 700424 | tf_op jit(solution)/shard_map/ppermute | solution.py:650
  (18 other events, 222.9 us)
